TPU v7x, 128 devices: a whole 4x4x4 slice. The times are simulated.
128 devices in a mesh: dp: 16 (over y, z), mp: 8 (over x, core).
Axes of the slice: x: 4, y: 4, z: 4, core: 2. Of those that a mesh axis runs over, the one named last changes fastest.
Arguments:
- grad_kv: bfloat16 [16, 2, 8192, 1024], P('dp', None, None, 'mp'), may hold values from -9 to 9
- error_kv: bfloat16 [16, 2, 8192, 1024], P('dp', None, None, 'mp'), may hold values from -3 to 3
- grad_out: bfloat16 [16, 4096, 4096], P('dp', None, 'mp'), may hold values from -9 to 9
- error_out: bfloat16 [16, 4096, 4096], P('dp', None, 'mp'), may hold values from -3 to 3
- basis_kv: float32 [2, 1024, 32], P(None, 'mp'), may hold values from -6 to 6
- basis_out: float32 [4096, 32], P('mp'), may hold values from -6 to 6
Outputs:
- left_kv: float32 [2, 8192, 32], replicated
- left_out: float32 [4096, 32], replicated
- right_kv: float32 [2, 1024, 32], P(None, 'mp')
- right_out: float32 [4096, 32], P('mp')
- new_error_kv: bfloat16 [16, 2, 8192, 1024], P('dp', None, None, 'mp')
- new_error_out: bfloat16 [16, 4096, 4096], P('dp', None, 'mp')
All inputs are finite; a program needn't handle non-finite values.
Results may differ from a plain program's by a relative error of at most 0.001.
Values sent between devices are 32-bit elements; how exact they have to be, the bound alone decides.
No kernel may reach another device: no remote copies, remote signals or barrier semaphores. Data moves between devices by JAX's collectives and lax.ppermute only.
A program may use at most 128 MiB of HBM per device.

v0:
```python
import jax
import jax.numpy as jnp
from jax import lax
from jax.sharding import PartitionSpec as P

HIGH = lax.Precision.HIGHEST


def gram_of(lead):
    return jnp.einsum("...dr,...ds->...rs", lead, lead, precision=HIGH)


def apply_low(gram, lead):
    low = jnp.linalg.cholesky(gram)
    return lax.linalg.triangular_solve(low, lead, left_side=False, lower=True, transpose_a=True)


def on_device(grad_kv, error_kv, grad_out, error_out, basis_kv, basis_out):
    merged_kv = grad_kv[0].astype(jnp.float32) + error_kv[0].astype(jnp.float32)
    merged_out = grad_out[0].astype(jnp.float32) + error_out[0].astype(jnp.float32)
    part_kv = jnp.einsum("adc,acr->adr", merged_kv, basis_kv, precision=HIGH)
    part_out = jnp.dot(merged_out, basis_out, precision=HIGH)
    lead_kv, lead_out = lax.psum((part_kv, part_out), ("dp", "mp"))
    ortho_kv = apply_low(gram_of(lead_kv), lead_kv)
    ortho_out = apply_low(gram_of(lead_out), lead_out)
    local_kv = jnp.einsum("adc,adr->acr", merged_kv, ortho_kv, precision=HIGH)
    local_out = jnp.dot(merged_out.T, ortho_out, precision=HIGH)
    sum_kv, sum_out = lax.psum((local_kv, local_out), "dp")
    replicas = lax.axis_size("dp")
    right_kv = sum_kv / replicas
    right_out = sum_out / replicas
    new_kv = (merged_kv - jnp.einsum("adr,acr->adc", ortho_kv, right_kv, precision=HIGH)).astype(
        jnp.bfloat16
    )
    new_out = (merged_out - jnp.dot(ortho_out, right_out.T, precision=HIGH)).astype(jnp.bfloat16)
    left_kv = jnp.sqrt(jnp.float32(ortho_kv.shape[1])) * ortho_kv
    left_out = jnp.sqrt(jnp.float32(ortho_out.shape[0])) * ortho_out
    return (left_kv, left_out, right_kv, right_out, new_kv[None], new_out[None])


def solution(mesh):
    placed = (
        P("dp", None, None, "mp"),
        P("dp", None, None, "mp"),
        P("dp", None, "mp"),
        P("dp", None, "mp"),
        P(None, "mp", None),
        P("mp", None),
    )
    return jax.shard_map(
        on_device,
        mesh=mesh,
        in_specs=placed,
        out_specs=(
            P(),
            P(),
            P(None, "mp", None),
            P("mp", None),
            P("dp", None, None, "mp"),
            P("dp", None, "mp"),
        ),
        check_vma=False,
    )
```

profile of v0, /device:TPU:0, one launch (start us, length us, event | category | flops | bytes accessed | tf_op | source)
XLA Modules:
  0.0 340.8 jit_solution(17692779092797803000)
XLA Ops:
  7.2 0.0 copy-start
  7.2 0.0 copy-start.7
  7.2 0.0 all-reduce.6.cloned.1.call-start
  7.2 0.8 copy-done
  8.0 0.0 copy-start.1
  8.0 0.0 copy-start.3
  8.0 11.8 %fusion.4 = f32[4096,32]{0,1:T(8,128)} fusion(f32[512,32]{0,1:T(8,128)S(1)} %copy-done, bf16[1,4096,512]{2,1,0:T(8,128)(2,1)} %param.9, bf16[1,4096,512]{2,1,0:T(8,128)(2,1)} %param.8), kind=kOutput, calls=%fused_computation.6 | convolution fusion | flops 811597824 | bytes 8978432 | tf_op jit(solution)/shard_map/dot_general | solution.py:22
  19.8 0.0 copy-done.7
  19.8 0.0 copy-done.1
  19.8 0.0 copy-done.3
  19.8 10.6 %fusion.9 = f32[2,8192,32]{1,2,0:T(8,128)} fusion(f32[2,128,32]{1,2,0:T(8,128)S(1)} %copy-done.7, bf16[1,2,8192,128]{3,2,1,0:T(8,128)(2,1)S(1)} %copy-done.1, bf16[1,2,8192,128]{3,2,1,0:T(8,128)(2,1)S(1)} %copy-done.3), kind=kOutput, calls=%fused_computation.11 | convolution fusion | flops 811597824 | bytes 10518528 | tf_op jit(solution)/shard_map/adc,acr->adr/dot_general | solution.py:21
  30.4 0.0 all-reduce.6.cloned.1.call-update
  30.4 0.2 all-reduce.4.cloned.1.call-start
  30.7 154.3 %all-reduce.6.cloned.1.call-done = (f32[2,8192,32]{1,2,0:T(8,128)}, f32[4096,32]{0,1:T(8,128)}) async-done(((f32[2,8192,32]{1,2,0:T(8,128)}, f32[4096,32]{0,1:T(8,128)}), (f32[2,8192,32]{1,2,0:T(8,128)}, f32[4096,32]{0,1:T(8,128)})) %all-reduce.6.cloned.1.call-update) | async-done | bytes 2621456 | tf_op jit(solution)/shard_map/psum | solution.py:23
  184.9 0.0 copy-start.4
  184.9 1.8 fusion.20
  186.7 0.1 copy.17
  186.8 2.9 cholesky.61
  189.8 0.6 compare_reduce_fusion
  190.4 0.7 fusion.15
  191.1 2.4 custom-call.15
  193.5 4.3 %fusion.19 = f32[2,32,32]{2,1,0:T(8,128)S(1)} fusion(f32[2,8192,32]{1,2,0:T(8,128)} %get-tuple-element.6), kind=kOutput, calls=%fused_computation.37 | convolution fusion | flops 201326592 | bytes 2105344 | tf_op jit(solution)/shard_map/...dr,...ds->...rs/dot_general | solution.py:10
  197.8 0.1 copy.15
  197.9 5.9 %custom-call.13 = f32[2,32,32]{2,1,0:T(8,128)S(1)} custom-call(f32[2,32,32]{2,1,0:T(8,128)S(1)} %fusion.14), custom_call_target="Cholesky" | custom-call | tf_op jit(solution)/shard_map/jit(cholesky)/cholesky | solution.py:14
  203.8 0.1 compare_reduce_fusion.1
  203.9 0.1 select_bitcast_fusion
  204.0 4.9 %custom-call.14 = f32[2,1,32,32]{2,3,1,0:T(8,128)S(1)} custom-call(f32[2,1,32,32]{3,2,1,0:T(8,128)S(1)} %select_bitcast_fusion), custom_call_target="InvertDiagBlocksLowerTriangular" | custom-call | tf_op jit(solution)/shard_map/triangular_solve | solution.py:15
  208.9 0.0 copy-done.4
  208.9 1.4 broadcast_multiply_fusion.1
  210.3 8.8 %fusion.2 = f32[512,32]{0,1:T(8,128)} fusion(f32[4096,32]{0,1:T(8,128)S(1)} %get-tuple-element.11, bf16[1,4096,512]{2,1,0:T(8,128)(2,1)} %param.9, bf16[1,4096,512]{2,1,0:T(8,128)(2,1)} %param.8), kind=kOutput, calls=%fused_computation.4 | convolution fusion | flops 811597824 | bytes 8978432 | tf_op jit(solution)/shard_map/dot_general | solution.py:27
  219.1 0.0 all-reduce.4.cloned.1.call-update
  219.2 0.0 copy-start.2
  219.2 5.0 %broadcast_multiply_fusion = (f32[2,8192,32]{1,2,0:T(8,128)}, f32[2,8192,32]{1,2,0:T(8,128)S(1)}) fusion(f32[2,8192,32]{1,2,0:T(8,128)} %get-tuple-element.6, f32[2,1,32,32]{2,3,1,0:T(8,128)S(1)} %custom-call.14), kind=kOutput, calls=%fused_computation.16 | convolution fusion | flops 201850880 | bytes 6299648 | tf_op jit(solution)/shard_map/triangular_solve | solution.py:15
  224.2 0.0 copy-done.2
  224.2 7.8 %fusion.7 = f32[2,128,32]{1,2,0:T(8,128)S(1)} fusion(f32[2,8192,32]{1,2,0:T(8,128)S(1)} %get-tuple-element.9, bf16[1,2,8192,128]{3,2,1,0:T(8,128)(2,1)S(1)} %copy-done.2, bf16[1,2,8192,128]{3,2,1,0:T(8,128)(2,1)} %param.6), kind=kOutput, calls=%fused_computation.9 | convolution fusion | flops 811597824 | bytes 10518528 | tf_op jit(solution)/shard_map/adc,adr->acr/dot_general | solution.py:26
  231.9 73.5 %psum.30 = f32[2,128,32]{1,2,0:T(8,128)S(1)} all-reduce(f32[2,128,32]{1,2,0:T(8,128)S(1)} %fusion.7), channel_id=1, replica_groups=mesh['dp'=16,'mp'=8] {'dp'}, use_global_device_ids=true, to_apply=%region_6.7 | all-reduce | flops 8192 | bytes 65536 | tf_op jit(solution)/shard_map/psum | solution.py:28
  305.4 0.0 copy-start.6
  305.4 16.4 %fusion.1 = bf16[1,2,8192,128]{3,2,1,0:T(8,128)(2,1)} fusion(f32[2,8192,32]{1,2,0:T(8,128)S(1)} %get-tuple-element.9, f32[2,128,32]{1,2,0:T(8,128)S(1)} %broadcast_multiply_fusion.3, bf16[1,2,8192,128]{3,2,1,0:T(8,128)(2,1)} %param.7, bf16[1,2,8192,128]{3,2,1,0:T(8,128)(2,1)} %param.6), kind=kOutput, calls=%fused_computation.2 | convolution fusion | flops 815792128 | bytes 14712832 | tf_op jit(solution)/shard_map/adr,acr->adc/dot_general | solution.py:32
  321.8 0.0 copy-done.6
  321.8 0.0 all-reduce.4.cloned.1.call-done
  321.8 0.8 broadcast_multiply_fusion.2
  322.7 0.0 copy-start.5
  322.7 11.3 %fusion.11 = bf16[1,4096,512]{2,1,0:T(8,128)(2,1)} fusion(f32[4096,32]{0,1:T(8,128)S(1)} %get-tuple-element.11, f32[512,32]{0,1:T(8,128)S(1)} %broadcast_multiply_fusion.2, bf16[1,4096,512]{2,1,0:T(8,128)(2,1)} %param.9, bf16[1,4096,512]{2,1,0:T(8,128)(2,1)} %param.8), kind=kOutput, calls=%fused_computation.15 | convolution fusion | flops 815792128 | bytes 13172736 | tf_op jit(solution)/shard_map/dot_general | solution.py:35
  333.9 0.0 copy-done.5
  (7 shorter events, 0.1 us)
Async XLA Ops:
  7.2 0.8 copy-start
  7.2 12.6 %copy-start.7 = (f32[2,128,32]{1,2,0:T(8,128)S(1)}, f32[2,128,32]{1,2,0:T(8,128)}, u32[]{:S(2)}) copy-start(f32[2,128,32]{1,2,0:T(8,128)} %param.10) | copy-start | bytes 98308
  7.2 177.7 %all-reduce.6.cloned.1.call-start = ((), (), s32[]{:S(2)}) async-start(), calls=%async_computation.1 | async-start | bytes 5242880 | tf_op jit(solution)/shard_map/psum | solution.py:23
  8.0 11.8 %copy-start.1 = (bf16[1,2,8192,128]{3,2,1,0:T(8,128)(2,1)S(1)}, bf16[1,2,8192,128]{3,2,1,0:T(8,128)(2,1)}, u32[]{:S(2)}) copy-start(bf16[1,2,8192,128]{3,2,1,0:T(8,128)(2,1)} %param.7) | copy-start | bytes 12582916
  8.0 11.8 %copy-start.3 = (bf16[1,2,8192,128]{3,2,1,0:T(8,128)(2,1)S(1)}, bf16[1,2,8192,128]{3,2,1,0:T(8,128)(2,1)}, u32[]{:S(2)}) copy-start(bf16[1,2,8192,128]{3,2,1,0:T(8,128)(2,1)} %param.6) | copy-start | bytes 12582916
  30.4 291.4 %all-reduce.4.cloned.1.call-start = ((), (), s32[]{:S(2)}) async-start(), calls=%async_computation | async-start | bytes 131072 | tf_op jit(solution)/shard_map/psum | solution.py:28
  184.9 24.0 %copy-start.4 = (f32[4096,32]{0,1:T(8,128)S(1)}, f32[4096,32]{0,1:T(8,128)}, u32[]{:S(2)}) copy-start(f32[4096,32]{0,1:T(8,128)} %get-tuple-element.7) | copy-start | bytes 1572868
  219.2 5.0 %copy-start.2 = (bf16[1,2,8192,128]{3,2,1,0:T(8,128)(2,1)S(1)}, bf16[1,2,8192,128]{3,2,1,0:T(8,128)(2,1)}, u32[]{:S(2)}) copy-start(bf16[1,2,8192,128]{3,2,1,0:T(8,128)(2,1)} %param.7) | copy-start | bytes 12582916
  305.4 16.4 %copy-start.6 = (f32[2,128,32]{1,2,0:T(8,128)}, f32[2,128,32]{1,2,0:T(8,128)S(1)}, u32[]{:S(2)}) copy-start(f32[2,128,32]{1,2,0:T(8,128)S(1)} %broadcast_multiply_fusion.3) | copy-start | bytes 98308
  322.7 11.3 %copy-start.5 = (f32[512,32]{0,1:T(8,128)}, f32[512,32]{0,1:T(8,128)S(1)}, u32[]{:S(2)}) copy-start(f32[512,32]{0,1:T(8,128)S(1)} %broadcast_multiply_fusion.2) | copy-start | bytes 196612
Sparse Core Ops, SparseCore 0:
  30.5 154.3 all-reduce.5
  219.3 79.6 all-reduce.3
where the time goes:
time: 341 us
  waiting for transfers between devices  154 us (45%)
  matrix products  79.1 us (23%)
  blocking collectives  73.5 us (22%)
  other arithmetic  18.6 us (5%)
  between operations  14.1 us (4%)
    psum x1, waiting for transfers between devices, on_device(): lead_kv, lead_out = lax.psum((part_kv, part_out), ('dp', 'mp'))  154 us
    psum x1, blocking collectives, on_device(): sum_kv, sum_out = lax.psum((local_kv, local_out), 'dp')  73.5 us
    dot_general x1, matrix products, on_device(): jnp.einsum('adr,acr->adc', ortho_kv, right_kv, precision=HIGH)  16.4 us
    dot_general x1, matrix products, on_device(): part_out = jnp.dot(merged_out, basis_out, precision=HIGH)  11.8 us
    dot_general x1, matrix products, on_device(): jnp.dot(ortho_out, right_out.T, precision=HIGH)  11.3 us
    dot_general x1, matrix products, on_device(): part_kv = jnp.einsum('adc,acr->adr', merged_kv, basis_kv, precision=HIGH)  10.6 us
    another operation x7, other arithmetic, apply_low(): low = jnp.linalg.cholesky(gram)  9.62 us
    dot_general x1, matrix products, on_device(): local_out = jnp.dot(merged_out.T, ortho_out, precision=HIGH)  8.81 us
  transfers between devices with their start and end apart: 2, of which 1 were waited for; matrix products, arithmetic and copies ran while one was open for 9% of the time, Pallas kernels for 0%

commit v1 on v0

v1 whole, which is shorter than its diff:
```python
import functools

import jax
import jax.numpy as jnp
from jax import lax
from jax.experimental import pallas as pl
from jax.experimental.pallas import tpu as pltpu
from jax.sharding import PartitionSpec as P

F32, BF16 = jnp.float32, jnp.bfloat16
ROWS, COLS = 8192, 128
OROWS, OCOLS = 4096, 512
RANK = 32
REPLICAS = 16
CH = ROWS // 8
OCH = OROWS // 8
HALF = OCH // 2
WIDE = CH + HALF
MIB = 1 << 20


def exchange(axis, turn):
    pairs = []
    for i in range(128):
        q, core = [(i // 2) % 4, i // 32, (i // 8) % 4], i % 2
        q[axis] ^= 1 if turn == core else 3
        pairs.append((i, ((q[1] * 4 + q[2]) * 4 + q[0]) * 2 + core))
    return pairs


CORES = [(i, i ^ 1) for i in range(128)]


def send(x, pairs):
    return lax.ppermute(x, ("dp", "mp"), pairs)


def my_chunk(dh, du, dv):
    dp, mp = lax.axis_index("dp"), lax.axis_index("mp")
    x, y = lax.div(mp, 2), lax.div(dp, 4)
    half = jnp.bitwise_xor(lax.rem(mp, 2), dh)

    def own(q):
        high, low = lax.div(q, 2), lax.rem(q, 2)
        return jnp.bitwise_xor(high, low * (1 - half))

    u = jnp.bitwise_xor(own(x), du)
    v = jnp.bitwise_xor(own(y), dv)
    return half * 4 + u * 2 + v


def dot_nt(a, b):
    return lax.dot_general(a, b, (((1,), (1,)), ((), ())), preferred_element_type=F32)


def dot(a, b):
    return jnp.dot(a, b, preferred_element_type=F32)


def split2(a):
    high = a.astype(BF16)
    return high, (a - high.astype(F32)).astype(BF16)


def split3(a):
    high = a.astype(BF16)
    rest = a - high.astype(F32)
    mid = rest.astype(BF16)
    return high, mid, (rest - mid.astype(F32)).astype(BF16)


def loads(refs, bufs, sems, slot, chunk):
    rows = pl.ds(pl.multiple_of(chunk * CH, CH), CH)
    orows = pl.ds(pl.multiple_of(chunk * OCH, OCH), OCH)
    gkv, ekv, gout, eout = refs
    bgkv, bekv, bgout, beout = bufs
    return [
        pltpu.make_async_copy(gkv.at[0, :, rows, :], bgkv.at[slot], sems.at[slot, 0]),
        pltpu.make_async_copy(ekv.at[0, :, rows, :], bekv.at[slot], sems.at[slot, 1]),
        pltpu.make_async_copy(gout.at[0, orows, :], bgout.at[slot], sems.at[slot, 2]),
        pltpu.make_async_copy(eout.at[0, orows, :], beout.at[slot], sems.at[slot, 3]),
    ]


def buffers(n):
    return [
        pltpu.VMEM((n, 2, CH, COLS), BF16),
        pltpu.VMEM((n, 2, CH, COLS), BF16),
        pltpu.VMEM((n, OCH, OCOLS), BF16),
        pltpu.VMEM((n, OCH, OCOLS), BF16),
        pltpu.SemaphoreType.DMA((n, 4)),
    ]


ANY = pl.BlockSpec(memory_space=pl.ANY)
VM = pl.BlockSpec(memory_space=pltpu.VMEM)


def part_kernel(dh, gkv, ekv, gout, eout, bkv, bout, out, bgkv, bekv, bgout, beout, sems):
    copies = [
        loads((gkv, ekv, gout, eout), (bgkv, bekv, bgout, beout), sems, j, my_chunk(dh, j // 2, j % 2))
        for j in range(4)
    ]
    for chunk in copies:
        for copy in chunk:
            copy.start()
    kv = [jnp.concatenate(split3(bkv[a]), axis=0) for a in range(2)]
    kv = [jnp.concatenate([b, b], axis=1) for b in kv]
    ob = jnp.concatenate(split3(bout[...]), axis=0)

    def fold(r):
        return r[:RANK] + (r[RANK : 2 * RANK] + r[2 * RANK :])

    for j in range(4):
        for copy in copies[j]:
            copy.wait()
        for a in range(2):
            both = jnp.concatenate([bgkv[j, a], bekv[j, a]], axis=1)
            out[j, a, :, :CH] = fold(dot_nt(kv[a], both))
        o = fold(dot_nt(ob, bgout[j]) + dot_nt(ob, beout[j]))
        out[j, 0, :, CH:] = o[:, :HALF]
        out[j, 1, :, CH:] = o[:, HALF:]


def part(dh, args):
    return pl.pallas_call(
        functools.partial(part_kernel, dh),
        out_shape=jax.ShapeDtypeStruct((4, 2, RANK, WIDE), F32),
        in_specs=[ANY] * 4 + [VM] * 2,
        out_specs=VM,
        scratch_shapes=buffers(4),
        compiler_params=pltpu.CompilerParams(vmem_limit_bytes=20 * MIB),
        cost_estimate=pl.CostEstimate(flops=800_000_000, bytes_accessed=9 * MIB, transcendentals=0),
        name="part",
    )(*args)


def piece(refs, du, dv):
    a_own, a_got, b_own, b_got = refs
    return (a_got if du else a_own)[dv], (b_got if dv else b_own)[du]


def right_kernel(dh, first, *refs):
    gkv, ekv, gout, eout = refs[:4]
    lead = refs[4:8]
    before = () if first else refs[8:10]
    right, gram, bgkv, bekv, bgout, beout, sems = refs[8 if first else 10 :]
    copies = [
        loads((gkv, ekv, gout, eout), (bgkv, bekv, bgout, beout), sems, j, my_chunk(dh, j // 2, j % 2))
        for j in range(4)
    ]
    for chunk in copies:
        for copy in chunk:
            copy.start()

    def fold(r):
        return r[:RANK] + r[RANK:]

    def square(parts):
        g = dot_nt(jnp.concatenate(parts, axis=0), jnp.concatenate(parts, axis=0))

        def at(i, j):
            return g[i * RANK : (i + 1) * RANK, j * RANK : (j + 1) * RANK]

        return at(0, 0) + ((at(0, 1) + at(1, 0)) + ((at(0, 2) + at(2, 0)) + at(1, 1)))

    grams = []
    sums = None
    for j in range(4):
        a, b = piece(lead, j // 2, j % 2)
        pa, pb = split3(a), split3(b)
        kva, kvb = [p[:, :CH] for p in pa], [p[:, :CH] for p in pb]
        oa, ob = [p[:, CH:] for p in pa], [p[:, CH:] for p in pb]
        o = [jnp.concatenate([p, q], axis=1) for p, q in zip(oa, ob)]
        grams.append([square(kva), square(kvb), square(o)])
        for copy in copies[j]:
            copy.wait()
        terms = []
        for k, parts in enumerate((kva, kvb)):
            both = jnp.concatenate([bgkv[j, k], bekv[j, k]], axis=1)
            r = fold(dot(jnp.concatenate(parts[:2], axis=0), both))
            terms.append(r[:, :COLS] + r[:, COLS:])
        two = jnp.concatenate(o[:2], axis=0)
        terms.append(fold(dot(two, bgout[j]) + dot(two, beout[j])))
        sums = terms if sums is None else [s + t for s, t in zip(sums, terms)]
    for k in range(3):
        gram_k = (grams[0][k] + grams[1][k]) + (grams[2][k] + grams[3][k])
        gram[k] = gram_k if first else gram_k + before[1][k]
    sums = jnp.concatenate(sums, axis=1)
    right[...] = sums if first else sums + before[0][...]


def right_part(dh, args, lead, before=()):
    return pl.pallas_call(
        functools.partial(right_kernel, dh, not before),
        out_shape=(
            jax.ShapeDtypeStruct((RANK, 2 * COLS + OCOLS), F32),
            jax.ShapeDtypeStruct((3, RANK, RANK), F32),
        ),
        in_specs=[ANY] * 4 + [VM] * (4 + len(before)),
        out_specs=(VM, VM),
        scratch_shapes=buffers(4),
        compiler_params=pltpu.CompilerParams(vmem_limit_bytes=20 * MIB),
        cost_estimate=pl.CostEstimate(flops=800_000_000, bytes_accessed=9 * MIB, transcendentals=0),
        name="right",
    )(*args, *lead, *before)


def factor_kernel(gram, out):
    row = lax.broadcasted_iota(jnp.int32, (RANK, 2 * RANK), 0)
    col = lax.broadcasted_iota(jnp.int32, (RANK, 2 * RANK), 1)
    eye = jnp.where(col == row + RANK, 1.0, 0.0).astype(F32)
    wide = [jnp.concatenate([gram[k], jnp.zeros((RANK, RANK), F32)], axis=1) + eye for k in range(3)]
    scale = [jnp.zeros((RANK, 1), F32)] * 3
    below = lax.broadcasted_iota(jnp.int32, (RANK, 1), 0)
    for i in range(RANK):
        for k in range(3):
            pivot = wide[k][i : i + 1, :]
            d = wide[k][i : i + 1, i : i + 1]
            scale[k] = jnp.where(below == i, lax.rsqrt(d), scale[k])
            factor = jnp.where(below > i, wide[k][:, i : i + 1] / d, 0.0)
            wide[k] = wide[k] - factor * pivot
    for k in range(3):
        out[k] = wide[k][:, RANK:] * scale[k]


def factor(gram):
    return pl.pallas_call(
        factor_kernel,
        out_shape=jax.ShapeDtypeStruct((3, RANK, RANK), F32),
        in_specs=[VM],
        out_specs=VM,
        cost_estimate=pl.CostEstimate(flops=10_000_000, bytes_accessed=3 * MIB, transcendentals=0),
        name="factor",
    )(gram)


def left_kernel(*refs):
    own, other, w = refs[:4], refs[4:8], refs[8]
    left_kv, left_out, ortho = refs[9:12]
    bkv, bout, sems = refs[12:]
    weights = []
    for k in range(3):
        w1, w2, w3 = split3(w[k])
        weights.append(jnp.concatenate([w1, w1, w2, w1, w2, w3], axis=1))

    def apply(k, x):
        l1, l2, l3 = split3(x)
        return dot(weights[k], jnp.concatenate([l1, l2, l1, l3, l2, l1], axis=0))

    def packed(o):
        high = o.astype(BF16).astype(F32)
        rest = o - high
        return jnp.transpose(jnp.concatenate([high, rest, high, jnp.zeros_like(o)], axis=0)).astype(BF16)

    copies = []
    for j in range(8):
        dh, du, dv = j // 4, (j // 2) % 2, j % 2
        a, b = piece(other if dh else own, du, dv)
        out = []
        for s, x in enumerate((a, b)):
            o_kv = apply(s, x[:, :CH])
            o_out = apply(2, x[:, CH:])
            bkv[j, s] = o_kv * (ROWS**0.5)
            out.append(o_out * (OROWS**0.5))
            ortho[j, s, :CH] = packed(o_kv)
            ortho[j, s, CH:] = packed(o_out)
        bout[j, :, :HALF] = out[0]
        bout[j, :, HALF:] = out[1]
        t = my_chunk(dh, du, dv)
        cols = pl.ds(pl.multiple_of(t * CH, CH), CH)
        ocols = pl.ds(pl.multiple_of(t * OCH, OCH), OCH)
        copies.append(pltpu.make_async_copy(bkv.at[j], left_kv.at[:, :, cols], sems.at[j, 0]))
        copies.append(pltpu.make_async_copy(bout.at[j], left_out.at[:, ocols], sems.at[j, 1]))
        copies[-2].start()
        copies[-1].start()
    for copy in copies:
        copy.wait()


def left_part(own, other, w):
    return pl.pallas_call(
        left_kernel,
        out_shape=(
            jax.ShapeDtypeStruct((2, RANK, ROWS), F32),
            jax.ShapeDtypeStruct((RANK, OROWS), F32),
            jax.ShapeDtypeStruct((8, 2, WIDE, 128), BF16),
        ),
        in_specs=[VM] * 9,
        out_specs=(ANY, ANY, VM),
        scratch_shapes=[
            pltpu.VMEM((8, 2, RANK, CH), F32),
            pltpu.VMEM((8, RANK, OCH), F32),
            pltpu.SemaphoreType.DMA((8, 2)),
        ],
        compiler_params=pltpu.CompilerParams(vmem_limit_bytes=24 * MIB),
        cost_estimate=pl.CostEstimate(flops=500_000_000, bytes_accessed=10 * MIB, transcendentals=0),
        name="left",
    )(*own, *other, w)


def error_kernel(*refs):
    gkv, ekv, gout, eout, total, w, ortho = refs[:7]
    right_kv, right_out, new_kv, new_out = refs[7:11]
    bgkv, bekv, bgout, beout, sems, nkv, nout, nsems = refs[11:]
    chunks = [my_chunk(j // 4, (j // 2) % 2, j % 2) for j in range(8)]
    copies = [loads((gkv, ekv, gout, eout), (bgkv, bekv, bgout, beout), sems, j, chunks[j]) for j in range(8)]
    for chunk in copies:
        for copy in chunk:
            copy.start()
    packed = []
    for k, (at, n) in enumerate(((0, COLS), (COLS, COLS), (2 * COLS, OCOLS))):
        w1, w2, w3 = split3(w[k])
        r1, r2, r3 = split3(total[:, at : at + n] * (1.0 / REPLICAS))
        right = dot(
            jnp.concatenate([w1, w1, w2, w1, w2, w3], axis=1),
            jnp.concatenate([r1, r2, r1, r3, r2, r1], axis=0),
        )
        if k < 2:
            right_kv[k] = right
        else:
            right_out[...] = right
        high, low = split2(right)
        packed.append(jnp.concatenate([high, high, low, jnp.zeros_like(high)], axis=0))
    stores = []
    for j in range(8):
        for copy in copies[j]:
            copy.wait()
        for s in range(2):
            merged = bgkv[j, s].astype(F32) + bekv[j, s].astype(F32)
            nkv[j, s] = (merged - dot(ortho[j, s, :CH], packed[s])).astype(BF16)
            rows = slice(s * HALF, (s + 1) * HALF)
            merged = bgout[j, rows].astype(F32) + beout[j, rows].astype(F32)
            nout[j, rows] = (merged - dot(ortho[j, s, CH:], packed[2])).astype(BF16)
        rows = pl.ds(pl.multiple_of(chunks[j] * CH, CH), CH)
        orows = pl.ds(pl.multiple_of(chunks[j] * OCH, OCH), OCH)
        stores.append(pltpu.make_async_copy(nkv.at[j], new_kv.at[0, :, rows, :], nsems.at[j, 0]))
        stores.append(pltpu.make_async_copy(nout.at[j], new_out.at[0, orows, :], nsems.at[j, 1]))
        stores[-2].start()
        stores[-1].start()
    for copy in stores:
        copy.wait()


def errors(args, total, w, ortho):
    return pl.pallas_call(
        error_kernel,
        out_shape=(
            jax.ShapeDtypeStruct((2, RANK, COLS), F32),
            jax.ShapeDtypeStruct((RANK, OCOLS), F32),
            jax.ShapeDtypeStruct((1, 2, ROWS, COLS), BF16),
            jax.ShapeDtypeStruct((1, OROWS, OCOLS), BF16),
        ),
        in_specs=[ANY] * 4 + [VM] * 3,
        out_specs=(VM, VM, ANY, ANY),
        scratch_shapes=buffers(8)
        + [
            pltpu.VMEM((8, 2, CH, COLS), BF16),
            pltpu.VMEM((8, OCH, OCOLS), BF16),
            pltpu.SemaphoreType.DMA((8, 2)),
        ],
        compiler_params=pltpu.CompilerParams(vmem_limit_bytes=40 * MIB),
        cost_estimate=pl.CostEstimate(flops=800_000_000, bytes_accessed=29 * MIB, transcendentals=0),
        name="errors",
    )(*args, total, w, ortho)


X, Y, Z = 0, 1, 2


def on_device(grad_kv, error_kv, grad_out, error_out, basis_kv, basis_out):
    grads = (grad_kv, error_kv, grad_out, error_out)
    args = (*grads, jnp.swapaxes(basis_kv, 1, 2), basis_out.T)
    got = send(part(1, args), CORES)
    kept = part(0, args) + got
    a, b = [kept[:, s].reshape(2, 2, RANK, WIDE) for s in range(2)]

    a = a[0] + send(a[1], exchange(X, 0))
    b = b[:, 0] + send(b[:, 1], exchange(Y, 0))
    a = a[0] + send(a[1], exchange(Y, 0))
    b = b[0] + send(b[1], exchange(X, 0))
    for axis_a, axis_b in (((Z, 0), (Y, 1)), ((X, 1), (Z, 0)), ((Z, 1), (X, 1)), ((Y, 1), (Z, 1))):
        a, b = a + send(a, exchange(*axis_a)), b + send(b, exchange(*axis_b))
    a_own = jnp.stack([a, send(a, exchange(Y, 0))])
    b_own = jnp.stack([b, send(b, exchange(X, 0))])
    a_got = send(a_own, exchange(X, 0))
    b_got = send(b_own, exchange(Y, 0))
    own = (a_own, a_got, b_own, b_got)
    other = [send(p, CORES) for p in own]

    total, gram = right_part(1, grads, other, right_part(0, grads, own))
    w = factor(gram)
    left_kv, left_out, ortho = left_part(own, other, w)
    for axis, turn in ((Y, 0), (Z, 0), (Y, 1), (Z, 1)):
        total = total + send(total, exchange(axis, turn))
    right_kv, right_out, new_kv, new_out = errors(grads, total, w, ortho)
    return (
        jnp.swapaxes(left_kv, 1, 2),
        left_out.T,
        jnp.swapaxes(right_kv, 1, 2),
        right_out.T,
        new_kv,
        new_out,
    )


def solution(mesh):
    placed = (
        P("dp", None, None, "mp"),
        P("dp", None, None, "mp"),
        P("dp", None, "mp"),
        P("dp", None, "mp"),
        P(None, "mp", None),
        P("mp", None),
    )
    return jax.shard_map(
        on_device,
        mesh=mesh,
        in_specs=placed,
        out_specs=(
            P(),
            P(),
            P(None, "mp", None),
            P("mp", None),
            P("dp", None, None, "mp"),
            P("dp", None, "mp"),
        ),
        check_vma=False,
    )
```

time: 341 us -> 130 us (0.38)
  waiting for transfers between devices: 154 us -> 34.1 us
  matrix products: 79.1 us -> 0 us
  blocking collectives: 73.5 us -> 0 us
  starting transfers between devices: 0.26 us -> 40.3 us
  Pallas kernels: 0 us -> 32.7 us
  local copies, waits for them, and re-layouts: 0.96 us -> 20.2 us
  other arithmetic: 18.6 us -> 0.52 us
  between operations: 14.1 us -> 1.11 us
    psum x2 -> x0, waiting for transfers between devices: 154 us -> none  [the longest x1 154 us: on_device(): lead_kv, lead_out = lax.psum((part_kv, part_out), ('dp', 'mp'))]
    psum x1 -> x0, blocking collectives: 73.5 us -> none  [on_device(): sum_kv, sum_out = lax.psum((local_kv, local_out), 'dp')]
    dot_general x8 -> x0, matrix products: 72.7 us -> none  [the longest x1 16.4 us: on_device(): jnp.einsum('adr,acr->adc', ortho_kv, right_kv, precision=HIGH)]
    ppermute x0 -> x25, starting transfers between devices: none -> 40.3 us  [send(): return lax.ppermute(x, ('dp', 'mp'), pairs)]
    ppermute x0 -> x25, waiting for transfers between devices: none -> 34.1 us  [send(): return lax.ppermute(x, ('dp', 'mp'), pairs)]
    pallas_call x0 -> x7, Pallas kernels: none -> 32.7 us  [the longest x1 9.04 us: errors(): pl.pallas_call(error_kernel, out_shape=(jax.ShapeDtypeStruct((2, RANK, CO...]
    unnamed x16 -> x26, local copies, waits for them, and re-layouts: 0.81 us -> 20 us
    another operation x12 -> x2, other arithmetic: 17.7 us -> 0.07 us  [the longest x1 0.04 us: on_device(): b_own = jnp.stack([b, send(b, exchange(X, 0))])]
  transfers between devices with their start and end apart: 2 -> 25, of which waited for: 1 -> 15; matrix products, arithmetic and copies ran while one was open for 9% -> 0% of each run, Pallas kernels for 0% -> 12%
where the time goes in v1:
time: 130 us; the launch traced here: 129 us
  starting transfers between devices  40.3 us (31%)
  waiting for transfers between devices  34.1 us (26%)
  Pallas kernels  32.7 us (25%)
  local copies, waits for them, and re-layouts  20.2 us (16%)
    ppermute x25, starting transfers between devices, send(): return lax.ppermute(x, ('dp', 'mp'), pairs)  40.3 us
    ppermute x25, waiting for transfers between devices, send(): return lax.ppermute(x, ('dp', 'mp'), pairs)  34.1 us
    unnamed x26, local copies, waits for them, and re-layouts  20 us
    pallas_call x1, Pallas kernels, errors(): pl.pallas_call(error_kernel, out_shape=(jax.ShapeDtypeStruct((2, RANK, CO...  9.04 us
    pallas_call x2, Pallas kernels, right_part(): pl.pallas_call(functools.partial(right_kernel, dh, not before), out_shape...  8.86 us
    pallas_call x2, Pallas kernels, part(): pl.pallas_call(functools.partial(part_kernel, dh), out_shape=jax.ShapeDty...  7.66 us
    pallas_call x1, Pallas kernels, factor(): pl.pallas_call(factor_kernel, out_shape=jax.ShapeDtypeStruct((3, RANK, RA...  4.29 us
    pallas_call x1, Pallas kernels, left_part(): pl.pallas_call(left_kernel, out_shape=(jax.ShapeDtypeStruct((2, RANK, ROW...  2.86 us
  transfers between devices with their start and end apart: 25, of which 15 were waited for; matrix products, arithmetic and copies ran while one was open for 0% of the time, Pallas kernels for 12%

profile of v1, /device:TPU:0, one launch (start us, length us, event | category | flops | bytes accessed | tf_op | source)
XLA Modules:
  0.0 129.0 jit_solution(10536704181304881791)
XLA Ops:
  0.6 0.0 copy-start
  0.6 2.2 %copy-done = bf16[1,2,8192,128]{3,2,1,0:T(8,128)(2,1)S(1)} copy-done((bf16[1,2,8192,128]{3,2,1,0:T(8,128)(2,1)S(1)}, bf16[1,2,8192,128]{3,2,1,0:T(8,128)(2,1)}, u32[]{:S(2)}) %copy-start) | copy-done | bytes 4194328
  2.8 2.2 %copy-done.2 = bf16[1,2,8192,128]{3,2,1,0:T(8,128)(2,1)S(1)} copy-done((bf16[1,2,8192,128]{3,2,1,0:T(8,128)(2,1)S(1)}, bf16[1,2,8192,128]{3,2,1,0:T(8,128)(2,1)}, u32[]{:S(2)}) %copy-start.2) | copy-done | bytes 4194328
  5.0 2.2 %copy-done.4 = bf16[1,4096,512]{2,1,0:T(8,128)(2,1)S(1)} copy-done((bf16[1,4096,512]{2,1,0:T(8,128)(2,1)S(1)}, bf16[1,4096,512]{2,1,0:T(8,128)(2,1)}, u32[]{:S(2)}) %copy-start.4) | copy-done | bytes 4194328
  7.2 2.2 %copy-done.6 = bf16[1,4096,512]{2,1,0:T(8,128)(2,1)S(1)} copy-done((bf16[1,4096,512]{2,1,0:T(8,128)(2,1)S(1)}, bf16[1,4096,512]{2,1,0:T(8,128)(2,1)}, u32[]{:S(2)}) %copy-start.6) | copy-done | bytes 4194328
  9.4 0.8 copy-done.10
  10.2 0.8 copy-done.11
  11.0 3.8 %part.3 = f32[4,2,32,1280]{3,2,1,0:T(8,128)S(1)} custom-call(bf16[1,2,8192,128]{3,2,1,0:T(8,128)(2,1)S(1)} %copy-done, bf16[1,2,8192,128]{3,2,1,0:T(8,128)(2,1)S(1)} %copy-done.2, bf16[1,4096,512]{2,1,0:T(8,128)(2,1)S(1)} %copy-done.4, bf16[1,4096,512]{2,1,0:T(8,128)(2,1)S(1)} %copy-done.6, f32[2,32,128]{2,1,0:T(8,128)S(1)} %bitcast.41, f32[32,512]{1,0:T(8,128)S(1)} %bitcast.39), custom_call_target="tpu_custom_call" | custom-call | flops 800000000 | bytes 9437184 | tf_op jit(solution)/shard_map/part/pallas_call | solution.py:126
  14.8 0.1 copy.14
  14.9 0.1 collective-permute-start
  15.0 3.8 %part.2 = f32[4,2,32,1280]{3,2,1,0:T(8,128)S(1)} custom-call(bf16[1,2,8192,128]{3,2,1,0:T(8,128)(2,1)S(1)} %copy-done, bf16[1,2,8192,128]{3,2,1,0:T(8,128)(2,1)S(1)} %copy-done.2, bf16[1,4096,512]{2,1,0:T(8,128)(2,1)S(1)} %copy-done.4, bf16[1,4096,512]{2,1,0:T(8,128)(2,1)S(1)} %copy-done.6, f32[2,32,128]{2,1,0:T(8,128)S(1)} %bitcast.42, f32[32,512]{1,0:T(8,128)S(1)} %bitcast.40), custom_call_target="tpu_custom_call" | custom-call | flops 800000000 | bytes 9437184 | tf_op jit(solution)/shard_map/part/pallas_call | solution.py:126
  18.9 0.1 copy_add_fusion
  19.1 1.7 %collective-permute-start.9 = (f32[2,32,1280]{2,1,0:T(8,128)S(1)}, f32[2,32,1280]{2,1,0:T(8,128)S(1)}, u32[]{:S(2)}, u32[]{:S(2)}) collective-permute-start(f32[2,32,1280]{2,1,0:T(8,128)S(1)} %slice_bitcast_fusion), channel_id=1, source_target_pairs={{0,32},{1,97},{2,34},{3,99},{4,36},{5,101},{6,38},{7,103},{8,40},{... | collective-permute-start | bytes 983048 | tf_op jit(solution)/shard_map/ppermute | solution.py:35
  20.9 1.6 %collective-permute-start.1 = (f32[2,32,1280]{2,1,0:T(8,128)S(1)}, f32[2,32,1280]{2,1,0:T(8,128)S(1)}, u32[]{:S(2)}, u32[]{:S(2)}) collective-permute-start(f32[2,32,1280]{2,1,0:T(8,128)S(1)} %slice_bitcast_fusion.2), channel_id=1, source_target_pairs={{0,2},{1,7},{2,0},{3,5},{4,6},{5,3},{6,4},{7,1},{8,10},{9,15},{10,... | collective-permute-start | bytes 983048 | tf_op jit(solution)/shard_map/ppermute | solution.py:35
  22.4 3.8 %collective-permute-done.9 = f32[2,32,1280]{2,1,0:T(8,128)S(1)} collective-permute-done((f32[2,32,1280]{2,1,0:T(8,128)S(1)}, f32[2,32,1280]{2,1,0:T(8,128)S(1)}, u32[]{:S(2)}, u32[]{:S(2)}) %collective-permute-start.9) | collective-permute-done | bytes 327712 | tf_op jit(solution)/shard_map/ppermute | solution.py:35
  26.3 1.6 %collective-permute-start.10 = (f32[32,1280]{1,0:T(8,128)S(1)}, f32[32,1280]{1,0:T(8,128)S(1)}, u32[]{:S(2)}, u32[]{:S(2)}) collective-permute-start(f32[32,1280]{1,0:T(8,128)S(1)} %slice_bitcast_fusion.4), channel_id=1, source_target_pairs={{0,2},{1,7},{2,0},{3,5},{4,6},{5,3},{6,4},{7,1},{8,10},{9,15},{10,... | collective-permute-start | bytes 491528 | tf_op jit(solution)/shard_map/ppermute | solution.py:35
  27.9 0.1 collective-permute-done.1
  28.1 1.6 %collective-permute-start.2 = (f32[32,1280]{1,0:T(8,128)S(1)}, f32[32,1280]{1,0:T(8,128)S(1)}, u32[]{:S(2)}, u32[]{:S(2)}) collective-permute-start(f32[32,1280]{1,0:T(8,128)S(1)} %slice_bitcast_fusion.6), channel_id=1, source_target_pairs={{0,32},{1,97},{2,34},{3,99},{4,36},{5,101},{6,38},{7,103},{8,40},{... | collective-permute-start | bytes 491528 | tf_op jit(solution)/shard_map/ppermute | solution.py:35
  29.7 2.0 %collective-permute-done.10 = f32[32,1280]{1,0:T(8,128)S(1)} collective-permute-done((f32[32,1280]{1,0:T(8,128)S(1)}, f32[32,1280]{1,0:T(8,128)S(1)}, u32[]{:S(2)}, u32[]{:S(2)}) %collective-permute-start.10) | collective-permute-done | bytes 163872 | tf_op jit(solution)/shard_map/ppermute | solution.py:35
  31.7 3.2 %collective-permute-start.11 = (f32[32,1280]{1,0:T(8,128)S(1)}, f32[32,1280]{1,0:T(8,128)S(1)}, u32[]{:S(2)}, u32[]{:S(2)}) collective-permute-start(f32[32,1280]{1,0:T(8,128)S(1)} %fusion.2), channel_id=1, source_target_pairs={{0,96},{1,33},{2,98},{3,35},{4,100},{5,37},{6,102},{7,39},{8,104},... | collective-permute-start | bytes 491528 | tf_op jit(solution)/shard_map/ppermute | solution.py:35
  34.9 2.0 %collective-permute-start.3 = (f32[32,1280]{1,0:T(8,128)S(1)}, f32[32,1280]{1,0:T(8,128)S(1)}, u32[]{:S(2)}, u32[]{:S(2)}) collective-permute-start(f32[32,1280]{1,0:T(8,128)S(1)} %fusion.3), channel_id=1, source_target_pairs={{0,8},{1,25},{2,10},{3,27},{4,12},{5,29},{6,14},{7,31},{8,0},{9,17... | collective-permute-start | bytes 491528 | tf_op jit(solution)/shard_map/ppermute | solution.py:35
  36.9 1.4 %collective-permute-done.11 = f32[32,1280]{1,0:T(8,128)S(1)} collective-permute-done((f32[32,1280]{1,0:T(8,128)S(1)}, f32[32,1280]{1,0:T(8,128)S(1)}, u32[]{:S(2)}, u32[]{:S(2)}) %collective-permute-start.11) | collective-permute-done | bytes 163872 | tf_op jit(solution)/shard_map/ppermute | solution.py:35
  38.4 2.1 %collective-permute-start.12 = (f32[32,1280]{1,0:T(8,128)S(1)}, f32[32,1280]{1,0:T(8,128)S(1)}, u32[]{:S(2)}, u32[]{:S(2)}) collective-permute-start(f32[32,1280]{1,0:T(8,128)S(1)} %add.60), channel_id=1, source_target_pairs={{0,8},{1,25},{2,10},{3,27},{4,12},{5,29},{6,14},{7,31},{8,0},{9,17... | collective-permute-start | bytes 491528 | tf_op jit(solution)/shard_map/ppermute | solution.py:35
  40.5 2.8 %collective-permute-start.4 = (f32[32,1280]{1,0:T(8,128)S(1)}, f32[32,1280]{1,0:T(8,128)S(1)}, u32[]{:S(2)}, u32[]{:S(2)}) collective-permute-start(f32[32,1280]{1,0:T(8,128)S(1)} %add.54), channel_id=1, source_target_pairs={{0,6},{1,3},{2,4},{3,1},{4,2},{5,7},{6,0},{7,5},{8,14},{9,11},{10,... | collective-permute-start | bytes 491528 | tf_op jit(solution)/shard_map/ppermute | solution.py:35
  43.3 0.5 collective-permute-done.12
  43.8 2.9 %collective-permute-start.13 = (f32[32,1280]{1,0:T(8,128)S(1)}, f32[32,1280]{1,0:T(8,128)S(1)}, u32[]{:S(2)}, u32[]{:S(2)}) collective-permute-start(f32[32,1280]{1,0:T(8,128)S(1)} %add.61), channel_id=1, source_target_pairs={{0,6},{1,3},{2,4},{3,1},{4,2},{5,7},{6,0},{7,5},{8,14},{9,11},{10,... | collective-permute-start | bytes 491528 | tf_op jit(solution)/shard_map/ppermute | solution.py:35
  46.7 0.4 collective-permute-done.4
  47.1 4.0 %collective-permute-start.5 = (f32[32,1280]{1,0:T(8,128)S(1)}, f32[32,1280]{1,0:T(8,128)S(1)}, u32[]{:S(2)}, u32[]{:S(2)}) collective-permute-start(f32[32,1280]{1,0:T(8,128)S(1)} %add.55), channel_id=1, source_target_pairs={{0,24},{1,9},{2,26},{3,11},{4,28},{5,13},{6,30},{7,15},{8,16},{9,1... | collective-permute-start | bytes 491528 | tf_op jit(solution)/shard_map/ppermute | solution.py:35
  51.1 0.0 collective-permute-done.13
  51.1 3.5 %collective-permute-start.14 = (f32[32,1280]{1,0:T(8,128)S(1)}, f32[32,1280]{1,0:T(8,128)S(1)}, u32[]{:S(2)}, u32[]{:S(2)}) collective-permute-start(f32[32,1280]{1,0:T(8,128)S(1)} %add.62), channel_id=1, source_target_pairs={{0,24},{1,9},{2,26},{3,11},{4,28},{5,13},{6,30},{7,15},{8,16},{9,1... | collective-permute-start | bytes 491528 | tf_op jit(solution)/shard_map/ppermute | solution.py:35
  54.6 0.0 collective-permute-done.5
  54.6 3.1 %collective-permute-start.6 = (f32[32,1280]{1,0:T(8,128)S(1)}, f32[32,1280]{1,0:T(8,128)S(1)}, u32[]{:S(2)}, u32[]{:S(2)}) collective-permute-start(f32[32,1280]{1,0:T(8,128)S(1)} %add.56), channel_id=1, source_target_pairs={{0,96},{1,33},{2,98},{3,35},{4,100},{5,37},{6,102},{7,39},{8,104},... | collective-permute-start | bytes 491528 | tf_op jit(solution)/shard_map/ppermute | solution.py:35
  57.7 0.2 collective-permute-done.14
  57.9 0.4 collective-permute-start.15
  58.3 4.0 %collective-permute-done.6 = f32[32,1280]{1,0:T(8,128)S(1)} collective-permute-done((f32[32,1280]{1,0:T(8,128)S(1)}, f32[32,1280]{1,0:T(8,128)S(1)}, u32[]{:S(2)}, u32[]{:S(2)}) %collective-permute-start.6) | collective-permute-done | bytes 163872 | tf_op jit(solution)/shard_map/ppermute | solution.py:35
  62.3 0.1 collective-permute-start.7
  62.4 0.9 collective-permute-done.15
  63.4 1.2 collective-permute-start.16
  64.6 3.2 %collective-permute-done.7 = f32[32,1280]{1,0:T(8,128)S(1)} collective-permute-done((f32[32,1280]{1,0:T(8,128)S(1)}, f32[32,1280]{1,0:T(8,128)S(1)}, u32[]{:S(2)}, u32[]{:S(2)}) %collective-permute-start.7) | collective-permute-done | bytes 163872 | tf_op jit(solution)/shard_map/ppermute | solution.py:35
  67.8 0.9 collective-permute-start.8
  68.7 0.0 collective-permute-start.19
  68.7 0.5 collective-permute-start.17
  69.2 2.0 %collective-permute-done.16.refs_7_.refs_3_ = f32[2,32,1280]{2,1,0:T(8,128)S(1)} collective-permute-done((f32[2,32,1280]{2,1,0:T(8,128)S(1)}, f32[2,32,1280]{2,1,0:T(8,128)S(1)}, u32[]{:S(2)}, u32[]{:S(2)}) %collective-permute-start.16) | collective-permute-done | bytes 327712 | tf_op jit(solution)/shard_map/ppermute | solution.py:35
  71.3 3.7 %collective-permute-done.8.refs_5_.refs_1_ = f32[2,32,1280]{2,1,0:T(8,128)S(1)} collective-permute-done((f32[2,32,1280]{2,1,0:T(8,128)S(1)}, f32[2,32,1280]{2,1,0:T(8,128)S(1)}, u32[]{:S(2)}, u32[]{:S(2)}) %collective-permute-start.8) | collective-permute-done | bytes 327712 | tf_op jit(solution)/shard_map/ppermute | solution.py:35
  74.9 0.0 collective-permute-start.18
  74.9 4.4 %right.2 = (f32[32,768]{1,0:T(8,128)S(1)}, f32[3,32,32]{2,1,0:T(8,128)S(1)}) custom-call(bf16[1,2,8192,128]{3,2,1,0:T(8,128)(2,1)S(1)} %copy-done, bf16[1,2,8192,128]{3,2,1,0:T(8,128)(2,1)S(1)} %copy-done.2, bf16[1,4096,512]{2,1,0:T(8,128)(2,1)S(1)} %copy-done.4, bf16[1,4096,512]{2,1,0:T(8,128)(2,1)S(1)} %copy-done.6, ...), custom_call_target="tpu_custom_call" | custom-call | flops 800000000 | bytes 9437184 | tf_op jit(solution)/shard_map/right/pallas_call | solution.py:194
  79.4 4.5 %right.3 = (f32[32,768]{1,0:T(8,128)S(1)}, f32[3,32,32]{2,1,0:T(8,128)S(1)}) custom-call(bf16[1,2,8192,128]{3,2,1,0:T(8,128)(2,1)S(1)} %copy-done, bf16[1,2,8192,128]{3,2,1,0:T(8,128)(2,1)S(1)} %copy-done.2, bf16[1,4096,512]{2,1,0:T(8,128)(2,1)S(1)} %copy-done.4, bf16[1,4096,512]{2,1,0:T(8,128)(2,1)S(1)} %copy-done.6, ...), custom_call_target="tpu_custom_call" | custom-call | flops 800000000 | bytes 9437184 | tf_op jit(solution)/shard_map/right/pallas_call | solution.py:194
  83.9 0.0 copy-start.12
  83.9 0.1 collective-permute-start.21
  84.0 4.6 %collective-permute-done.21 = f32[32,768]{1,0:T(8,128)S(1)} collective-permute-done((f32[32,768]{1,0:T(8,128)S(1)}, f32[32,768]{1,0:T(8,128)S(1)}, u32[]{:S(2)}, u32[]{:S(2)}) %collective-permute-start.21) | collective-permute-done | bytes 98336 | tf_op jit(solution)/shard_map/ppermute | solution.py:35
  88.6 0.1 collective-permute-start.22
  88.7 4.6 %collective-permute-done.22 = f32[32,768]{1,0:T(8,128)S(1)} collective-permute-done((f32[32,768]{1,0:T(8,128)S(1)}, f32[32,768]{1,0:T(8,128)S(1)}, u32[]{:S(2)}, u32[]{:S(2)}) %collective-permute-start.22) | collective-permute-done | bytes 98336 | tf_op jit(solution)/shard_map/ppermute | solution.py:35
  93.3 3.1 %collective-permute-start.23 = (f32[32,768]{1,0:T(8,128)S(1)}, f32[32,768]{1,0:T(8,128)S(1)}, u32[]{:S(2)}, u32[]{:S(2)}) collective-permute-start(f32[32,768]{1,0:T(8,128)S(1)} %add.65), channel_id=1, source_target_pairs={{0,96},{1,33},{2,98},{3,35},{4,100},{5,37},{6,102},{7,39},{8,104},... | collective-permute-start | bytes 294920 | tf_op jit(solution)/shard_map/ppermute | solution.py:35
  96.4 2.8 %collective-permute-done.23 = f32[32,768]{1,0:T(8,128)S(1)} collective-permute-done((f32[32,768]{1,0:T(8,128)S(1)}, f32[32,768]{1,0:T(8,128)S(1)}, u32[]{:S(2)}, u32[]{:S(2)}) %collective-permute-start.23) | collective-permute-done | bytes 98336 | tf_op jit(solution)/shard_map/ppermute | solution.py:35
  99.2 3.7 %collective-permute-start.24 = (f32[32,768]{1,0:T(8,128)S(1)}, f32[32,768]{1,0:T(8,128)S(1)}, u32[]{:S(2)}, u32[]{:S(2)}) collective-permute-start(f32[32,768]{1,0:T(8,128)S(1)} %add.66), channel_id=1, source_target_pairs={{0,24},{1,9},{2,26},{3,11},{4,28},{5,13},{6,30},{7,15},{8,16},{9,1... | collective-permute-start | bytes 294920 | tf_op jit(solution)/shard_map/ppermute | solution.py:35
  102.9 4.3 %factor.1.refs_8_.refs_5_ = f32[3,32,32]{2,1,0:T(8,128)} custom-call(f32[3,32,32]{2,1,0:T(8,128)} %copy-done.12), custom_call_target="tpu_custom_call" | custom-call | flops 10000000 | bytes 3145728 | tf_op jit(solution)/shard_map/factor/pallas_call | solution.py:228
  107.2 0.8 copy-done.8
  108.0 2.9 %left.1 = (f32[2,32,8192]{2,1,0:T(8,128)}, f32[32,4096]{1,0:T(8,128)}, bf16[8,2,1280,128]{3,2,1,0:T(8,128)(2,1)S(1)}) custom-call(f32[2,32,1280]{2,1,0:T(8,128)S(1)} %pad_maximum_fusion.refs_4_.refs_0_, f32[2,32,1280]{2,1,0:T(8,128)S(1)} %collective-permute-done.8.refs_5_.refs_1_, f32[2,32,1280]{2,1,0:T(8,128)S(1)} %pad_maximum_fusion.1.refs_6_.refs_2_, ...), custom_call_target="tpu_custom_call" | custom-call | flops 500000000 | bytes 10485760 | tf_op jit(solution)/shard_map/left/pallas_call | solution.py:282
  110.9 2.3 %copy-done.7 = bf16[8,2,1280,128]{3,2,1,0:T(8,128)(2,1)} copy-done((bf16[8,2,1280,128]{3,2,1,0:T(8,128)(2,1)}, bf16[8,2,1280,128]{3,2,1,0:T(8,128)(2,1)S(1)}, u32[]{:S(2)}) %copy-start.7) | copy-done | bytes 5242904
  113.2 0.0 copy-start.1
  113.2 2.2 %copy-done.1 = bf16[1,2,8192,128]{3,2,1,0:T(8,128)(2,1)S(1)} copy-done((bf16[1,2,8192,128]{3,2,1,0:T(8,128)(2,1)S(1)}, bf16[1,2,8192,128]{3,2,1,0:T(8,128)(2,1)}, u32[]{:S(2)}) %copy-start.1) | copy-done | bytes 4194328
  115.4 2.2 %copy-done.3 = bf16[1,2,8192,128]{3,2,1,0:T(8,128)(2,1)S(1)} copy-done((bf16[1,2,8192,128]{3,2,1,0:T(8,128)(2,1)S(1)}, bf16[1,2,8192,128]{3,2,1,0:T(8,128)(2,1)}, u32[]{:S(2)}) %copy-start.3) | copy-done | bytes 4194328
  117.6 2.2 %copy-done.5 = bf16[1,4096,512]{2,1,0:T(8,128)(2,1)S(1)} copy-done((bf16[1,4096,512]{2,1,0:T(8,128)(2,1)S(1)}, bf16[1,4096,512]{2,1,0:T(8,128)(2,1)}, u32[]{:S(2)}) %copy-start.5) | copy-done | bytes 4194328
  119.8 9.0 %errors.1 = (f32[2,32,128]{2,1,0:T(8,128)}, f32[32,512]{1,0:T(8,128)}, bf16[1,2,8192,128]{3,2,1,0:T(8,128)(2,1)}, bf16[1,4096,512]{2,1,0:T(8,128)(2,1)}) custom-call(bf16[1,2,8192,128]{3,2,1,0:T(8,128)(2,1)S(1)} %copy-done.1, bf16[1,2,8192,128]{3,2,1,0:T(8,128)(2,1)S(1)} %copy-done.3, bf16[1,4096,512]{2,1,0:T(8,128)(2,1)S(1)} %copy-done.5, ...), custom_call_target="tpu_custom_call" | custom-call | flops 800000000 | bytes 30408704 | tf_op jit(solution)/shard_map/errors/pallas_call | solution.py:346
  (44 shorter events, 0.5 us)
Async XLA Ops:
  0.6 2.2 %copy-start = (bf16[1,2,8192,128]{3,2,1,0:T(8,128)(2,1)S(1)}, bf16[1,2,8192,128]{3,2,1,0:T(8,128)(2,1)}, u32[]{:S(2)}) copy-start(bf16[1,2,8192,128]{3,2,1,0:T(8,128)(2,1)} %refs_0_.5) | copy-start | bytes 12582916
  2.8 2.2 %copy-start.2 = (bf16[1,2,8192,128]{3,2,1,0:T(8,128)(2,1)S(1)}, bf16[1,2,8192,128]{3,2,1,0:T(8,128)(2,1)}, u32[]{:S(2)}) copy-start(bf16[1,2,8192,128]{3,2,1,0:T(8,128)(2,1)} %refs_1_.5) | copy-start | bytes 12582916
  5.0 2.2 %copy-start.4 = (bf16[1,4096,512]{2,1,0:T(8,128)(2,1)S(1)}, bf16[1,4096,512]{2,1,0:T(8,128)(2,1)}, u32[]{:S(2)}) copy-start(bf16[1,4096,512]{2,1,0:T(8,128)(2,1)} %refs_2_.5) | copy-start | bytes 12582916
  7.2 2.2 %copy-start.6 = (bf16[1,4096,512]{2,1,0:T(8,128)(2,1)S(1)}, bf16[1,4096,512]{2,1,0:T(8,128)(2,1)}, u32[]{:S(2)}) copy-start(bf16[1,4096,512]{2,1,0:T(8,128)(2,1)} %refs_3_.5) | copy-start | bytes 12582916
  9.4 0.8 copy-start.10
  10.2 0.8 copy-start.11
  14.9 3.9 %collective-permute-start = (f32[4,2,32,1280]{3,2,0,1:T(8,128)S(1)}, f32[4,2,32,1280]{3,2,0,1:T(8,128)S(1)}, u32[]{:S(2)}, u32[]{:S(2)}) collective-permute-start(f32[4,2,32,1280]{3,2,0,1:T(8,128)S(1)} %copy.14), channel_id=1, source_target_pairs={{0,1},{1,0},{2,3},{3,2},{4,5},{5,4},{6,7},{7,6},{8,9},{9,8},{10,11... | collective-permute-start | bytes 3932168 | tf_op jit(solution)/shard_map/ppermute | solution.py:35
  19.1 7.2 %collective-permute-start.9 = (f32[2,32,1280]{2,1,0:T(8,128)S(1)}, f32[2,32,1280]{2,1,0:T(8,128)S(1)}, u32[]{:S(2)}, u32[]{:S(2)}) collective-permute-start(f32[2,32,1280]{2,1,0:T(8,128)S(1)} %slice_bitcast_fusion), channel_id=1, source_target_pairs={{0,32},{1,97},{2,34},{3,99},{4,36},{5,101},{6,38},{7,103},{8,40},{... | collective-permute-start | bytes 983048 | tf_op jit(solution)/shard_map/ppermute | solution.py:35
  20.9 7.2 %collective-permute-start.1 = (f32[2,32,1280]{2,1,0:T(8,128)S(1)}, f32[2,32,1280]{2,1,0:T(8,128)S(1)}, u32[]{:S(2)}, u32[]{:S(2)}) collective-permute-start(f32[2,32,1280]{2,1,0:T(8,128)S(1)} %slice_bitcast_fusion.2), channel_id=1, source_target_pairs={{0,2},{1,7},{2,0},{3,5},{4,6},{5,3},{6,4},{7,1},{8,10},{9,15},{10,... | collective-permute-start | bytes 983048 | tf_op jit(solution)/shard_map/ppermute | solution.py:35
  26.3 5.4 %collective-permute-start.10 = (f32[32,1280]{1,0:T(8,128)S(1)}, f32[32,1280]{1,0:T(8,128)S(1)}, u32[]{:S(2)}, u32[]{:S(2)}) collective-permute-start(f32[32,1280]{1,0:T(8,128)S(1)} %slice_bitcast_fusion.4), channel_id=1, source_target_pairs={{0,2},{1,7},{2,0},{3,5},{4,6},{5,3},{6,4},{7,1},{8,10},{9,15},{10,... | collective-permute-start | bytes 491528 | tf_op jit(solution)/shard_map/ppermute | solution.py:35
  28.1 6.8 %collective-permute-start.2 = (f32[32,1280]{1,0:T(8,128)S(1)}, f32[32,1280]{1,0:T(8,128)S(1)}, u32[]{:S(2)}, u32[]{:S(2)}) collective-permute-start(f32[32,1280]{1,0:T(8,128)S(1)} %slice_bitcast_fusion.6), channel_id=1, source_target_pairs={{0,32},{1,97},{2,34},{3,99},{4,36},{5,101},{6,38},{7,103},{8,40},{... | collective-permute-start | bytes 491528 | tf_op jit(solution)/shard_map/ppermute | solution.py:35
  31.7 6.6 %collective-permute-start.11 = (f32[32,1280]{1,0:T(8,128)S(1)}, f32[32,1280]{1,0:T(8,128)S(1)}, u32[]{:S(2)}, u32[]{:S(2)}) collective-permute-start(f32[32,1280]{1,0:T(8,128)S(1)} %fusion.2), channel_id=1, source_target_pairs={{0,96},{1,33},{2,98},{3,35},{4,100},{5,37},{6,102},{7,39},{8,104},... | collective-permute-start | bytes 491528 | tf_op jit(solution)/shard_map/ppermute | solution.py:35
  34.9 5.5 %collective-permute-start.3 = (f32[32,1280]{1,0:T(8,128)S(1)}, f32[32,1280]{1,0:T(8,128)S(1)}, u32[]{:S(2)}, u32[]{:S(2)}) collective-permute-start(f32[32,1280]{1,0:T(8,128)S(1)} %fusion.3), channel_id=1, source_target_pairs={{0,8},{1,25},{2,10},{3,27},{4,12},{5,29},{6,14},{7,31},{8,0},{9,17... | collective-permute-start | bytes 491528 | tf_op jit(solution)/shard_map/ppermute | solution.py:35
  38.4 5.4 %collective-permute-start.12 = (f32[32,1280]{1,0:T(8,128)S(1)}, f32[32,1280]{1,0:T(8,128)S(1)}, u32[]{:S(2)}, u32[]{:S(2)}) collective-permute-start(f32[32,1280]{1,0:T(8,128)S(1)} %add.60), channel_id=1, source_target_pairs={{0,8},{1,25},{2,10},{3,27},{4,12},{5,29},{6,14},{7,31},{8,0},{9,17... | collective-permute-start | bytes 491528 | tf_op jit(solution)/shard_map/ppermute | solution.py:35
  40.5 6.6 %collective-permute-start.4 = (f32[32,1280]{1,0:T(8,128)S(1)}, f32[32,1280]{1,0:T(8,128)S(1)}, u32[]{:S(2)}, u32[]{:S(2)}) collective-permute-start(f32[32,1280]{1,0:T(8,128)S(1)} %add.54), channel_id=1, source_target_pairs={{0,6},{1,3},{2,4},{3,1},{4,2},{5,7},{6,0},{7,5},{8,14},{9,11},{10,... | collective-permute-start | bytes 491528 | tf_op jit(solution)/shard_map/ppermute | solution.py:35
  43.8 7.3 %collective-permute-start.13 = (f32[32,1280]{1,0:T(8,128)S(1)}, f32[32,1280]{1,0:T(8,128)S(1)}, u32[]{:S(2)}, u32[]{:S(2)}) collective-permute-start(f32[32,1280]{1,0:T(8,128)S(1)} %add.61), channel_id=1, source_target_pairs={{0,6},{1,3},{2,4},{3,1},{4,2},{5,7},{6,0},{7,5},{8,14},{9,11},{10,... | collective-permute-start | bytes 491528 | tf_op jit(solution)/shard_map/ppermute | solution.py:35
  47.1 7.5 %collective-permute-start.5 = (f32[32,1280]{1,0:T(8,128)S(1)}, f32[32,1280]{1,0:T(8,128)S(1)}, u32[]{:S(2)}, u32[]{:S(2)}) collective-permute-start(f32[32,1280]{1,0:T(8,128)S(1)} %add.55), channel_id=1, source_target_pairs={{0,24},{1,9},{2,26},{3,11},{4,28},{5,13},{6,30},{7,15},{8,16},{9,1... | collective-permute-start | bytes 491528 | tf_op jit(solution)/shard_map/ppermute | solution.py:35
  51.1 6.8 %collective-permute-start.14 = (f32[32,1280]{1,0:T(8,128)S(1)}, f32[32,1280]{1,0:T(8,128)S(1)}, u32[]{:S(2)}, u32[]{:S(2)}) collective-permute-start(f32[32,1280]{1,0:T(8,128)S(1)} %add.62), channel_id=1, source_target_pairs={{0,24},{1,9},{2,26},{3,11},{4,28},{5,13},{6,30},{7,15},{8,16},{9,1... | collective-permute-start | bytes 491528 | tf_op jit(solution)/shard_map/ppermute | solution.py:35
  54.6 7.7 %collective-permute-start.6 = (f32[32,1280]{1,0:T(8,128)S(1)}, f32[32,1280]{1,0:T(8,128)S(1)}, u32[]{:S(2)}, u32[]{:S(2)}) collective-permute-start(f32[32,1280]{1,0:T(8,128)S(1)} %add.56), channel_id=1, source_target_pairs={{0,96},{1,33},{2,98},{3,35},{4,100},{5,37},{6,102},{7,39},{8,104},... | collective-permute-start | bytes 491528 | tf_op jit(solution)/shard_map/ppermute | solution.py:35
  57.9 5.4 %collective-permute-start.15 = (f32[32,1280]{1,0:T(8,128)S(1)}, f32[32,1280]{1,0:T(8,128)S(1)}, u32[]{:S(2)}, u32[]{:S(2)}) collective-permute-start(f32[32,1280]{1,0:T(8,128)S(1)} %add.63), channel_id=1, source_target_pairs={{0,2},{1,7},{2,0},{3,5},{4,6},{5,3},{6,4},{7,1},{8,10},{9,15},{10,... | collective-permute-start | bytes 491528 | tf_op jit(solution)/shard_map/ppermute | solution.py:35
  62.3 5.4 %collective-permute-start.7 = (f32[32,1280]{1,0:T(8,128)S(1)}, f32[32,1280]{1,0:T(8,128)S(1)}, u32[]{:S(2)}, u32[]{:S(2)}) collective-permute-start(f32[32,1280]{1,0:T(8,128)S(1)} %add.57), channel_id=1, source_target_pairs={{0,32},{1,97},{2,34},{3,99},{4,36},{5,101},{6,38},{7,103},{8,40},{... | collective-permute-start | bytes 491528 | tf_op jit(solution)/shard_map/ppermute | solution.py:35
  63.4 7.9 %collective-permute-start.16 = (f32[2,32,1280]{2,1,0:T(8,128)S(1)}, f32[2,32,1280]{2,1,0:T(8,128)S(1)}, u32[]{:S(2)}, u32[]{:S(2)}) collective-permute-start(f32[2,32,1280]{2,1,0:T(8,128)S(1)} %pad_maximum_fusion.1.refs_6_.refs_2_), channel_id=1, source_target_pairs={{0,32},{1,97},{2,34},{3,99},{4,36},{5,101},{6,38},{7,103},{8,40},{... | collective-permute-start | bytes 983048 | tf_op jit(solution)/shard_map/ppermute | solution.py:35
  67.8 7.2 %collective-permute-start.8 = (f32[2,32,1280]{2,1,0:T(8,128)S(1)}, f32[2,32,1280]{2,1,0:T(8,128)S(1)}, u32[]{:S(2)}, u32[]{:S(2)}) collective-permute-start(f32[2,32,1280]{2,1,0:T(8,128)S(1)} %pad_maximum_fusion.refs_4_.refs_0_), channel_id=1, source_target_pairs={{0,2},{1,7},{2,0},{3,5},{4,6},{5,3},{6,4},{7,1},{8,10},{9,15},{10,... | collective-permute-start | bytes 983048 | tf_op jit(solution)/shard_map/ppermute | solution.py:35
  68.7 10.7 %collective-permute-start.19 = (f32[2,32,1280]{2,1,0:T(8,128)S(1)}, f32[2,32,1280]{2,1,0:T(8,128)S(1)}, u32[]{:S(2)}, u32[]{:S(2)}) collective-permute-start(f32[2,32,1280]{2,1,0:T(8,128)S(1)} %pad_maximum_fusion.1.refs_6_.refs_2_), channel_id=1, source_target_pairs={{0,1},{1,0},{2,3},{3,2},{4,5},{5,4},{6,7},{7,6},{8,9},{9,8},{10,11... | collective-permute-start | bytes 983048 | tf_op jit(solution)/shard_map/ppermute | solution.py:35
  68.7 10.7 %collective-permute-start.17 = (f32[2,32,1280]{2,1,0:T(8,128)S(1)}, f32[2,32,1280]{2,1,0:T(8,128)S(1)}, u32[]{:S(2)}, u32[]{:S(2)}) collective-permute-start(f32[2,32,1280]{2,1,0:T(8,128)S(1)} %pad_maximum_fusion.refs_4_.refs_0_), channel_id=1, source_target_pairs={{0,1},{1,0},{2,3},{3,2},{4,5},{5,4},{6,7},{7,6},{8,9},{9,8},{10,11... | collective-permute-start | bytes 983048 | tf_op jit(solution)/shard_map/ppermute | solution.py:35
  71.3 8.1 %collective-permute-start.20 = (f32[2,32,1280]{2,1,0:T(8,128)S(1)}, f32[2,32,1280]{2,1,0:T(8,128)S(1)}, u32[]{:S(2)}, u32[]{:S(2)}) collective-permute-start(f32[2,32,1280]{2,1,0:T(8,128)S(1)} %collective-permute-done.16.refs_7_.refs_3_), channel_id=1, source_target_pairs={{0,1},{1,0},{2,3},{3,2},{4,5},{5,4},{6,7},{7,6},{8,9},{9,8},{10,11... | collective-permute-start | bytes 983048 | tf_op jit(solution)/shard_map/ppermute | solution.py:35
  74.9 4.5 %collective-permute-start.18 = (f32[2,32,1280]{2,1,0:T(8,128)S(1)}, f32[2,32,1280]{2,1,0:T(8,128)S(1)}, u32[]{:S(2)}, u32[]{:S(2)}) collective-permute-start(f32[2,32,1280]{2,1,0:T(8,128)S(1)} %collective-permute-done.8.refs_5_.refs_1_), channel_id=1, source_target_pairs={{0,1},{1,0},{2,3},{3,2},{4,5},{5,4},{6,7},{7,6},{8,9},{9,8},{10,11... | collective-permute-start | bytes 983048 | tf_op jit(solution)/shard_map/ppermute | solution.py:35
  83.9 4.7 %copy-start.12 = (f32[3,32,32]{2,1,0:T(8,128)}, f32[3,32,32]{2,1,0:T(8,128)S(1)}, u32[]{:S(2)}) copy-start(f32[3,32,32]{2,1,0:T(8,128)S(1)} %get-tuple-element.19.gram) | copy-start | bytes 36868
  83.9 4.7 %collective-permute-start.21 = (f32[32,768]{1,0:T(8,128)S(1)}, f32[32,768]{1,0:T(8,128)S(1)}, u32[]{:S(2)}, u32[]{:S(2)}) collective-permute-start(f32[32,768]{1,0:T(8,128)S(1)} %get-tuple-element.22), channel_id=1, source_target_pairs={{0,32},{1,97},{2,34},{3,99},{4,36},{5,101},{6,38},{7,103},{8,40},{... | collective-permute-start | bytes 294920 | tf_op jit(solution)/shard_map/ppermute | solution.py:35
  88.6 4.7 %collective-permute-start.22 = (f32[32,768]{1,0:T(8,128)S(1)}, f32[32,768]{1,0:T(8,128)S(1)}, u32[]{:S(2)}, u32[]{:S(2)}) collective-permute-start(f32[32,768]{1,0:T(8,128)S(1)} %add.64), channel_id=1, source_target_pairs={{0,8},{1,25},{2,10},{3,27},{4,12},{5,29},{6,14},{7,31},{8,0},{9,17... | collective-permute-start | bytes 294920 | tf_op jit(solution)/shard_map/ppermute | solution.py:35
  93.3 5.9 %collective-permute-start.23 = (f32[32,768]{1,0:T(8,128)S(1)}, f32[32,768]{1,0:T(8,128)S(1)}, u32[]{:S(2)}, u32[]{:S(2)}) collective-permute-start(f32[32,768]{1,0:T(8,128)S(1)} %add.65), channel_id=1, source_target_pairs={{0,96},{1,33},{2,98},{3,35},{4,100},{5,37},{6,102},{7,39},{8,104},... | collective-permute-start | bytes 294920 | tf_op jit(solution)/shard_map/ppermute | solution.py:35
  99.2 13.9 %collective-permute-start.24 = (f32[32,768]{1,0:T(8,128)S(1)}, f32[32,768]{1,0:T(8,128)S(1)}, u32[]{:S(2)}, u32[]{:S(2)}) collective-permute-start(f32[32,768]{1,0:T(8,128)S(1)} %add.66), channel_id=1, source_target_pairs={{0,24},{1,9},{2,26},{3,11},{4,28},{5,13},{6,30},{7,15},{8,16},{9,1... | collective-permute-start | bytes 294920 | tf_op jit(solution)/shard_map/ppermute | solution.py:35
  107.2 0.8 copy-start.8
  108.0 5.2 %copy-start.9 = (f32[3,32,32]{2,1,0:T(8,128)S(1)}, f32[3,32,32]{2,1,0:T(8,128)}, u32[]{:S(2)}) copy-start(f32[3,32,32]{2,1,0:T(8,128)} %factor.1.refs_8_.refs_5_) | copy-start | bytes 36868
  110.9 2.3 %copy-start.7 = (bf16[8,2,1280,128]{3,2,1,0:T(8,128)(2,1)}, bf16[8,2,1280,128]{3,2,1,0:T(8,128)(2,1)S(1)}, u32[]{:S(2)}) copy-start(bf16[8,2,1280,128]{3,2,1,0:T(8,128)(2,1)S(1)} %get-tuple-element.23.refs_6_) | copy-start | bytes 15728644
  113.2 2.2 %copy-start.1 = (bf16[1,2,8192,128]{3,2,1,0:T(8,128)(2,1)S(1)}, bf16[1,2,8192,128]{3,2,1,0:T(8,128)(2,1)}, u32[]{:S(2)}) copy-start(bf16[1,2,8192,128]{3,2,1,0:T(8,128)(2,1)} %refs_0_.5) | copy-start | bytes 12582916
  115.4 2.2 %copy-start.3 = (bf16[1,2,8192,128]{3,2,1,0:T(8,128)(2,1)S(1)}, bf16[1,2,8192,128]{3,2,1,0:T(8,128)(2,1)}, u32[]{:S(2)}) copy-start(bf16[1,2,8192,128]{3,2,1,0:T(8,128)(2,1)} %refs_1_.5) | copy-start | bytes 12582916
  117.6 2.2 %copy-start.5 = (bf16[1,4096,512]{2,1,0:T(8,128)(2,1)S(1)}, bf16[1,4096,512]{2,1,0:T(8,128)(2,1)}, u32[]{:S(2)}) copy-start(bf16[1,4096,512]{2,1,0:T(8,128)(2,1)} %refs_2_.5) | copy-start | bytes 12582916

commit v2 on v1

v2 whole, which is shorter than its diff:
```python
import functools

import jax
import jax.numpy as jnp
from jax import lax
from jax.experimental import pallas as pl
from jax.experimental.pallas import tpu as pltpu
from jax.sharding import PartitionSpec as P

F32, BF16 = jnp.float32, jnp.bfloat16
ROWS, COLS = 8192, 128
OROWS, OCOLS = 4096, 512
RANK = 32
REPLICAS = 16
CH = ROWS // 8
OCH = OROWS // 8
HALF = OCH // 2
WIDE = CH + HALF
MIB = 1 << 20


def exchange(axis, turn):
    pairs = []
    for i in range(128):
        q, core = [(i // 2) % 4, i // 32, (i // 8) % 4], i % 2
        q[axis] ^= 1 if turn == core else 3
        pairs.append((i, ((q[1] * 4 + q[2]) * 4 + q[0]) * 2 + core))
    return pairs


CORES = [(i, i ^ 1) for i in range(128)]


def send(x, pairs):
    return lax.ppermute(x, ("dp", "mp"), pairs)


def my_chunk(dh, du, dv):
    dp, mp = lax.axis_index("dp"), lax.axis_index("mp")
    x, y = lax.div(mp, 2), lax.div(dp, 4)
    half = jnp.bitwise_xor(lax.rem(mp, 2), dh)

    def own(q):
        high, low = lax.div(q, 2), lax.rem(q, 2)
        return jnp.bitwise_xor(high, low * (1 - half))

    u = jnp.bitwise_xor(own(x), du)
    v = jnp.bitwise_xor(own(y), dv)
    return half * 4 + u * 2 + v


def dot_nt(a, b):
    return lax.dot_general(a, b, (((1,), (1,)), ((), ())), preferred_element_type=F32)


def dot(a, b):
    return jnp.dot(a, b, preferred_element_type=F32)


def split2(a):
    high = a.astype(BF16)
    return high, (a - high.astype(F32)).astype(BF16)


def split3(a):
    high = a.astype(BF16)
    rest = a - high.astype(F32)
    mid = rest.astype(BF16)
    return high, mid, (rest - mid.astype(F32)).astype(BF16)


def loads(refs, bufs, sems, slot, chunk):
    rows = pl.ds(pl.multiple_of(chunk * CH, CH), CH)
    orows = pl.ds(pl.multiple_of(chunk * OCH, OCH), OCH)
    gkv, ekv, gout, eout = refs
    bgkv, bekv, bgout, beout = bufs
    return [
        pltpu.make_async_copy(gkv.at[0, :, rows, :], bgkv.at[slot], sems.at[slot, 0]),
        pltpu.make_async_copy(ekv.at[0, :, rows, :], bekv.at[slot], sems.at[slot, 1]),
        pltpu.make_async_copy(gout.at[0, orows, :], bgout.at[slot], sems.at[slot, 2]),
        pltpu.make_async_copy(eout.at[0, orows, :], beout.at[slot], sems.at[slot, 3]),
    ]


ANY = pl.BlockSpec(memory_space=pl.ANY)
HBM = pl.BlockSpec(memory_space=pltpu.HBM)
VM = pl.BlockSpec(memory_space=pltpu.VMEM)


def cost(us):
    return pl.CostEstimate(flops=0, bytes_accessed=int(us * 3_000_000), transcendentals=0)


def part_kernel(dh, gkv, ekv, gout, eout, bkv_hbm, bout_hbm, out, bgkv, bekv, bgout, beout, bkv, bout, bsems, sems):
    basis = [
        pltpu.make_async_copy(bkv_hbm, bkv, bsems.at[0]),
        pltpu.make_async_copy(bout_hbm, bout, bsems.at[1]),
    ]
    copies = [
        loads((gkv, ekv, gout, eout), (bgkv, bekv, bgout, beout), sems, j, my_chunk(dh, j // 2, j % 2))
        for j in range(4)
    ]
    for copy in basis:
        copy.start()
    for chunk in copies:
        for copy in chunk:
            copy.start()
    for copy in basis:
        copy.wait()
    kv = [jnp.concatenate(split3(bkv[a]), axis=0) for a in range(2)]
    kv = [jnp.concatenate([b, b], axis=1) for b in kv]
    ob = jnp.concatenate(split3(bout[...]), axis=0)

    def fold(r):
        return r[:RANK] + (r[RANK : 2 * RANK] + r[2 * RANK :])

    for j in range(4):
        for copy in copies[j]:
            copy.wait()
        for a in range(2):
            both = jnp.concatenate([bgkv[j, a], bekv[j, a]], axis=1)
            out[a, j, :, :CH] = fold(dot_nt(kv[a], both))
        o = fold(dot_nt(ob, bgout[j]) + dot_nt(ob, beout[j]))
        out[0, j, :, CH:] = o[:, :HALF]
        out[1, j, :, CH:] = o[:, HALF:]


def part(dh, args):
    kv = jax.ShapeDtypeStruct((4, 2, CH, COLS), BF16)
    out = jax.ShapeDtypeStruct((4, OCH, OCOLS), BF16)
    result = pl.pallas_call(
        functools.partial(part_kernel, dh),
        out_shape=(jax.ShapeDtypeStruct((2, 4, RANK, WIDE), F32), kv, kv, out, out),
        in_specs=[HBM] * 6,
        out_specs=(VM,) * 5,
        scratch_shapes=[
            pltpu.VMEM((2, RANK, COLS), F32),
            pltpu.VMEM((RANK, OCOLS), F32),
            pltpu.SemaphoreType.DMA((2,)),
            pltpu.SemaphoreType.DMA((4, 4)),
        ],
        compiler_params=pltpu.CompilerParams(vmem_limit_bytes=20 * MIB),
        cost_estimate=cost(4),
        name="part",
    )(*args)
    return result[0], result[1:]


def right_kernel(got, n_before, *refs):
    bgkv, bekv, bgout, beout, lead_a, lead_b = refs[:6]
    before = refs[6 : 6 + n_before]
    right, gram = refs[6 + n_before :]

    def fold(r):
        return r[:RANK] + r[RANK:]

    def square(parts):
        g = dot_nt(jnp.concatenate(parts, axis=0), jnp.concatenate(parts, axis=0))

        def at(i, j):
            return g[i * RANK : (i + 1) * RANK, j * RANK : (j + 1) * RANK]

        return at(0, 0) + ((at(0, 1) + at(1, 0)) + ((at(0, 2) + at(2, 0)) + at(1, 1)))

    sums = [0.0, 0.0, 0.0]
    grams = [[], [], []]
    for j in range(2):
        for k, x in enumerate((lead_a, lead_b)):
            chunk = (got * 2 + j) if k == 0 else (j * 2 + got)
            parts = split3(x[j])
            kv, o = [p[:, :CH] for p in parts], [p[:, CH:] for p in parts]
            grams[k].append(square(kv))
            grams[2].append(square(o))
            both = jnp.concatenate([bgkv[chunk, k], bekv[chunk, k]], axis=1)
            r = fold(dot(jnp.concatenate(kv[:2], axis=0), both))
            sums[k] += r[:, :COLS] + r[:, COLS:]
            two = jnp.concatenate(o[:2], axis=0)
            rows = slice(k * HALF, (k + 1) * HALF)
            sums[2] += fold(dot(two, bgout[chunk, rows]) + dot(two, beout[chunk, rows]))
    gram[0] = grams[0][0] + grams[0][1]
    gram[1] = grams[1][0] + grams[1][1]
    gram[2] = (grams[2][0] + grams[2][2]) + (grams[2][1] + grams[2][3])
    sums = jnp.concatenate(sums, axis=1)
    for other in before:
        sums += other[...]
    right[...] = sums


def right_part(got, bufs, lead, before=()):
    return pl.pallas_call(
        functools.partial(right_kernel, got, len(before)),
        out_shape=(
            jax.ShapeDtypeStruct((RANK, 2 * COLS + OCOLS), F32),
            jax.ShapeDtypeStruct((3, RANK, RANK), F32),
        ),
        in_specs=[VM] * (6 + len(before)),
        out_specs=(VM, VM),
        compiler_params=pltpu.CompilerParams(vmem_limit_bytes=20 * MIB),
        cost_estimate=cost(2),
        name="right",
    )(*bufs, *lead, *before)


def factor_kernel(g0, g1, g2, g3, out):
    row = lax.broadcasted_iota(jnp.int32, (RANK, 2 * RANK), 0)
    col = lax.broadcasted_iota(jnp.int32, (RANK, 2 * RANK), 1)
    eye = jnp.where(col == row + RANK, 1.0, 0.0).astype(F32)
    gram = [(g0[k] + g1[k]) + (g2[k] + g3[k]) for k in range(3)]
    wide = [jnp.concatenate([gram[k], jnp.zeros((RANK, RANK), F32)], axis=1) + eye for k in range(3)]
    scale = [jnp.zeros((RANK, 1), F32)] * 3
    below = lax.broadcasted_iota(jnp.int32, (RANK, 1), 0)
    for i in range(RANK):
        for k in range(3):
            pivot = wide[k][i : i + 1, :]
            d = wide[k][i : i + 1, i : i + 1]
            scale[k] = jnp.where(below == i, lax.rsqrt(d), scale[k])
            factor = jnp.where(below > i, wide[k][:, i : i + 1] / d, 0.0)
            wide[k] = wide[k] - factor * pivot
    for k in range(3):
        out[k] = wide[k][:, RANK:] * scale[k]


def factor(grams):
    return pl.pallas_call(
        factor_kernel,
        out_shape=jax.ShapeDtypeStruct((3, RANK, RANK), F32),
        in_specs=[VM] * 4,
        out_specs=VM,
        cost_estimate=cost(4),
        name="factor",
    )(*grams)


def left_kernel(dh, *refs):
    a_own, a_got, b_own, b_got, w = refs[:5]
    left_kv, left_out, ortho, bkv, bout, sems = refs[-6:]
    weights = []
    for k in range(3):
        w1, w2, w3 = split3(w[k])
        weights.append(jnp.concatenate([w1, w1, w2, w1, w2, w3], axis=1))

    def apply(k, x):
        l1, l2, l3 = split3(x)
        return dot(weights[k], jnp.concatenate([l1, l2, l1, l3, l2, l1], axis=0))

    def packed(o):
        high = o.astype(BF16).astype(F32)
        rest = o - high
        return jnp.transpose(jnp.concatenate([high, rest, high, jnp.zeros_like(o)], axis=0)).astype(BF16)

    copies = []
    for j in range(4):
        du, dv = j // 2, j % 2
        out = []
        for s, x in enumerate(((a_got if du else a_own)[dv], (b_got if dv else b_own)[du])):
            o_kv = apply(s, x[:, :CH])
            o_out = apply(2, x[:, CH:])
            bkv[j, s] = o_kv * (ROWS**0.5)
            out.append(o_out * (OROWS**0.5))
            ortho[j, s, :CH] = packed(o_kv)
            ortho[j, s, CH:] = packed(o_out)
        bout[j, :, :HALF] = out[0]
        bout[j, :, HALF:] = out[1]
        t = my_chunk(dh, du, dv)
        cols = pl.ds(pl.multiple_of(t * CH, CH), CH)
        ocols = pl.ds(pl.multiple_of(t * OCH, OCH), OCH)
        copies.append(pltpu.make_async_copy(bkv.at[j], left_kv.at[:, :, cols], sems.at[j, 0]))
        copies.append(pltpu.make_async_copy(bout.at[j], left_out.at[:, ocols], sems.at[j, 1]))
        copies[-2].start()
        copies[-1].start()
    for copy in copies:
        copy.wait()


def left_part(dh, lead, w, before=()):
    return pl.pallas_call(
        functools.partial(left_kernel, dh),
        out_shape=(
            jax.ShapeDtypeStruct((2, RANK, ROWS), F32),
            jax.ShapeDtypeStruct((RANK, OROWS), F32),
            jax.ShapeDtypeStruct((4, 2, WIDE, 128), BF16),
        ),
        in_specs=[VM] * 5 + [HBM] * len(before),
        out_specs=(HBM, HBM, VM),
        scratch_shapes=[
            pltpu.VMEM((4, 2, RANK, CH), F32),
            pltpu.VMEM((4, RANK, OCH), F32),
            pltpu.SemaphoreType.DMA((4, 2)),
        ],
        input_output_aliases={5: 0, 6: 1} if before else {},
        compiler_params=pltpu.CompilerParams(vmem_limit_bytes=16 * MIB),
        cost_estimate=cost(2),
        name="left",
    )(*lead, w, *before)


def error_kernel(*refs):
    halves = (refs[:4], refs[4:8])
    total, w, ortho = refs[8], refs[9], refs[10:12]
    right_kv, right_out, new_kv, new_out, nkv, nout, nsems = refs[12:]
    packed = []
    for k, (at, n) in enumerate(((0, COLS), (COLS, COLS), (2 * COLS, OCOLS))):
        w1, w2, w3 = split3(w[k])
        r1, r2, r3 = split3(total[:, at : at + n] * (1.0 / REPLICAS))
        right = dot(
            jnp.concatenate([w1, w1, w2, w1, w2, w3], axis=1),
            jnp.concatenate([r1, r2, r1, r3, r2, r1], axis=0),
        )
        if k < 2:
            right_kv[k] = right
        else:
            right_out[...] = right
        high, low = split2(right)
        packed.append(jnp.concatenate([high, high, low, jnp.zeros_like(high)], axis=0))
    stores = []
    for j in range(8):
        dh, i = j // 4, j % 4
        bgkv, bekv, bgout, beout = halves[dh]
        for s in range(2):
            merged = bgkv[i, s].astype(F32) + bekv[i, s].astype(F32)
            nkv[j, s] = (merged - dot(ortho[dh][i, s, :CH], packed[s])).astype(BF16)
            rows = slice(s * HALF, (s + 1) * HALF)
            merged = bgout[i, rows].astype(F32) + beout[i, rows].astype(F32)
            nout[j, rows] = (merged - dot(ortho[dh][i, s, CH:], packed[2])).astype(BF16)
        t = my_chunk(dh, i // 2, i % 2)
        rows = pl.ds(pl.multiple_of(t * CH, CH), CH)
        orows = pl.ds(pl.multiple_of(t * OCH, OCH), OCH)
        stores.append(pltpu.make_async_copy(nkv.at[j], new_kv.at[0, :, rows, :], nsems.at[j, 0]))
        stores.append(pltpu.make_async_copy(nout.at[j], new_out.at[0, orows, :], nsems.at[j, 1]))
        stores[-2].start()
        stores[-1].start()
    for copy in stores:
        copy.wait()


def errors(bufs, total, w, ortho):
    return pl.pallas_call(
        error_kernel,
        out_shape=(
            jax.ShapeDtypeStruct((2, RANK, COLS), F32),
            jax.ShapeDtypeStruct((RANK, OCOLS), F32),
            jax.ShapeDtypeStruct((1, 2, ROWS, COLS), BF16),
            jax.ShapeDtypeStruct((1, OROWS, OCOLS), BF16),
        ),
        in_specs=[VM] * 12,
        out_specs=(VM, VM, HBM, HBM),
        scratch_shapes=[
            pltpu.VMEM((8, 2, CH, COLS), BF16),
            pltpu.VMEM((8, OCH, OCOLS), BF16),
            pltpu.SemaphoreType.DMA((8, 2)),
        ],
        compiler_params=pltpu.CompilerParams(vmem_limit_bytes=24 * MIB),
        cost_estimate=cost(5),
        name="errors",
    )(*bufs, total, w, *ortho)


X, Y, Z = 0, 1, 2


def on_device(grad_kv, error_kv, grad_out, error_out, basis_kv, basis_out):
    args = (grad_kv, error_kv, grad_out, error_out, jnp.swapaxes(basis_kv, 1, 2), basis_out.T)
    args = [pltpu.with_memory_space_constraint(x, pltpu.HBM) for x in args]
    lead, bufs_other = part(1, args)
    got = send(lead, CORES)
    lead, bufs_own = part(0, args)
    kept = lead + got
    a, b = kept.reshape(2, 2, 2, RANK, WIDE)

    a = a[0] + send(a[1], exchange(X, 0))
    b = b[:, 0] + send(b[:, 1], exchange(Y, 0))
    a = a[0] + send(a[1], exchange(Y, 0))
    b = b[0] + send(b[1], exchange(X, 0))
    for axis_a, axis_b in (((Z, 0), (Y, 1)), ((X, 1), (Z, 0)), ((Z, 1), (X, 1)), ((Y, 1), (Z, 1))):
        a, b = a + send(a, exchange(*axis_a)), b + send(b, exchange(*axis_b))
    a_own = jnp.stack([a, send(a, exchange(Y, 0))])
    b_own = jnp.stack([b, send(b, exchange(X, 0))])
    a_got = send(a_own, exchange(X, 0))
    b_got = send(b_own, exchange(Y, 0))
    a_own2, b_own2 = send(a_own, CORES), send(b_own, CORES)
    sum1, gram1 = right_part(0, bufs_own, (a_own, b_own))
    sum2, gram2 = right_part(0, bufs_other, (a_own2, b_own2))
    a_got, b_got, sum1, sum2 = lax.optimization_barrier((a_got, b_got, sum1, sum2))
    a_got2, b_got2 = send(a_got, CORES), send(b_got, CORES)
    sum3, gram3 = right_part(1, bufs_own, (a_got, b_got))
    total, gram4 = right_part(1, bufs_other, (a_got2, b_got2), (sum1, sum2, sum3))
    w = factor((gram1, gram3, gram2, gram4))
    total = total + send(total, exchange(Y, 0))
    total, w = lax.optimization_barrier((total, w))
    *left, ortho_own = left_part(0, (a_own, a_got, b_own, b_got), w)
    total = total + send(total, exchange(Z, 0))
    total, left = lax.optimization_barrier((total, left))
    left_kv, left_out, ortho_other = left_part(1, (a_own2, a_got2, b_own2, b_got2), w, left)
    total = total + send(total, exchange(Y, 1))
    total, ortho_other = lax.optimization_barrier((total, ortho_other))
    total = total + send(total, exchange(Z, 1))
    right_kv, right_out, new_kv, new_out = errors(
        (*bufs_own, *bufs_other), total, w, (ortho_own, ortho_other)
    )
    return (
        jnp.swapaxes(left_kv, 1, 2),
        left_out.T,
        jnp.swapaxes(right_kv, 1, 2),
        right_out.T,
        new_kv,
        new_out,
    )


def solution(mesh):
    placed = (
        P("dp", None, None, "mp"),
        P("dp", None, None, "mp"),
        P("dp", None, "mp"),
        P("dp", None, "mp"),
        P(None, "mp", None),
        P("mp", None),
    )
    return jax.shard_map(
        on_device,
        mesh=mesh,
        in_specs=placed,
        out_specs=(
            P(),
            P(),
            P(None, "mp", None),
            P("mp", None),
            P("dp", None, None, "mp"),
            P("dp", None, "mp"),
        ),
        check_vma=False,
    )
```

time: 130 us -> 115 us (0.88)
  local copies, waits for them, and re-layouts: 20.2 us -> 12.5 us
  waiting for transfers between devices: 34.1 us -> 26.8 us
    unnamed x26 -> x56, local copies, waits for them, and re-layouts: 20 us -> 12.3 us
    ppermute x25, waiting for transfers between devices: 34.1 us -> 26.8 us  [send(): return lax.ppermute(x, ('dp', 'mp'), pairs)]
    pallas_call x5 -> x8, Pallas kernels: 19.4 us -> 24.2 us  [the longest x2 16 us: part(): pl.pallas_call(functools.partial(part_kernel, dh), out_shape=(jax.ShapeDt...]
    pallas_call x1, Pallas kernels: 9.04 us -> 4.65 us  [errors(): pl.pallas_call(error_kernel, out_shape=(jax.ShapeDtypeStruct((2, RANK, CO...]
  transfers between devices with their start and end apart: 25 -> 25, of which waited for: 15 -> 17; matrix products, arithmetic and copies ran while one was open for 0% -> 0% of each run, Pallas kernels for 12% -> 18%
where the time goes in v2:
time: 115 us; the launch traced here: 114 us
  starting transfers between devices  39.2 us (34%)
  Pallas kernels  33.2 us (29%)
  waiting for transfers between devices  26.8 us (23%)
  local copies, waits for them, and re-layouts  12.5 us (11%)
  other arithmetic  1.54 us (1%)
  between operations  1.23 us (1%)
    ppermute x25, starting transfers between devices, send(): return lax.ppermute(x, ('dp', 'mp'), pairs)  39.2 us
    ppermute x25, waiting for transfers between devices, send(): return lax.ppermute(x, ('dp', 'mp'), pairs)  26.8 us
    pallas_call x2, Pallas kernels, part(): pl.pallas_call(functools.partial(part_kernel, dh), out_shape=(jax.ShapeDt...  16 us
    unnamed x56, local copies, waits for them, and re-layouts  12.3 us
    pallas_call x1, Pallas kernels, errors(): pl.pallas_call(error_kernel, out_shape=(jax.ShapeDtypeStruct((2, RANK, CO...  4.65 us
    pallas_call x4, Pallas kernels, right_part(): pl.pallas_call(functools.partial(right_kernel, got, len(before)), out_sha...  4.54 us
    pallas_call x1, Pallas kernels, factor(): pl.pallas_call(factor_kernel, out_shape=jax.ShapeDtypeStruct((3, RANK, RA...  4.35 us
    pallas_call x2, Pallas kernels, left_part(): pl.pallas_call(functools.partial(left_kernel, dh), out_shape=(jax.ShapeDt...  3.66 us
  transfers between devices with their start and end apart: 25, of which 17 were waited for; matrix products, arithmetic and copies ran while one was open for 0% of the time, Pallas kernels for 18%

profile of v2, /device:TPU:0, one launch (start us, length us, event | category | flops | bytes accessed | tf_op | source)
XLA Modules:
  0.0 114.4 jit_solution(278900692153881694)
XLA Ops:
  0.6 6.6 %part.3 = (f32[2,4,32,1280]{3,2,1,0:T(8,128)S(1)}, bf16[4,2,1024,128]{3,2,1,0:T(8,128)(2,1)S(1)}, bf16[4,2,1024,128]{3,2,1,0:T(8,128)(2,1)S(1)}, bf16[4,512,512]...) custom-call(bf16[1,2,8192,128]{3,2,1,0:T(8,128)(2,1)} %gkv.3, bf16[1,2,8192,128]{3,2,1,0:T(8,128)(2,1)} %ekv.3, ...), custom_call_target="tpu_custom_call" | custom-call | bytes 12000000 | tf_op jit(solution)/shard_map/part/pallas_call | solution.py:131
  7.3 0.1 collective-permute-start
  7.4 9.3 %part.2 = (f32[2,4,32,1280]{3,2,1,0:T(8,128)S(1)}, bf16[4,2,1024,128]{3,2,1,0:T(8,128)(2,1)S(1)}, bf16[4,2,1024,128]{3,2,1,0:T(8,128)(2,1)S(1)}, bf16[4,512,512]...) custom-call(bf16[1,2,8192,128]{3,2,1,0:T(8,128)(2,1)} %gkv.3, bf16[1,2,8192,128]{3,2,1,0:T(8,128)(2,1)} %ekv.3, ...), custom_call_target="tpu_custom_call" | custom-call | bytes 12000000 | tf_op jit(solution)/shard_map/part/pallas_call | solution.py:131
  16.8 0.1 add.51
  17.0 1.7 %collective-permute-start.10 = (f32[2,32,1280]{2,1,0:T(8,128)S(1)}, f32[2,32,1280]{2,1,0:T(8,128)S(1)}, u32[]{:S(2)}, u32[]{:S(2)}) collective-permute-start(f32[2,32,1280]{2,1,0:T(8,128)S(1)} %slice_bitcast_fusion), channel_id=1, source_target_pairs={{0,32},{1,97},{2,34},{3,99},{4,36},{5,101},{6,38},{7,103},{8,40},{... | collective-permute-start | bytes 983048 | tf_op jit(solution)/shard_map/ppermute | solution.py:35
  18.8 1.6 %collective-permute-start.1 = (f32[2,32,1280]{2,1,0:T(8,128)S(1)}, f32[2,32,1280]{2,1,0:T(8,128)S(1)}, u32[]{:S(2)}, u32[]{:S(2)}) collective-permute-start(f32[2,32,1280]{2,1,0:T(8,128)S(1)} %slice_bitcast_fusion.2), channel_id=1, source_target_pairs={{0,2},{1,7},{2,0},{3,5},{4,6},{5,3},{6,4},{7,1},{8,10},{9,15},{10,... | collective-permute-start | bytes 983048 | tf_op jit(solution)/shard_map/ppermute | solution.py:35
  20.3 3.8 %collective-permute-done.10 = f32[2,32,1280]{2,1,0:T(8,128)S(1)} collective-permute-done((f32[2,32,1280]{2,1,0:T(8,128)S(1)}, f32[2,32,1280]{2,1,0:T(8,128)S(1)}, u32[]{:S(2)}, u32[]{:S(2)}) %collective-permute-start.10) | collective-permute-done | bytes 327712 | tf_op jit(solution)/shard_map/ppermute | solution.py:35
  24.2 1.6 %collective-permute-start.11 = (f32[32,1280]{1,0:T(8,128)S(1)}, f32[32,1280]{1,0:T(8,128)S(1)}, u32[]{:S(2)}, u32[]{:S(2)}) collective-permute-start(f32[32,1280]{1,0:T(8,128)S(1)} %slice_bitcast_fusion.4), channel_id=1, source_target_pairs={{0,2},{1,7},{2,0},{3,5},{4,6},{5,3},{6,4},{7,1},{8,10},{9,15},{10,... | collective-permute-start | bytes 491528 | tf_op jit(solution)/shard_map/ppermute | solution.py:35
  25.9 0.1 collective-permute-done.1
  26.0 1.6 %collective-permute-start.2 = (f32[32,1280]{1,0:T(8,128)S(1)}, f32[32,1280]{1,0:T(8,128)S(1)}, u32[]{:S(2)}, u32[]{:S(2)}) collective-permute-start(f32[32,1280]{1,0:T(8,128)S(1)} %slice_bitcast_fusion.6), channel_id=1, source_target_pairs={{0,32},{1,97},{2,34},{3,99},{4,36},{5,101},{6,38},{7,103},{8,40},{... | collective-permute-start | bytes 491528 | tf_op jit(solution)/shard_map/ppermute | solution.py:35
  27.6 2.0 %collective-permute-done.11 = f32[32,1280]{1,0:T(8,128)S(1)} collective-permute-done((f32[32,1280]{1,0:T(8,128)S(1)}, f32[32,1280]{1,0:T(8,128)S(1)}, u32[]{:S(2)}, u32[]{:S(2)}) %collective-permute-start.11) | collective-permute-done | bytes 163872 | tf_op jit(solution)/shard_map/ppermute | solution.py:35
  29.6 3.2 %collective-permute-start.12 = (f32[32,1280]{1,0:T(8,128)S(1)}, f32[32,1280]{1,0:T(8,128)S(1)}, u32[]{:S(2)}, u32[]{:S(2)}) collective-permute-start(f32[32,1280]{1,0:T(8,128)S(1)} %fusion.2), channel_id=1, source_target_pairs={{0,96},{1,33},{2,98},{3,35},{4,100},{5,37},{6,102},{7,39},{8,104},... | collective-permute-start | bytes 491528 | tf_op jit(solution)/shard_map/ppermute | solution.py:35
  32.8 2.0 %collective-permute-start.3 = (f32[32,1280]{1,0:T(8,128)S(1)}, f32[32,1280]{1,0:T(8,128)S(1)}, u32[]{:S(2)}, u32[]{:S(2)}) collective-permute-start(f32[32,1280]{1,0:T(8,128)S(1)} %fusion.3), channel_id=1, source_target_pairs={{0,8},{1,25},{2,10},{3,27},{4,12},{5,29},{6,14},{7,31},{8,0},{9,17... | collective-permute-start | bytes 491528 | tf_op jit(solution)/shard_map/ppermute | solution.py:35
  34.8 1.4 %collective-permute-done.12 = f32[32,1280]{1,0:T(8,128)S(1)} collective-permute-done((f32[32,1280]{1,0:T(8,128)S(1)}, f32[32,1280]{1,0:T(8,128)S(1)}, u32[]{:S(2)}, u32[]{:S(2)}) %collective-permute-start.12) | collective-permute-done | bytes 163872 | tf_op jit(solution)/shard_map/ppermute | solution.py:35
  36.3 2.1 %collective-permute-start.13 = (f32[32,1280]{1,0:T(8,128)S(1)}, f32[32,1280]{1,0:T(8,128)S(1)}, u32[]{:S(2)}, u32[]{:S(2)}) collective-permute-start(f32[32,1280]{1,0:T(8,128)S(1)} %add.60), channel_id=1, source_target_pairs={{0,8},{1,25},{2,10},{3,27},{4,12},{5,29},{6,14},{7,31},{8,0},{9,17... | collective-permute-start | bytes 491528 | tf_op jit(solution)/shard_map/ppermute | solution.py:35
  38.4 2.8 %collective-permute-start.4 = (f32[32,1280]{1,0:T(8,128)S(1)}, f32[32,1280]{1,0:T(8,128)S(1)}, u32[]{:S(2)}, u32[]{:S(2)}) collective-permute-start(f32[32,1280]{1,0:T(8,128)S(1)} %add.54), channel_id=1, source_target_pairs={{0,6},{1,3},{2,4},{3,1},{4,2},{5,7},{6,0},{7,5},{8,14},{9,11},{10,... | collective-permute-start | bytes 491528 | tf_op jit(solution)/shard_map/ppermute | solution.py:35
  41.2 0.5 collective-permute-done.13
  41.7 2.9 %collective-permute-start.14 = (f32[32,1280]{1,0:T(8,128)S(1)}, f32[32,1280]{1,0:T(8,128)S(1)}, u32[]{:S(2)}, u32[]{:S(2)}) collective-permute-start(f32[32,1280]{1,0:T(8,128)S(1)} %add.61), channel_id=1, source_target_pairs={{0,6},{1,3},{2,4},{3,1},{4,2},{5,7},{6,0},{7,5},{8,14},{9,11},{10,... | collective-permute-start | bytes 491528 | tf_op jit(solution)/shard_map/ppermute | solution.py:35
  44.6 0.4 collective-permute-done.4
  45.0 4.0 %collective-permute-start.5 = (f32[32,1280]{1,0:T(8,128)S(1)}, f32[32,1280]{1,0:T(8,128)S(1)}, u32[]{:S(2)}, u32[]{:S(2)}) collective-permute-start(f32[32,1280]{1,0:T(8,128)S(1)} %add.55), channel_id=1, source_target_pairs={{0,24},{1,9},{2,26},{3,11},{4,28},{5,13},{6,30},{7,15},{8,16},{9,1... | collective-permute-start | bytes 491528 | tf_op jit(solution)/shard_map/ppermute | solution.py:35
  49.0 3.5 %collective-permute-start.15 = (f32[32,1280]{1,0:T(8,128)S(1)}, f32[32,1280]{1,0:T(8,128)S(1)}, u32[]{:S(2)}, u32[]{:S(2)}) collective-permute-start(f32[32,1280]{1,0:T(8,128)S(1)} %add.62), channel_id=1, source_target_pairs={{0,24},{1,9},{2,26},{3,11},{4,28},{5,13},{6,30},{7,15},{8,16},{9,1... | collective-permute-start | bytes 491528 | tf_op jit(solution)/shard_map/ppermute | solution.py:35
  52.5 3.1 %collective-permute-start.6 = (f32[32,1280]{1,0:T(8,128)S(1)}, f32[32,1280]{1,0:T(8,128)S(1)}, u32[]{:S(2)}, u32[]{:S(2)}) collective-permute-start(f32[32,1280]{1,0:T(8,128)S(1)} %add.56), channel_id=1, source_target_pairs={{0,96},{1,33},{2,98},{3,35},{4,100},{5,37},{6,102},{7,39},{8,104},... | collective-permute-start | bytes 491528 | tf_op jit(solution)/shard_map/ppermute | solution.py:35
  55.7 0.2 collective-permute-done.15
  55.8 0.4 collective-permute-start.16
  56.2 4.1 %collective-permute-done.6 = f32[32,1280]{1,0:T(8,128)S(1)} collective-permute-done((f32[32,1280]{1,0:T(8,128)S(1)}, f32[32,1280]{1,0:T(8,128)S(1)}, u32[]{:S(2)}, u32[]{:S(2)}) %collective-permute-start.6) | collective-permute-done | bytes 163872 | tf_op jit(solution)/shard_map/ppermute | solution.py:35
  60.4 0.1 collective-permute-start.7
  60.4 0.8 collective-permute-done.16
  61.3 0.1 collective-permute-start.18
  61.4 4.4 %collective-permute-done.7 = f32[32,1280]{1,0:T(8,128)S(1)} collective-permute-done((f32[32,1280]{1,0:T(8,128)S(1)}, f32[32,1280]{1,0:T(8,128)S(1)}, u32[]{:S(2)}, u32[]{:S(2)}) %collective-permute-start.7) | collective-permute-done | bytes 163872 | tf_op jit(solution)/shard_map/ppermute | solution.py:35
  65.8 0.1 collective-permute-start.8
  65.9 0.1 collective-permute-start.17
  66.0 0.3 collective-permute-start.9
  66.3 1.1 right.4
  67.5 0.0 collective-permute-done.8.refs_4_.refs_0_
  67.5 1.1 right.5
  68.7 0.6 copy-done.25
  69.3 3.8 %collective-permute-done.17.refs_5_.refs_3_ = f32[2,32,1280]{2,1,0:T(8,128)S(1)} collective-permute-done((f32[2,32,1280]{2,1,0:T(8,128)S(1)}, f32[2,32,1280]{2,1,0:T(8,128)S(1)}, u32[]{:S(2)}, u32[]{:S(2)}) %collective-permute-start.17) | collective-permute-done | bytes 327712 | tf_op jit(solution)/shard_map/ppermute | solution.py:35
  73.0 0.1 collective-permute-done.9.refs_4_.refs_1_
  73.1 2.4 %collective-permute-start.19 = (f32[2,32,1280]{2,1,0:T(8,128)S(1)}, f32[2,32,1280]{2,1,0:T(8,128)S(1)}, u32[]{:S(2)}, u32[]{:S(2)}) collective-permute-start(f32[2,32,1280]{2,1,0:T(8,128)S(1)} %collective-permute-done.9.refs_4_.refs_1_), channel_id=1, source_target_pairs={{0,1},{1,0},{2,3},{3,2},{4,5},{5,4},{6,7},{7,6},{8,9},{9,8},{10,11... | collective-permute-start | bytes 983048 | tf_op jit(solution)/shard_map/ppermute | solution.py:35
  75.5 1.1 right.6
  76.7 0.1 collective-permute-done.19.refs_4_.refs_1_
  76.8 0.5 collective-permute-done.20.refs_5_.refs_3_
  77.3 1.1 right.7
  78.4 0.6 copy-done.27
  79.1 4.4 %factor.1.refs_4_.refs_9_ = f32[3,32,32]{2,1,0:T(8,128)} custom-call(f32[3,32,32]{2,1,0:T(8,128)} %copy-done.24, f32[3,32,32]{2,1,0:T(8,128)} %copy-done.26, f32[3,32,32]{2,1,0:T(8,128)} %copy-done.25, f32[3,32,32]{2,1,0:T(8,128)} %copy-done.27), custom_call_target="tpu_custom_call" | custom-call | bytes 12000000 | tf_op jit(solution)/shard_map/factor/pallas_call | solution.py:224
  83.4 0.4 collective-permute-done.21
  83.8 1.1 add.64
  84.8 0.3 collective-permute-start.22
  85.2 0.8 copy-done.22
  86.0 1.8 %left.2 = (f32[2,32,8192]{2,1,0:T(8,128)}, f32[32,4096]{1,0:T(8,128)}, bf16[4,2,1280,128]{3,2,1,0:T(8,128)(2,1)S(1)}) custom-call(f32[2,32,1280]{2,1,0:T(8,128)S(1)} %pad_maximum_fusion.refs_4_.refs_0_, f32[2,32,1280]{2,1,0:T(8,128)S(1)} %collective-permute-done.9.refs_4_.refs_1_, f32[2,32,1280]{2,1,0:T(8,128)S(1)} %pad_maximum_fusion.1.refs_5_.refs_2_, ...), custom_call_target="tpu_custom_call" | custom-call | bytes 6000000 | tf_op jit(solution)/shard_map/left/pallas_call | solution.py:276
  87.8 1.7 %collective-permute-done.22 = f32[32,768]{1,0:T(8,128)S(1)} collective-permute-done((f32[32,768]{1,0:T(8,128)S(1)}, f32[32,768]{1,0:T(8,128)S(1)}, u32[]{:S(2)}, u32[]{:S(2)}) %collective-permute-start.22) | collective-permute-done | bytes 98336 | tf_op jit(solution)/shard_map/ppermute | solution.py:35
  89.6 1.9 %collective-permute-start.23 = (f32[32,768]{1,0:T(8,128)S(1)}, f32[32,768]{1,0:T(8,128)S(1)}, u32[]{:S(2)}, u32[]{:S(2)}) collective-permute-start(f32[32,768]{1,0:T(8,128)S(1)} %add.65), channel_id=1, source_target_pairs={{0,96},{1,33},{2,98},{3,35},{4,100},{5,37},{6,102},{7,39},{8,104},... | collective-permute-start | bytes 294920 | tf_op jit(solution)/shard_map/ppermute | solution.py:35
  91.5 1.0 copy-done.15
  92.5 1.0 copy-done.17
  93.4 1.0 copy-done.19
  94.4 1.0 copy-done.21
  95.4 1.8 %left.3 = (f32[2,32,8192]{2,1,0:T(8,128)}, f32[32,4096]{1,0:T(8,128)}, bf16[4,2,1280,128]{3,2,1,0:T(8,128)(2,1)S(1)}) custom-call(f32[2,32,1280]{2,1,0:T(8,128)S(1)} %copy-done.17, f32[2,32,1280]{2,1,0:T(8,128)S(1)} %copy-done.19, f32[2,32,1280]{2,1,0:T(8,128)S(1)} %copy-done.15, ...), custom_call_target="tpu_custom_call", output_to_operand_aliasing={{0}: (5, {}), {1}: (6, {})} | custom-call | bytes 6000000 | tf_op jit(solution)/shard_map/left/pallas_call | solution.py:276
  97.3 3.3 %collective-permute-start.24 = (f32[32,768]{1,0:T(8,128)S(1)}, f32[32,768]{1,0:T(8,128)S(1)}, u32[]{:S(2)}, u32[]{:S(2)}) collective-permute-start(f32[32,768]{1,0:T(8,128)S(1)} %add.66), channel_id=1, source_target_pairs={{0,24},{1,9},{2,26},{3,11},{4,28},{5,13},{6,30},{7,15},{8,16},{9,1... | collective-permute-start | bytes 294920 | tf_op jit(solution)/shard_map/ppermute | solution.py:35
  100.5 2.6 %collective-permute-done.24 = f32[32,768]{1,0:T(8,128)S(1)} collective-permute-done((f32[32,768]{1,0:T(8,128)S(1)}, f32[32,768]{1,0:T(8,128)S(1)}, u32[]{:S(2)}, u32[]{:S(2)}) %collective-permute-start.24) | collective-permute-done | bytes 98336 | tf_op jit(solution)/shard_map/ppermute | solution.py:35
  103.2 1.6 %copy-done.7 = bf16[4,2,1024,128]{3,2,1,0:T(8,128)(2,1)S(1)} copy-done((bf16[4,2,1024,128]{3,2,1,0:T(8,128)(2,1)S(1)}, bf16[4,2,1024,128]{3,2,1,0:T(8,128)(2,1)}, u32[]{:S(2)}) %copy-start.7) | copy-done | bytes 2097176
  104.8 1.6 %copy-done.9 = bf16[4,2,1024,128]{3,2,1,0:T(8,128)(2,1)S(1)} copy-done((bf16[4,2,1024,128]{3,2,1,0:T(8,128)(2,1)S(1)}, bf16[4,2,1024,128]{3,2,1,0:T(8,128)(2,1)}, u32[]{:S(2)}) %copy-start.9) | copy-done | bytes 2097176
  106.4 1.6 %copy-done.11 = bf16[4,512,512]{2,1,0:T(8,128)(2,1)S(1)} copy-done((bf16[4,512,512]{2,1,0:T(8,128)(2,1)S(1)}, bf16[4,512,512]{2,1,0:T(8,128)(2,1)}, u32[]{:S(2)}) %copy-start.11) | copy-done | bytes 2097176
  108.0 1.6 %copy-done.13 = bf16[4,512,512]{2,1,0:T(8,128)(2,1)S(1)} copy-done((bf16[4,512,512]{2,1,0:T(8,128)(2,1)S(1)}, bf16[4,512,512]{2,1,0:T(8,128)(2,1)}, u32[]{:S(2)}) %copy-start.13) | copy-done | bytes 2097176
  109.6 4.7 %errors.1 = (f32[2,32,128]{2,1,0:T(8,128)}, f32[32,512]{1,0:T(8,128)}, bf16[1,2,8192,128]{3,2,1,0:T(8,128)(2,1)}, bf16[1,4096,512]{2,1,0:T(8,128)(2,1)}) custom-call(bf16[4,2,1024,128]{3,2,1,0:T(8,128)(2,1)S(1)} %get-tuple-element.47.refs_0_, bf16[4,2,1024,128]{3,2,1,0:T(8,128)(2,1)S(1)} %copy-done.1, bf16[4,512,512]{2,1,0:T(8,128)(2,1)S(1)} %copy-done.3, ...), custom_call_target="tpu_custom_call" | custom-call | bytes 15000000 | tf_op jit(solution)/shard_map/errors/pallas_call | solution.py:337
  (76 shorter events, 0.6 us)
Async XLA Ops:
  7.2 70.0 %copy-start.6 = (bf16[4,2,1024,128]{3,2,1,0:T(8,128)(2,1)}, bf16[4,2,1024,128]{3,2,1,0:T(8,128)(2,1)S(1)}, u32[]{:S(2)}) copy-start(bf16[4,2,1024,128]{3,2,1,0:T(8,128)(2,1)S(1)} %get-tuple-element.52.refs_0_.refs_4_) | copy-start | bytes 6291460
  7.3 70.0 %copy-start.8 = (bf16[4,2,1024,128]{3,2,1,0:T(8,128)(2,1)}, bf16[4,2,1024,128]{3,2,1,0:T(8,128)(2,1)S(1)}, u32[]{:S(2)}) copy-start(bf16[4,2,1024,128]{3,2,1,0:T(8,128)(2,1)S(1)} %get-tuple-element.53.refs_1_.refs_5_) | copy-start | bytes 6291460
  7.3 70.0 %copy-start.10 = (bf16[4,512,512]{2,1,0:T(8,128)(2,1)}, bf16[4,512,512]{2,1,0:T(8,128)(2,1)S(1)}, u32[]{:S(2)}) copy-start(bf16[4,512,512]{2,1,0:T(8,128)(2,1)S(1)} %get-tuple-element.54.refs_2_.refs_6_) | copy-start | bytes 6291460
  7.3 70.0 %copy-start.12 = (bf16[4,512,512]{2,1,0:T(8,128)(2,1)}, bf16[4,512,512]{2,1,0:T(8,128)(2,1)S(1)}, u32[]{:S(2)}) copy-start(bf16[4,512,512]{2,1,0:T(8,128)(2,1)S(1)} %get-tuple-element.55.refs_3_.refs_7_) | copy-start | bytes 6291460
  7.3 9.5 %collective-permute-start = (f32[2,4,32,1280]{3,2,1,0:T(8,128)S(1)}, f32[2,4,32,1280]{3,2,1,0:T(8,128)S(1)}, u32[]{:S(2)}, u32[]{:S(2)}) collective-permute-start(f32[2,4,32,1280]{3,2,1,0:T(8,128)S(1)} %get-tuple-element.46), channel_id=1, source_target_pairs={{0,1},{1,0},{2,3},{3,2},{4,5},{5,4},{6,7},{7,6},{8,9},{9,8},{10,11... | collective-permute-start | bytes 3932168 | tf_op jit(solution)/shard_map/ppermute | solution.py:35
  16.7 58.8 %copy-start = (bf16[4,2,1024,128]{3,2,1,0:T(8,128)(2,1)}, bf16[4,2,1024,128]{3,2,1,0:T(8,128)(2,1)S(1)}, u32[]{:S(2)}) copy-start(bf16[4,2,1024,128]{3,2,1,0:T(8,128)(2,1)S(1)} %get-tuple-element.48.refs_1_) | copy-start | bytes 6291460
  16.7 58.8 %copy-start.2 = (bf16[4,512,512]{2,1,0:T(8,128)(2,1)}, bf16[4,512,512]{2,1,0:T(8,128)(2,1)S(1)}, u32[]{:S(2)}) copy-start(bf16[4,512,512]{2,1,0:T(8,128)(2,1)S(1)} %get-tuple-element.49.refs_2_) | copy-start | bytes 6291460
  16.8 58.8 %copy-start.4 = (bf16[4,512,512]{2,1,0:T(8,128)(2,1)}, bf16[4,512,512]{2,1,0:T(8,128)(2,1)S(1)}, u32[]{:S(2)}) copy-start(bf16[4,512,512]{2,1,0:T(8,128)(2,1)S(1)} %get-tuple-element.50.refs_3_) | copy-start | bytes 6291460
  17.0 7.2 %collective-permute-start.10 = (f32[2,32,1280]{2,1,0:T(8,128)S(1)}, f32[2,32,1280]{2,1,0:T(8,128)S(1)}, u32[]{:S(2)}, u32[]{:S(2)}) collective-permute-start(f32[2,32,1280]{2,1,0:T(8,128)S(1)} %slice_bitcast_fusion), channel_id=1, source_target_pairs={{0,32},{1,97},{2,34},{3,99},{4,36},{5,101},{6,38},{7,103},{8,40},{... | collective-permute-start | bytes 983048 | tf_op jit(solution)/shard_map/ppermute | solution.py:35
  18.8 7.2 %collective-permute-start.1 = (f32[2,32,1280]{2,1,0:T(8,128)S(1)}, f32[2,32,1280]{2,1,0:T(8,128)S(1)}, u32[]{:S(2)}, u32[]{:S(2)}) collective-permute-start(f32[2,32,1280]{2,1,0:T(8,128)S(1)} %slice_bitcast_fusion.2), channel_id=1, source_target_pairs={{0,2},{1,7},{2,0},{3,5},{4,6},{5,3},{6,4},{7,1},{8,10},{9,15},{10,... | collective-permute-start | bytes 983048 | tf_op jit(solution)/shard_map/ppermute | solution.py:35
  24.2 5.4 %collective-permute-start.11 = (f32[32,1280]{1,0:T(8,128)S(1)}, f32[32,1280]{1,0:T(8,128)S(1)}, u32[]{:S(2)}, u32[]{:S(2)}) collective-permute-start(f32[32,1280]{1,0:T(8,128)S(1)} %slice_bitcast_fusion.4), channel_id=1, source_target_pairs={{0,2},{1,7},{2,0},{3,5},{4,6},{5,3},{6,4},{7,1},{8,10},{9,15},{10,... | collective-permute-start | bytes 491528 | tf_op jit(solution)/shard_map/ppermute | solution.py:35
  26.0 6.8 %collective-permute-start.2 = (f32[32,1280]{1,0:T(8,128)S(1)}, f32[32,1280]{1,0:T(8,128)S(1)}, u32[]{:S(2)}, u32[]{:S(2)}) collective-permute-start(f32[32,1280]{1,0:T(8,128)S(1)} %slice_bitcast_fusion.6), channel_id=1, source_target_pairs={{0,32},{1,97},{2,34},{3,99},{4,36},{5,101},{6,38},{7,103},{8,40},{... | collective-permute-start | bytes 491528 | tf_op jit(solution)/shard_map/ppermute | solution.py:35
  29.6 6.6 %collective-permute-start.12 = (f32[32,1280]{1,0:T(8,128)S(1)}, f32[32,1280]{1,0:T(8,128)S(1)}, u32[]{:S(2)}, u32[]{:S(2)}) collective-permute-start(f32[32,1280]{1,0:T(8,128)S(1)} %fusion.2), channel_id=1, source_target_pairs={{0,96},{1,33},{2,98},{3,35},{4,100},{5,37},{6,102},{7,39},{8,104},... | collective-permute-start | bytes 491528 | tf_op jit(solution)/shard_map/ppermute | solution.py:35
  32.8 5.5 %collective-permute-start.3 = (f32[32,1280]{1,0:T(8,128)S(1)}, f32[32,1280]{1,0:T(8,128)S(1)}, u32[]{:S(2)}, u32[]{:S(2)}) collective-permute-start(f32[32,1280]{1,0:T(8,128)S(1)} %fusion.3), channel_id=1, source_target_pairs={{0,8},{1,25},{2,10},{3,27},{4,12},{5,29},{6,14},{7,31},{8,0},{9,17... | collective-permute-start | bytes 491528 | tf_op jit(solution)/shard_map/ppermute | solution.py:35
  36.3 5.4 %collective-permute-start.13 = (f32[32,1280]{1,0:T(8,128)S(1)}, f32[32,1280]{1,0:T(8,128)S(1)}, u32[]{:S(2)}, u32[]{:S(2)}) collective-permute-start(f32[32,1280]{1,0:T(8,128)S(1)} %add.60), channel_id=1, source_target_pairs={{0,8},{1,25},{2,10},{3,27},{4,12},{5,29},{6,14},{7,31},{8,0},{9,17... | collective-permute-start | bytes 491528 | tf_op jit(solution)/shard_map/ppermute | solution.py:35
  38.4 6.6 %collective-permute-start.4 = (f32[32,1280]{1,0:T(8,128)S(1)}, f32[32,1280]{1,0:T(8,128)S(1)}, u32[]{:S(2)}, u32[]{:S(2)}) collective-permute-start(f32[32,1280]{1,0:T(8,128)S(1)} %add.54), channel_id=1, source_target_pairs={{0,6},{1,3},{2,4},{3,1},{4,2},{5,7},{6,0},{7,5},{8,14},{9,11},{10,... | collective-permute-start | bytes 491528 | tf_op jit(solution)/shard_map/ppermute | solution.py:35
  41.7 7.3 %collective-permute-start.14 = (f32[32,1280]{1,0:T(8,128)S(1)}, f32[32,1280]{1,0:T(8,128)S(1)}, u32[]{:S(2)}, u32[]{:S(2)}) collective-permute-start(f32[32,1280]{1,0:T(8,128)S(1)} %add.61), channel_id=1, source_target_pairs={{0,6},{1,3},{2,4},{3,1},{4,2},{5,7},{6,0},{7,5},{8,14},{9,11},{10,... | collective-permute-start | bytes 491528 | tf_op jit(solution)/shard_map/ppermute | solution.py:35
  45.0 7.5 %collective-permute-start.5 = (f32[32,1280]{1,0:T(8,128)S(1)}, f32[32,1280]{1,0:T(8,128)S(1)}, u32[]{:S(2)}, u32[]{:S(2)}) collective-permute-start(f32[32,1280]{1,0:T(8,128)S(1)} %add.55), channel_id=1, source_target_pairs={{0,24},{1,9},{2,26},{3,11},{4,28},{5,13},{6,30},{7,15},{8,16},{9,1... | collective-permute-start | bytes 491528 | tf_op jit(solution)/shard_map/ppermute | solution.py:35
  49.0 6.8 %collective-permute-start.15 = (f32[32,1280]{1,0:T(8,128)S(1)}, f32[32,1280]{1,0:T(8,128)S(1)}, u32[]{:S(2)}, u32[]{:S(2)}) collective-permute-start(f32[32,1280]{1,0:T(8,128)S(1)} %add.62), channel_id=1, source_target_pairs={{0,24},{1,9},{2,26},{3,11},{4,28},{5,13},{6,30},{7,15},{8,16},{9,1... | collective-permute-start | bytes 491528 | tf_op jit(solution)/shard_map/ppermute | solution.py:35
  52.5 7.8 %collective-permute-start.6 = (f32[32,1280]{1,0:T(8,128)S(1)}, f32[32,1280]{1,0:T(8,128)S(1)}, u32[]{:S(2)}, u32[]{:S(2)}) collective-permute-start(f32[32,1280]{1,0:T(8,128)S(1)} %add.56), channel_id=1, source_target_pairs={{0,96},{1,33},{2,98},{3,35},{4,100},{5,37},{6,102},{7,39},{8,104},... | collective-permute-start | bytes 491528 | tf_op jit(solution)/shard_map/ppermute | solution.py:35
  55.8 5.4 %collective-permute-start.16 = (f32[32,1280]{1,0:T(8,128)S(1)}, f32[32,1280]{1,0:T(8,128)S(1)}, u32[]{:S(2)}, u32[]{:S(2)}) collective-permute-start(f32[32,1280]{1,0:T(8,128)S(1)} %add.63), channel_id=1, source_target_pairs={{0,2},{1,7},{2,0},{3,5},{4,6},{5,3},{6,4},{7,1},{8,10},{9,15},{10,... | collective-permute-start | bytes 491528 | tf_op jit(solution)/shard_map/ppermute | solution.py:35
  60.4 5.4 %collective-permute-start.7 = (f32[32,1280]{1,0:T(8,128)S(1)}, f32[32,1280]{1,0:T(8,128)S(1)}, u32[]{:S(2)}, u32[]{:S(2)}) collective-permute-start(f32[32,1280]{1,0:T(8,128)S(1)} %add.57), channel_id=1, source_target_pairs={{0,32},{1,97},{2,34},{3,99},{4,36},{5,101},{6,38},{7,103},{8,40},{... | collective-permute-start | bytes 491528 | tf_op jit(solution)/shard_map/ppermute | solution.py:35
  61.3 6.2 %collective-permute-start.18 = (f32[2,32,1280]{2,1,0:T(8,128)S(1)}, f32[2,32,1280]{2,1,0:T(8,128)S(1)}, u32[]{:S(2)}, u32[]{:S(2)}) collective-permute-start(f32[2,32,1280]{2,1,0:T(8,128)S(1)} %pad_maximum_fusion.1.refs_5_.refs_2_), channel_id=1, source_target_pairs={{0,1},{1,0},{2,3},{3,2},{4,5},{5,4},{6,7},{7,6},{8,9},{9,8},{10,11... | collective-permute-start | bytes 983048 | tf_op jit(solution)/shard_map/ppermute | solution.py:35
  65.8 1.7 %collective-permute-start.8 = (f32[2,32,1280]{2,1,0:T(8,128)S(1)}, f32[2,32,1280]{2,1,0:T(8,128)S(1)}, u32[]{:S(2)}, u32[]{:S(2)}) collective-permute-start(f32[2,32,1280]{2,1,0:T(8,128)S(1)} %pad_maximum_fusion.refs_4_.refs_0_), channel_id=1, source_target_pairs={{0,1},{1,0},{2,3},{3,2},{4,5},{5,4},{6,7},{7,6},{8,9},{9,8},{10,11... | collective-permute-start | bytes 983048 | tf_op jit(solution)/shard_map/ppermute | solution.py:35
  65.9 7.2 %collective-permute-start.17 = (f32[2,32,1280]{2,1,0:T(8,128)S(1)}, f32[2,32,1280]{2,1,0:T(8,128)S(1)}, u32[]{:S(2)}, u32[]{:S(2)}) collective-permute-start(f32[2,32,1280]{2,1,0:T(8,128)S(1)} %pad_maximum_fusion.1.refs_5_.refs_2_), channel_id=1, source_target_pairs={{0,32},{1,97},{2,34},{3,99},{4,36},{5,101},{6,38},{7,103},{8,40},{... | collective-permute-start | bytes 983048 | tf_op jit(solution)/shard_map/ppermute | solution.py:35
  66.0 7.2 %collective-permute-start.9 = (f32[2,32,1280]{2,1,0:T(8,128)S(1)}, f32[2,32,1280]{2,1,0:T(8,128)S(1)}, u32[]{:S(2)}, u32[]{:S(2)}) collective-permute-start(f32[2,32,1280]{2,1,0:T(8,128)S(1)} %pad_maximum_fusion.refs_4_.refs_0_), channel_id=1, source_target_pairs={{0,2},{1,7},{2,0},{3,5},{4,6},{5,3},{6,4},{7,1},{8,10},{9,15},{10,... | collective-permute-start | bytes 983048 | tf_op jit(solution)/shard_map/ppermute | solution.py:35
  67.4 1.2 %copy-start.24 = (f32[3,32,32]{2,1,0:T(8,128)}, f32[3,32,32]{2,1,0:T(8,128)S(1)}, u32[]{:S(2)}) copy-start(f32[3,32,32]{2,1,0:T(8,128)S(1)} %get-tuple-element.63.g0) | copy-start | bytes 36868
  67.5 1.2 %copy-start.14 = (f32[2,32,1280]{2,1,0:T(8,128)}, f32[2,32,1280]{2,1,0:T(8,128)S(1)}, u32[]{:S(2)}) copy-start(f32[2,32,1280]{2,1,0:T(8,128)S(1)} %collective-permute-done.18.refs_5_.refs_2_) | copy-start | bytes 983044
  67.5 1.2 %copy-start.16 = (f32[2,32,1280]{2,1,0:T(8,128)}, f32[2,32,1280]{2,1,0:T(8,128)S(1)}, u32[]{:S(2)}) copy-start(f32[2,32,1280]{2,1,0:T(8,128)S(1)} %collective-permute-done.8.refs_4_.refs_0_) | copy-start | bytes 983044
  68.6 0.6 copy-start.25
  73.1 3.7 %collective-permute-start.19 = (f32[2,32,1280]{2,1,0:T(8,128)S(1)}, f32[2,32,1280]{2,1,0:T(8,128)S(1)}, u32[]{:S(2)}, u32[]{:S(2)}) collective-permute-start(f32[2,32,1280]{2,1,0:T(8,128)S(1)} %collective-permute-done.9.refs_4_.refs_1_), channel_id=1, source_target_pairs={{0,1},{1,0},{2,3},{3,2},{4,5},{5,4},{6,7},{7,6},{8,9},{9,8},{10,11... | collective-permute-start | bytes 983048 | tf_op jit(solution)/shard_map/ppermute | solution.py:35
  75.5 1.7 %collective-permute-start.20 = (f32[2,32,1280]{2,1,0:T(8,128)S(1)}, f32[2,32,1280]{2,1,0:T(8,128)S(1)}, u32[]{:S(2)}, u32[]{:S(2)}) collective-permute-start(f32[2,32,1280]{2,1,0:T(8,128)S(1)} %collective-permute-done.17.refs_5_.refs_3_), channel_id=1, source_target_pairs={{0,1},{1,0},{2,3},{3,2},{4,5},{5,4},{6,7},{7,6},{8,9},{9,8},{10,11... | collective-permute-start | bytes 983048 | tf_op jit(solution)/shard_map/ppermute | solution.py:35
  76.7 1.7 %copy-start.26 = (f32[3,32,32]{2,1,0:T(8,128)}, f32[3,32,32]{2,1,0:T(8,128)S(1)}, u32[]{:S(2)}) copy-start(f32[3,32,32]{2,1,0:T(8,128)S(1)} %get-tuple-element.64.g1) | copy-start | bytes 36868
  76.8 1.6 %copy-start.18 = (f32[2,32,1280]{2,1,0:T(8,128)}, f32[2,32,1280]{2,1,0:T(8,128)S(1)}, u32[]{:S(2)}) copy-start(f32[2,32,1280]{2,1,0:T(8,128)S(1)} %collective-permute-done.19.refs_4_.refs_1_) | copy-start | bytes 983044
  77.2 1.2 %copy-start.20 = (f32[2,32,1280]{2,1,0:T(8,128)}, f32[2,32,1280]{2,1,0:T(8,128)S(1)}, u32[]{:S(2)}) copy-start(f32[2,32,1280]{2,1,0:T(8,128)S(1)} %collective-permute-done.20.refs_5_.refs_3_) | copy-start | bytes 983044
  78.4 0.6 copy-start.27
  79.1 4.7 %collective-permute-start.21 = (f32[32,768]{1,0:T(8,128)S(1)}, f32[32,768]{1,0:T(8,128)}, u32[]{:S(2)}, u32[]{:S(2)}) collective-permute-start(f32[32,768]{1,0:T(8,128)S(1)} %get-tuple-element.62), channel_id=1, source_target_pairs={{0,32},{1,97},{2,34},{3,99},{4,36},{5,101},{6,38},{7,103},{8,40},{... | collective-permute-start | bytes 294920 | tf_op jit(solution)/shard_map/ppermute | solution.py:35
  83.8 19.4 %copy-start.5 = (bf16[4,512,512]{2,1,0:T(8,128)(2,1)S(1)}, bf16[4,512,512]{2,1,0:T(8,128)(2,1)}, u32[]{:S(2)}) copy-start(bf16[4,512,512]{2,1,0:T(8,128)(2,1)} %copy-done.4) | copy-start | bytes 6291460
  84.8 4.7 %collective-permute-start.22 = (f32[32,768]{1,0:T(8,128)S(1)}, f32[32,768]{1,0:T(8,128)S(1)}, u32[]{:S(2)}, u32[]{:S(2)}) collective-permute-start(f32[32,768]{1,0:T(8,128)S(1)} %add.64), channel_id=1, source_target_pairs={{0,8},{1,25},{2,10},{3,27},{4,12},{5,29},{6,14},{7,31},{8,0},{9,17... | collective-permute-start | bytes 294920 | tf_op jit(solution)/shard_map/ppermute | solution.py:35
  85.2 0.8 copy-start.22
  89.6 13.6 %copy-start.1 = (bf16[4,2,1024,128]{3,2,1,0:T(8,128)(2,1)S(1)}, bf16[4,2,1024,128]{3,2,1,0:T(8,128)(2,1)}, u32[]{:S(2)}) copy-start(bf16[4,2,1024,128]{3,2,1,0:T(8,128)(2,1)} %copy-done) | copy-start | bytes 6291460
  89.6 13.6 %copy-start.3 = (bf16[4,512,512]{2,1,0:T(8,128)(2,1)S(1)}, bf16[4,512,512]{2,1,0:T(8,128)(2,1)}, u32[]{:S(2)}) copy-start(bf16[4,512,512]{2,1,0:T(8,128)(2,1)} %copy-done.2) | copy-start | bytes 6291460
  89.6 7.6 %collective-permute-start.23 = (f32[32,768]{1,0:T(8,128)S(1)}, f32[32,768]{1,0:T(8,128)S(1)}, u32[]{:S(2)}, u32[]{:S(2)}) collective-permute-start(f32[32,768]{1,0:T(8,128)S(1)} %add.65), channel_id=1, source_target_pairs={{0,96},{1,33},{2,98},{3,35},{4,100},{5,37},{6,102},{7,39},{8,104},... | collective-permute-start | bytes 294920 | tf_op jit(solution)/shard_map/ppermute | solution.py:35
  91.5 1.0 copy-start.15
  92.5 1.0 copy-start.17
  93.4 1.0 copy-start.19
  94.4 1.0 copy-start.21
  95.4 7.8 %copy-start.23 = (f32[3,32,32]{2,1,0:T(8,128)S(1)}, f32[3,32,32]{2,1,0:T(8,128)}, u32[]{:S(2)}) copy-start(f32[3,32,32]{2,1,0:T(8,128)} %factor.1.refs_4_.refs_9_) | copy-start | bytes 36868
  97.3 5.9 %collective-permute-start.24 = (f32[32,768]{1,0:T(8,128)S(1)}, f32[32,768]{1,0:T(8,128)S(1)}, u32[]{:S(2)}, u32[]{:S(2)}) collective-permute-start(f32[32,768]{1,0:T(8,128)S(1)} %add.66), channel_id=1, source_target_pairs={{0,24},{1,9},{2,26},{3,11},{4,28},{5,13},{6,30},{7,15},{8,16},{9,1... | collective-permute-start | bytes 294920 | tf_op jit(solution)/shard_map/ppermute | solution.py:35
  103.2 1.6 %copy-start.7 = (bf16[4,2,1024,128]{3,2,1,0:T(8,128)(2,1)S(1)}, bf16[4,2,1024,128]{3,2,1,0:T(8,128)(2,1)}, u32[]{:S(2)}) copy-start(bf16[4,2,1024,128]{3,2,1,0:T(8,128)(2,1)} %copy-done.6) | copy-start | bytes 6291460
  104.8 1.6 %copy-start.9 = (bf16[4,2,1024,128]{3,2,1,0:T(8,128)(2,1)S(1)}, bf16[4,2,1024,128]{3,2,1,0:T(8,128)(2,1)}, u32[]{:S(2)}) copy-start(bf16[4,2,1024,128]{3,2,1,0:T(8,128)(2,1)} %copy-done.8) | copy-start | bytes 6291460
  106.4 1.6 %copy-start.11 = (bf16[4,512,512]{2,1,0:T(8,128)(2,1)S(1)}, bf16[4,512,512]{2,1,0:T(8,128)(2,1)}, u32[]{:S(2)}) copy-start(bf16[4,512,512]{2,1,0:T(8,128)(2,1)} %copy-done.10) | copy-start | bytes 6291460
  108.0 1.6 %copy-start.13 = (bf16[4,512,512]{2,1,0:T(8,128)(2,1)S(1)}, bf16[4,512,512]{2,1,0:T(8,128)(2,1)}, u32[]{:S(2)}) copy-start(bf16[4,512,512]{2,1,0:T(8,128)(2,1)} %copy-done.12) | copy-start | bytes 6291460

commit v3 on v2

v3 whole, which is shorter than its diff:
```python
import functools

import jax
import jax.numpy as jnp
from jax import lax
from jax.experimental import pallas as pl
from jax.experimental.pallas import tpu as pltpu
from jax.sharding import PartitionSpec as P

F32, BF16 = jnp.float32, jnp.bfloat16
ROWS, COLS = 8192, 128
OROWS, OCOLS = 4096, 512
RANK = 32
REPLICAS = 16
STEPS = 3
PARTS = 1 << STEPS
CH = ROWS // (2 * PARTS)
OCH = OROWS // (4 * PARTS)
WIDE = CH + OCH
MIB = 1 << 20

X, Y, Z = 0, 1, 2


def other_turn(steps):
    return [(axis, 1 - turn) for axis, turn in steps]


FIRST = [(X, 0), (Y, 0), (Z, 0), (X, 1), (Y, 1), (Z, 1)]
SECOND = [(Y, 0), (Z, 0), (X, 0), (Y, 1), (Z, 1), (X, 1)]
CHAINS = ((FIRST, other_turn(FIRST)), (SECOND, other_turn(SECOND)))
RIGHT = ([(Y, 0), (Z, 0), (Y, 1), (Z, 1)], [(Z, 0), (Y, 0), (Z, 1), (Y, 1)])


def pairs(steps, k):
    out = []
    for i in range(128):
        q, core = [(i // 2) % 4, i // 32, (i // 8) % 4], i % 2
        axis, turn = steps[core][k]
        q[axis] ^= 3 if turn else 1
        out.append((i, ((q[1] * 4 + q[2]) * 4 + q[0]) * 2 + core))
    return out


CORES = [(i, i ^ 1) for i in range(128)]


def send(x, to):
    return lax.ppermute(x, ("dp", "mp"), to)


def my_chunk(chain, dh, i):
    dp, mp = lax.axis_index("dp"), lax.axis_index("mp")
    q = (lax.div(mp, 2), lax.div(dp, 4), lax.rem(dp, 4))
    half = jnp.bitwise_xor(lax.rem(mp, 2), dh)

    def own(step):
        axis, turn = step
        high, low = lax.div(q[axis], 2), lax.rem(q[axis], 2)
        return high if turn else jnp.bitwise_xor(high, low)

    chunk = half
    for k in range(STEPS):
        bit = (1 - half) * own(CHAINS[chain][0][k]) + half * own(CHAINS[chain][1][k])
        chunk = 2 * chunk + jnp.bitwise_xor(bit, (i >> (STEPS - 1 - k)) & 1)
    return chunk


def chunk_rows(chain, dh, i):
    t = my_chunk(chain, dh, i)
    return pl.ds(pl.multiple_of(t * CH, CH), CH), pl.ds(pl.multiple_of(chain * (OROWS // 2) + t * OCH, OCH), OCH)


def dot_nt(a, b):
    return lax.dot_general(a, b, (((1,), (1,)), ((), ())), preferred_element_type=F32)


def dot(a, b):
    return jnp.dot(a, b, preferred_element_type=F32)


def split2(a):
    high = a.astype(BF16)
    return high, (a - high.astype(F32)).astype(BF16)


def split3(a):
    high = a.astype(BF16)
    rest = a - high.astype(F32)
    mid = rest.astype(BF16)
    return high, mid, (rest - mid.astype(F32)).astype(BF16)


def loads(refs, bufs, sems, dh, i):
    gkv, ekv, gout, eout = refs
    bgkv, bekv, bgout, beout = bufs
    copies = []
    for chain in range(2):
        rows, orows = chunk_rows(chain, dh, i)
        for n, (src, dst) in enumerate(
            (
                (gkv.at[0, chain, rows, :], bgkv),
                (ekv.at[0, chain, rows, :], bekv),
                (gout.at[0, orows, :], bgout),
                (eout.at[0, orows, :], beout),
            )
        ):
            copies.append(pltpu.make_async_copy(src, dst.at[i, chain], sems.at[i, chain, n]))
    return copies


HBM = pl.BlockSpec(memory_space=pltpu.HBM)
VM = pl.BlockSpec(memory_space=pltpu.VMEM)


def cost(us):
    return pl.CostEstimate(flops=0, bytes_accessed=int(us * 3_000_000), transcendentals=0)


def part_kernel(dh, gkv, ekv, gout, eout, bkv_hbm, bout_hbm, out, bgkv, bekv, bgout, beout, bkv, bout, bsems, sems):
    basis = [
        pltpu.make_async_copy(bkv_hbm, bkv, bsems.at[0]),
        pltpu.make_async_copy(bout_hbm, bout, bsems.at[1]),
    ]
    copies = [loads((gkv, ekv, gout, eout), (bgkv, bekv, bgout, beout), sems, dh, i) for i in range(PARTS)]
    for copy in basis:
        copy.start()
    for i in range(AHEAD):
        for copy in copies[i]:
            copy.start()
    for copy in basis:
        copy.wait()
    kv = [jnp.concatenate(split3(bkv[a]), axis=0) for a in range(2)]
    kv = [jnp.concatenate([b, b], axis=1) for b in kv]
    ob = jnp.concatenate(split3(bout[...]), axis=0)

    def fold(r):
        return r[:RANK] + (r[RANK : 2 * RANK] + r[2 * RANK :])

    for i in range(PARTS):
        for copy in copies[i]:
            copy.wait()
        if i + AHEAD < PARTS:
            for copy in copies[i + AHEAD]:
                copy.start()
        for a in range(2):
            both = jnp.concatenate([bgkv[i, a], bekv[i, a]], axis=1)
            out[a, i, :, :CH] = fold(dot_nt(kv[a], both))
            out[a, i, :, CH:] = fold(dot_nt(ob, bgout[i, a]) + dot_nt(ob, beout[i, a]))


AHEAD = 3


def part(dh, args):
    kv = jax.ShapeDtypeStruct((PARTS, 2, CH, COLS), BF16)
    out = jax.ShapeDtypeStruct((PARTS, 2, OCH, OCOLS), BF16)
    result = pl.pallas_call(
        functools.partial(part_kernel, dh),
        out_shape=(jax.ShapeDtypeStruct((2, PARTS, RANK, WIDE), F32), kv, kv, out, out),
        in_specs=[HBM] * 6,
        out_specs=(VM,) * 5,
        scratch_shapes=[
            pltpu.VMEM((2, RANK, COLS), F32),
            pltpu.VMEM((RANK, OCOLS), F32),
            pltpu.SemaphoreType.DMA((2,)),
            pltpu.SemaphoreType.DMA((PARTS, 2, 4)),
        ],
        compiler_params=pltpu.CompilerParams(vmem_limit_bytes=20 * MIB),
        cost_estimate=cost(4),
        name="part",
    )(*args)
    return result[0], result[1:]


def tree(items):
    while len(items) > 1:
        items = [a + b for a, b in zip(items[::2], items[1::2])]
    return items[0]


def right_kernel(group, n_before, *refs):
    bgkv, bekv, bgout, beout, lead_a, lead_b = refs[:6]
    before = refs[6 : 6 + n_before]
    right, gram = refs[6 + n_before :]

    def fold(r):
        return r[:RANK] + r[RANK:]

    def square(parts):
        g = dot_nt(jnp.concatenate(parts, axis=0), jnp.concatenate(parts, axis=0))

        def at(i, j):
            return g[i * RANK : (i + 1) * RANK, j * RANK : (j + 1) * RANK]

        return at(0, 0) + ((at(0, 1) + at(1, 0)) + ((at(0, 2) + at(2, 0)) + at(1, 1)))

    sums = [0.0, 0.0, 0.0]
    grams = [[], [], [], []]
    for j in range(PARTS // 2):
        i = group * (PARTS // 2) + j
        for k, x in enumerate((lead_a, lead_b)):
            parts = split3(x[j])
            kv, o = [p[:, :CH] for p in parts], [p[:, CH:] for p in parts]
            grams[k].append(square(kv))
            grams[2 + k].append(square(o))
            both = jnp.concatenate([bgkv[i, k], bekv[i, k]], axis=1)
            r = fold(dot(jnp.concatenate(kv[:2], axis=0), both))
            sums[k] += r[:, :COLS] + r[:, COLS:]
            two = jnp.concatenate(o[:2], axis=0)
            sums[2] += fold(dot(two, bgout[i, k]) + dot(two, beout[i, k]))
    for k in range(4):
        gram[k] = tree(grams[k])
    sums = jnp.concatenate(sums, axis=1)
    for other in before:
        sums += other[...]
    right[...] = sums


def right_part(group, bufs, lead, before=()):
    return pl.pallas_call(
        functools.partial(right_kernel, group, len(before)),
        out_shape=(
            jax.ShapeDtypeStruct((RANK, 2 * COLS + OCOLS), F32),
            jax.ShapeDtypeStruct((4, RANK, RANK), F32),
        ),
        in_specs=[VM] * (6 + len(before)),
        out_specs=(VM, VM),
        compiler_params=pltpu.CompilerParams(vmem_limit_bytes=20 * MIB),
        cost_estimate=cost(2),
        name="right",
    )(*bufs, *lead, *before)


def factor_kernel(g0, g1, g2, g3, out):
    row = lax.broadcasted_iota(jnp.int32, (RANK, 2 * RANK), 0)
    col = lax.broadcasted_iota(jnp.int32, (RANK, 2 * RANK), 1)
    eye = jnp.where(col == row + RANK, 1.0, 0.0).astype(F32)
    gram = [(g0[k] + g1[k]) + (g2[k] + g3[k]) for k in range(4)]
    gram[2] += gram[3]
    wide = [jnp.concatenate([gram[k], jnp.zeros((RANK, RANK), F32)], axis=1) + eye for k in range(3)]
    scale = [jnp.zeros((RANK, 1), F32)] * 3
    below = lax.broadcasted_iota(jnp.int32, (RANK, 1), 0)
    for i in range(RANK):
        for k in range(3):
            pivot = wide[k][i : i + 1, :]
            d = wide[k][i : i + 1, i : i + 1]
            scale[k] = jnp.where(below == i, lax.rsqrt(d), scale[k])
            factor = jnp.where(below > i, wide[k][:, i : i + 1] / d, 0.0)
            wide[k] = wide[k] - factor * pivot
    for k in range(3):
        out[k] = wide[k][:, RANK:] * scale[k]


def factor(grams):
    return pl.pallas_call(
        factor_kernel,
        out_shape=jax.ShapeDtypeStruct((3, RANK, RANK), F32),
        in_specs=[VM] * 4,
        out_specs=VM,
        compiler_params=pltpu.CompilerParams(vmem_limit_bytes=4 * MIB),
        cost_estimate=cost(4),
        name="factor",
    )(*grams)


def left_kernel(dh, *refs):
    a_own, a_got, b_own, b_got, w = refs[:5]
    left_kv, left_out, ortho, bkv, bout, sems = refs[-6:]
    weights = []
    for k in range(3):
        w1, w2, w3 = split3(w[k])
        weights.append(jnp.concatenate([w1, w1, w2, w1, w2, w3], axis=1))

    def apply(k, x):
        l1, l2, l3 = split3(x)
        return dot(weights[k], jnp.concatenate([l1, l2, l1, l3, l2, l1], axis=0))

    def packed(o):
        high = o.astype(BF16).astype(F32)
        rest = o - high
        return jnp.transpose(jnp.concatenate([high, rest, high, jnp.zeros_like(o)], axis=0)).astype(BF16)

    copies = []
    for i in range(PARTS):
        for s, (own, got) in enumerate(((a_own, a_got), (b_own, b_got))):
            x = (own, got)[i // (PARTS // 2)][i % (PARTS // 2)]
            o_kv = apply(s, x[:, :CH])
            o_out = apply(2, x[:, CH:])
            bkv[i, s] = o_kv * (ROWS**0.5)
            bout[i, s] = o_out * (OROWS**0.5)
            ortho[i, s, :CH] = packed(o_kv)
            ortho[i, s, CH:] = packed(o_out)
            rows, orows = chunk_rows(s, dh, i)
            copies.append(pltpu.make_async_copy(bkv.at[i, s], left_kv.at[s, :, rows], sems.at[i, s, 0]))
            copies.append(pltpu.make_async_copy(bout.at[i, s], left_out.at[:, orows], sems.at[i, s, 1]))
            copies[-2].start()
            copies[-1].start()
    for copy in copies:
        copy.wait()


def left_part(dh, lead, w, before=()):
    return pl.pallas_call(
        functools.partial(left_kernel, dh),
        out_shape=(
            jax.ShapeDtypeStruct((2, RANK, ROWS), F32),
            jax.ShapeDtypeStruct((RANK, OROWS), F32),
            jax.ShapeDtypeStruct((PARTS, 2, WIDE, 128), BF16),
        ),
        in_specs=[VM] * 5 + [HBM] * len(before),
        out_specs=(HBM, HBM, VM),
        scratch_shapes=[
            pltpu.VMEM((PARTS, 2, RANK, CH), F32),
            pltpu.VMEM((PARTS, 2, RANK, OCH), F32),
            pltpu.SemaphoreType.DMA((PARTS, 2, 2)),
        ],
        input_output_aliases={5: 0, 6: 1} if before else {},
        compiler_params=pltpu.CompilerParams(vmem_limit_bytes=16 * MIB),
        cost_estimate=cost(2),
        name="left",
    )(*lead, w, *before)


def error_kernel(*refs):
    halves = (refs[:4], refs[4:8])
    total, w, ortho = refs[8], refs[9], refs[10:12]
    right_kv, right_out, new_kv, new_out, nkv, nout, nsems = refs[12:]
    packed = []
    for k, (at, n) in enumerate(((0, COLS), (COLS, COLS), (2 * COLS, OCOLS))):
        w1, w2, w3 = split3(w[k])
        r1, r2, r3 = split3(total[:, at : at + n] * (1.0 / REPLICAS))
        right = dot(
            jnp.concatenate([w1, w1, w2, w1, w2, w3], axis=1),
            jnp.concatenate([r1, r2, r1, r3, r2, r1], axis=0),
        )
        if k < 2:
            right_kv[k] = right
        else:
            right_out[...] = right
        high, low = split2(right)
        packed.append(jnp.concatenate([high, high, low, jnp.zeros_like(high)], axis=0))
    stores = []
    for j in range(2 * PARTS):
        dh, i = j // PARTS, j % PARTS
        bgkv, bekv, bgout, beout = halves[dh]
        for s in range(2):
            merged = bgkv[i, s].astype(F32) + bekv[i, s].astype(F32)
            nkv[j, s] = (merged - dot(ortho[dh][i, s, :CH], packed[s])).astype(BF16)
            merged = bgout[i, s].astype(F32) + beout[i, s].astype(F32)
            nout[j, s] = (merged - dot(ortho[dh][i, s, CH:], packed[2])).astype(BF16)
            rows, orows = chunk_rows(s, dh, i)
            stores.append(pltpu.make_async_copy(nkv.at[j, s], new_kv.at[0, s, rows, :], nsems.at[j, s, 0]))
            stores.append(pltpu.make_async_copy(nout.at[j, s], new_out.at[0, orows, :], nsems.at[j, s, 1]))
            stores[-2].start()
            stores[-1].start()
    for copy in stores:
        copy.wait()


def errors(bufs, total, w, ortho):
    return pl.pallas_call(
        error_kernel,
        out_shape=(
            jax.ShapeDtypeStruct((2, RANK, COLS), F32),
            jax.ShapeDtypeStruct((RANK, OCOLS), F32),
            jax.ShapeDtypeStruct((1, 2, ROWS, COLS), BF16),
            jax.ShapeDtypeStruct((1, OROWS, OCOLS), BF16),
        ),
        in_specs=[VM] * 12,
        out_specs=(VM, VM, HBM, HBM),
        scratch_shapes=[
            pltpu.VMEM((2 * PARTS, 2, CH, COLS), BF16),
            pltpu.VMEM((2 * PARTS, 2, OCH, OCOLS), BF16),
            pltpu.SemaphoreType.DMA((2 * PARTS, 2, 2)),
        ],
        compiler_params=pltpu.CompilerParams(vmem_limit_bytes=24 * MIB),
        cost_estimate=cost(5),
        name="errors",
    )(*bufs, total, w, *ortho)


def on_device(grad_kv, error_kv, grad_out, error_out, basis_kv, basis_out):
    args = (grad_kv, error_kv, grad_out, error_out, jnp.swapaxes(basis_kv, 1, 2), basis_out.T)
    args = [pltpu.with_memory_space_constraint(x, pltpu.HBM) for x in args]
    lead, bufs_other = part(1, args)
    got = send(lead, CORES)
    lead, bufs_own = part(0, args)
    both = list(lead + got)

    for k in range(2 * STEPS):
        for s in range(2):
            x = both[s]
            if k < STEPS:
                n = x.shape[0] // 2
                both[s] = x[:n] + send(x[n:], pairs(CHAINS[s], k))
            else:
                both[s] = x + send(x, pairs(CHAINS[s], k))
    for k in reversed(range(1, STEPS)):
        both = [jnp.concatenate([x, send(x, pairs(CHAINS[s], k))]) for s, x in enumerate(both)]
    own0 = both
    own1 = [send(x, pairs(CHAINS[s], 0)) for s, x in enumerate(both)]
    other0 = [send(x, CORES) for x in own0]
    sum1, gram1 = right_part(0, bufs_own, own0)
    sum2, gram2 = right_part(0, bufs_other, other0)
    own1, sum1, sum2 = lax.optimization_barrier((own1, sum1, sum2))
    other1 = [send(x, CORES) for x in own1]
    sum3, gram3 = right_part(1, bufs_own, own1)
    total, gram4 = right_part(1, bufs_other, other1, (sum1, sum2, sum3))
    own = (own0[0], own1[0], own0[1], own1[1])
    other = (other0[0], other1[0], other0[1], other1[1])
    w = factor((gram1, gram3, gram2, gram4))
    total = total + send(total, pairs(RIGHT, 0))
    total, w = lax.optimization_barrier((total, w))
    *left, ortho_own = left_part(0, own, w)
    total = total + send(total, pairs(RIGHT, 1))
    total, left = lax.optimization_barrier((total, left))
    left_kv, left_out, ortho_other = left_part(1, other, w, left)
    total = total + send(total, pairs(RIGHT, 2))
    total, ortho_other = lax.optimization_barrier((total, ortho_other))
    total = total + send(total, pairs(RIGHT, 3))
    right_kv, right_out, new_kv, new_out = errors((*bufs_own, *bufs_other), total, w, (ortho_own, ortho_other))
    return (
        jnp.swapaxes(left_kv, 1, 2),
        left_out.T,
        jnp.swapaxes(right_kv, 1, 2),
        right_out.T,
        new_kv,
        new_out,
    )


def solution(mesh):
    placed = (
        P("dp", None, None, "mp"),
        P("dp", None, None, "mp"),
        P("dp", None, "mp"),
        P("dp", None, "mp"),
        P(None, "mp", None),
        P("mp", None),
    )
    return jax.shard_map(
        on_device,
        mesh=mesh,
        in_specs=placed,
        out_specs=(
            P(),
            P(),
            P(None, "mp", None),
            P("mp", None),
            P("dp", None, None, "mp"),
            P("dp", None, "mp"),
        ),
        check_vma=False,
    )
```

time: 115 us -> 104 us (0.904)
  local copies, waits for them, and re-layouts: 12.5 us -> 0.08 us
  waiting for transfers between devices: 26.8 us -> 36.1 us
  Pallas kernels: 33.2 us -> 29.2 us
  starting transfers between devices: 39.2 us -> 36.3 us
    unnamed x56 -> x0, local copies, waits for them, and re-layouts: 12.3 us -> none
    ppermute x25 -> x27, waiting for transfers between devices: 26.8 us -> 36.1 us  [send(): return lax.ppermute(x, ('dp', 'mp'), to)]
    pallas_call x2, Pallas kernels: 16 us -> 12.4 us  [part(): pl.pallas_call(functools.partial(part_kernel, dh), out_shape=(jax.ShapeDt...]
    ppermute x25 -> x27, starting transfers between devices: 39.2 us -> 36.3 us  [send(): return lax.ppermute(x, ('dp', 'mp'), to)]
    pallas_call x1, Pallas kernels: 4.35 us -> 2.87 us  [factor(): pl.pallas_call(factor_kernel, out_shape=jax.ShapeDtypeStruct((3, RANK, RA...]
  transfers between devices with their start and end apart: 25 -> 27, of which waited for: 17 -> 20; matrix products, arithmetic and copies ran while one was open for 0% -> 0% of each run, Pallas kernels for 18% -> 16%
where the time goes in v3:
time: 104 us; the launch traced here: 103 us
  starting transfers between devices  36.3 us (35%)
  waiting for transfers between devices  36.1 us (35%)
  Pallas kernels  29.2 us (28%)
  between operations  1.06 us (1%)
    ppermute x27, starting transfers between devices, send(): return lax.ppermute(x, ('dp', 'mp'), to)  36.3 us
    ppermute x27, waiting for transfers between devices, send(): return lax.ppermute(x, ('dp', 'mp'), to)  36.1 us
    pallas_call x2, Pallas kernels, part(): pl.pallas_call(functools.partial(part_kernel, dh), out_shape=(jax.ShapeDt...  12.4 us
    pallas_call x4, Pallas kernels, right_part(): pl.pallas_call(functools.partial(right_kernel, group, len(before)), out_s...  4.95 us
    pallas_call x1, Pallas kernels, errors(): pl.pallas_call(error_kernel, out_shape=(jax.ShapeDtypeStruct((2, RANK, CO...  4.85 us
    pallas_call x2, Pallas kernels, left_part(): pl.pallas_call(functools.partial(left_kernel, dh), out_shape=(jax.ShapeDt...  4.17 us
    pallas_call x1, Pallas kernels, factor(): pl.pallas_call(factor_kernel, out_shape=jax.ShapeDtypeStruct((3, RANK, RA...  2.87 us
  transfers between devices with their start and end apart: 27, of which 20 were waited for; matrix products, arithmetic and copies ran while one was open for 0% of the time, Pallas kernels for 16%

profile of v3, /device:TPU:0, one launch (start us, length us, event | category | flops | bytes accessed | tf_op | source)
XLA Modules:
  0.0 103.3 jit_solution(16544135773315027140)
XLA Ops:
  0.6 6.2 %part.3 = (f32[2,8,32,640]{3,2,1,0:T(8,128)S(1)}, bf16[8,2,512,128]{3,2,1,0:T(8,128)(2,1)S(1)}, bf16[8,2,512,128]{3,2,1,0:T(8,128)(2,1)S(1)}, bf16[8,2,128,512]{...) custom-call(bf16[1,2,8192,128]{3,2,1,0:T(8,128)(2,1)} %gkv.3, bf16[1,2,8192,128]{3,2,1,0:T(8,128)(2,1)} %ekv.3, ...), custom_call_target="tpu_custom_call" | custom-call | bytes 12000000 | tf_op jit(solution)/shard_map/part/pallas_call | solution.py:158
  6.8 0.1 collective-permute-start
  6.9 6.2 %part.2 = (f32[2,8,32,640]{3,2,1,0:T(8,128)S(1)}, bf16[8,2,512,128]{3,2,1,0:T(8,128)(2,1)S(1)}, bf16[8,2,512,128]{3,2,1,0:T(8,128)(2,1)S(1)}, bf16[8,2,128,512]{...) custom-call(bf16[1,2,8192,128]{3,2,1,0:T(8,128)(2,1)} %gkv.3, bf16[1,2,8192,128]{3,2,1,0:T(8,128)(2,1)} %ekv.3, ...), custom_call_target="tpu_custom_call" | custom-call | bytes 12000000 | tf_op jit(solution)/shard_map/part/pallas_call | solution.py:158
  13.1 0.0 collective-permute-done
  13.1 0.1 add.51
  13.3 1.7 %collective-permute-start.11 = (f32[4,32,640]{2,1,0:T(8,128)S(1)}, f32[4,32,640]{2,1,0:T(8,128)S(1)}, u32[]{:S(2)}, u32[]{:S(2)}) collective-permute-start(f32[4,32,640]{2,1,0:T(8,128)S(1)} %get-tuple-element.86), channel_id=1, source_target_pairs={{0,32},{1,97},{2,34},{3,99},{4,36},{5,101},{6,38},{7,103},{8,40},{... | collective-permute-start | bytes 983048 | tf_op jit(solution)/shard_map/ppermute | solution.py:49
  15.1 1.5 %collective-permute-start.1 = (f32[4,32,640]{2,1,0:T(8,128)S(1)}, f32[4,32,640]{2,1,0:T(8,128)S(1)}, u32[]{:S(2)}, u32[]{:S(2)}) collective-permute-start(f32[4,32,640]{2,1,0:T(8,128)S(1)} %get-tuple-element.87), channel_id=1, source_target_pairs={{0,2},{1,7},{2,0},{3,5},{4,6},{5,3},{6,4},{7,1},{8,10},{9,15},{10,... | collective-permute-start | bytes 983048 | tf_op jit(solution)/shard_map/ppermute | solution.py:49
  16.6 3.9 %collective-permute-done.11 = f32[4,32,640]{2,1,0:T(8,128)S(1)} collective-permute-done((f32[4,32,640]{2,1,0:T(8,128)S(1)}, f32[4,32,640]{2,1,0:T(8,128)S(1)}, u32[]{:S(2)}, u32[]{:S(2)}) %collective-permute-start.11) | collective-permute-done | bytes 327712 | tf_op jit(solution)/shard_map/ppermute | solution.py:49
  20.5 1.7 %collective-permute-done.1 = f32[4,32,640]{2,1,0:T(8,128)S(1)} collective-permute-done((f32[4,32,640]{2,1,0:T(8,128)S(1)}, f32[4,32,640]{2,1,0:T(8,128)S(1)}, u32[]{:S(2)}, u32[]{:S(2)}) %collective-permute-start.1) | collective-permute-done | bytes 327712 | tf_op jit(solution)/shard_map/ppermute | solution.py:49
  22.2 0.1 fusion
  22.2 2.0 %collective-permute-start.12 = (f32[2,32,640]{2,1,0:T(8,128)S(1)}, f32[2,32,640]{2,1,0:T(8,128)S(1)}, u32[]{:S(2)}, u32[]{:S(2)}) collective-permute-start(f32[2,32,640]{2,1,0:T(8,128)S(1)} %slice.77), channel_id=1, source_target_pairs={{0,8},{1,25},{2,10},{3,27},{4,12},{5,29},{6,14},{7,31},{8,0},{9,17... | collective-permute-start | bytes 491528 | tf_op jit(solution)/shard_map/ppermute | solution.py:49
  24.3 0.5 collective-permute-start.2
  24.8 2.9 %collective-permute-done.12 = f32[2,32,640]{2,1,0:T(8,128)S(1)} collective-permute-done((f32[2,32,640]{2,1,0:T(8,128)S(1)}, f32[2,32,640]{2,1,0:T(8,128)S(1)}, u32[]{:S(2)}, u32[]{:S(2)}) %collective-permute-start.12) | collective-permute-done | bytes 163872 | tf_op jit(solution)/shard_map/ppermute | solution.py:49
  27.7 1.6 %collective-permute-start.13 = (f32[1,32,640]{2,1,0:T(8,128)S(1)}, f32[1,32,640]{2,1,0:T(8,128)S(1)}, u32[]{:S(2)}, u32[]{:S(2)}) collective-permute-start(f32[1,32,640]{2,1,0:T(8,128)S(1)} %slice.79), channel_id=1, source_target_pairs={{0,2},{1,7},{2,0},{3,5},{4,6},{5,3},{6,4},{7,1},{8,10},{9,15},{10,... | collective-permute-start | bytes 245768 | tf_op jit(solution)/shard_map/ppermute | solution.py:49
  29.3 0.4 collective-permute-done.2
  29.7 1.6 %collective-permute-start.3 = (f32[1,32,640]{2,1,0:T(8,128)S(1)}, f32[1,32,640]{2,1,0:T(8,128)S(1)}, u32[]{:S(2)}, u32[]{:S(2)}) collective-permute-start(f32[1,32,640]{2,1,0:T(8,128)S(1)} %slice.73), channel_id=1, source_target_pairs={{0,8},{1,25},{2,10},{3,27},{4,12},{5,29},{6,14},{7,31},{8,0},{9,17... | collective-permute-start | bytes 245768 | tf_op jit(solution)/shard_map/ppermute | solution.py:49
  31.3 0.9 collective-permute-done.13
  32.2 2.3 %collective-permute-start.14 = (f32[1,32,640]{2,1,0:T(8,128)S(1)}, f32[1,32,640]{2,1,0:T(8,128)S(1)}, u32[]{:S(2)}, u32[]{:S(2)}) collective-permute-start(f32[1,32,640]{2,1,0:T(8,128)S(1)} %slice_add_fusion.2), channel_id=1, source_target_pairs={{0,96},{1,33},{2,98},{3,35},{4,100},{5,37},{6,102},{7,39},{8,104},... | collective-permute-start | bytes 245768 | tf_op jit(solution)/shard_map/ppermute | solution.py:49
  34.5 0.0 collective-permute-done.3
  34.5 2.8 %collective-permute-start.4 = (f32[1,32,640]{2,1,0:T(8,128)S(1)}, f32[1,32,640]{2,1,0:T(8,128)S(1)}, u32[]{:S(2)}, u32[]{:S(2)}) collective-permute-start(f32[1,32,640]{2,1,0:T(8,128)S(1)} %slice_add_fusion.3), channel_id=1, source_target_pairs={{0,6},{1,3},{2,4},{3,1},{4,2},{5,7},{6,0},{7,5},{8,14},{9,11},{10,... | collective-permute-start | bytes 245768 | tf_op jit(solution)/shard_map/ppermute | solution.py:49
  37.3 0.6 collective-permute-done.14
  38.0 4.1 %collective-permute-start.15 = (f32[1,32,640]{2,1,0:T(8,128)S(1)}, f32[1,32,640]{2,1,0:T(8,128)S(1)}, u32[]{:S(2)}, u32[]{:S(2)}) collective-permute-start(f32[1,32,640]{2,1,0:T(8,128)S(1)} %add.61), channel_id=1, source_target_pairs={{0,24},{1,9},{2,26},{3,11},{4,28},{5,13},{6,30},{7,15},{8,16},{9,1... | collective-permute-start | bytes 245768 | tf_op jit(solution)/shard_map/ppermute | solution.py:49
  42.1 0.0 collective-permute-done.4
  42.1 2.3 %collective-permute-start.5 = (f32[1,32,640]{2,1,0:T(8,128)S(1)}, f32[1,32,640]{2,1,0:T(8,128)S(1)}, u32[]{:S(2)}, u32[]{:S(2)}) collective-permute-start(f32[1,32,640]{2,1,0:T(8,128)S(1)} %add.55), channel_id=1, source_target_pairs={{0,96},{1,33},{2,98},{3,35},{4,100},{5,37},{6,102},{7,39},{8,104},... | collective-permute-start | bytes 245768 | tf_op jit(solution)/shard_map/ppermute | solution.py:49
  44.4 0.1 collective-permute-done.15
  44.5 2.8 %collective-permute-start.16 = (f32[1,32,640]{2,1,0:T(8,128)S(1)}, f32[1,32,640]{2,1,0:T(8,128)S(1)}, u32[]{:S(2)}, u32[]{:S(2)}) collective-permute-start(f32[1,32,640]{2,1,0:T(8,128)S(1)} %add.62), channel_id=1, source_target_pairs={{0,6},{1,3},{2,4},{3,1},{4,2},{5,7},{6,0},{7,5},{8,14},{9,11},{10,... | collective-permute-start | bytes 245768 | tf_op jit(solution)/shard_map/ppermute | solution.py:49
  47.4 0.5 collective-permute-done.5
  47.9 2.8 %collective-permute-start.6 = (f32[1,32,640]{2,1,0:T(8,128)S(1)}, f32[1,32,640]{2,1,0:T(8,128)S(1)}, u32[]{:S(2)}, u32[]{:S(2)}) collective-permute-start(f32[1,32,640]{2,1,0:T(8,128)S(1)} %add.56), channel_id=1, source_target_pairs={{0,24},{1,9},{2,26},{3,11},{4,28},{5,13},{6,30},{7,15},{8,16},{9,1... | collective-permute-start | bytes 245768 | tf_op jit(solution)/shard_map/ppermute | solution.py:49
  50.7 0.7 collective-permute-start.17
  51.4 2.6 %collective-permute-done.6 = f32[1,32,640]{2,1,0:T(8,128)S(1)} collective-permute-done((f32[1,32,640]{2,1,0:T(8,128)S(1)}, f32[1,32,640]{2,1,0:T(8,128)S(1)}, u32[]{:S(2)}, u32[]{:S(2)}) %collective-permute-start.6) | collective-permute-done | bytes 81952 | tf_op jit(solution)/shard_map/ppermute | solution.py:49
  54.0 0.1 collective-permute-start.7
  54.1 1.2 %collective-permute-done.17 = f32[1,32,640]{2,1,0:T(8,128)S(1)} collective-permute-done((f32[1,32,640]{2,1,0:T(8,128)S(1)}, f32[1,32,640]{2,1,0:T(8,128)S(1)}, u32[]{:S(2)}, u32[]{:S(2)}) %collective-permute-start.17) | collective-permute-done | bytes 81952 | tf_op jit(solution)/shard_map/ppermute | solution.py:49
  55.2 0.9 collective-permute-start.18
  56.2 2.3 %collective-permute-done.7 = f32[1,32,640]{2,1,0:T(8,128)S(1)} collective-permute-done((f32[1,32,640]{2,1,0:T(8,128)S(1)}, f32[1,32,640]{2,1,0:T(8,128)S(1)}, u32[]{:S(2)}, u32[]{:S(2)}) %collective-permute-start.7) | collective-permute-done | bytes 81952 | tf_op jit(solution)/shard_map/ppermute | solution.py:49
  58.5 0.1 collective-permute-start.8
  58.6 2.1 %collective-permute-done.18 = f32[2,32,640]{2,1,0:T(8,128)S(1)} collective-permute-done((f32[2,32,640]{2,1,0:T(8,128)S(1)}, f32[2,32,640]{2,1,0:T(8,128)S(1)}, u32[]{:S(2)}, u32[]{:S(2)}) %collective-permute-start.18) | collective-permute-done | bytes 163872 | tf_op jit(solution)/shard_map/ppermute | solution.py:49
  60.7 0.1 collective-permute-start.20
  60.8 3.1 %collective-permute-done.8 = f32[2,32,640]{2,1,0:T(8,128)S(1)} collective-permute-done((f32[2,32,640]{2,1,0:T(8,128)S(1)}, f32[2,32,640]{2,1,0:T(8,128)S(1)}, u32[]{:S(2)}, u32[]{:S(2)}) %collective-permute-start.8) | collective-permute-done | bytes 163872 | tf_op jit(solution)/shard_map/ppermute | solution.py:49
  63.9 0.1 collective-permute-start.9
  64.0 0.1 collective-permute-start.19
  64.1 1.4 %collective-permute-start.10 = (f32[4,32,640]{2,1,0:T(8,128)S(1)}, f32[4,32,640]{2,1,0:T(8,128)S(1)}, u32[]{:S(2)}, u32[]{:S(2)}) collective-permute-start(f32[4,32,640]{2,1,0:T(8,128)S(1)} %pad_maximum_fusion.refs_4_.refs_0_), channel_id=1, source_target_pairs={{0,2},{1,7},{2,0},{3,5},{4,6},{5,3},{6,4},{7,1},{8,10},{9,15},{10,... | collective-permute-start | bytes 983048 | tf_op jit(solution)/shard_map/ppermute | solution.py:49
  65.5 1.2 %right.4 = (f32[32,768]{1,0:T(8,128)S(1)}, f32[4,32,32]{2,1,0:T(8,128)S(1)}) custom-call(bf16[8,2,512,128]{3,2,1,0:T(8,128)(2,1)S(1)} %get-tuple-element.47.refs_0_, bf16[8,2,512,128]{3,2,1,0:T(8,128)(2,1)S(1)} %get-tuple-element.48.refs_1_, bf16[8,2,128,512]{3,2,1,0:T(8,128)(2,1)S(1)} %get-tuple-element.49.refs_2_, ...), custom_call_target="tpu_custom_call" | custom-call | bytes 6000000 | tf_op jit(solution)/shard_map/right/pallas_call | solution.py:221
  66.7 0.0 collective-permute-done.20.refs_5_.refs_2_
  66.8 1.2 %right.5 = (f32[32,768]{1,0:T(8,128)S(1)}, f32[4,32,32]{2,1,0:T(8,128)S(1)}) custom-call(bf16[8,2,512,128]{3,2,1,0:T(8,128)(2,1)S(1)} %get-tuple-element.52.refs_0_.refs_4_, bf16[8,2,512,128]{3,2,1,0:T(8,128)(2,1)S(1)} %get-tuple-element.53.refs_1_.refs_5_, bf16[8,2,128,512]{3,2,1,0:T(8,128)(2,1)S(1)} %get-tuple-element.54.refs_2_.refs_6_, ...), custom_call_target="tpu_custom_call" | custom-call | bytes 6000000 | tf_op jit(solution)/shard_map/right/pallas_call | solution.py:221
  68.0 3.2 %collective-permute-done.19.refs_5_.refs_3_ = f32[4,32,640]{2,1,0:T(8,128)S(1)} collective-permute-done((f32[4,32,640]{2,1,0:T(8,128)S(1)}, f32[4,32,640]{2,1,0:T(8,128)S(1)}, u32[]{:S(2)}, u32[]{:S(2)}) %collective-permute-start.19) | collective-permute-done | bytes 327712 | tf_op jit(solution)/shard_map/ppermute | solution.py:49
  71.2 0.3 collective-permute-done.10.refs_4_.refs_1_
  71.4 2.3 %collective-permute-start.21 = (f32[4,32,640]{2,1,0:T(8,128)S(1)}, f32[4,32,640]{2,1,0:T(8,128)S(1)}, u32[]{:S(2)}, u32[]{:S(2)}) collective-permute-start(f32[4,32,640]{2,1,0:T(8,128)S(1)} %collective-permute-done.10.refs_4_.refs_1_), channel_id=1, source_target_pairs={{0,1},{1,0},{2,3},{3,2},{4,5},{5,4},{6,7},{7,6},{8,9},{9,8},{10,11... | collective-permute-start | bytes 983048 | tf_op jit(solution)/shard_map/ppermute | solution.py:49
  73.8 0.0 collective-permute-start.22
  73.8 1.2 %right.6 = (f32[32,768]{1,0:T(8,128)S(1)}, f32[4,32,32]{2,1,0:T(8,128)S(1)}) custom-call(bf16[8,2,512,128]{3,2,1,0:T(8,128)(2,1)S(1)} %get-tuple-element.47.refs_0_, bf16[8,2,512,128]{3,2,1,0:T(8,128)(2,1)S(1)} %get-tuple-element.48.refs_1_, bf16[8,2,128,512]{3,2,1,0:T(8,128)(2,1)S(1)} %get-tuple-element.49.refs_2_, ...), custom_call_target="tpu_custom_call" | custom-call | bytes 6000000 | tf_op jit(solution)/shard_map/right/pallas_call | solution.py:221
  75.0 0.0 collective-permute-done.21.refs_4_.refs_1_
  75.0 0.5 collective-permute-done.22.refs_5_.refs_3_
  75.5 1.2 %right.7 = (f32[32,768]{1,0:T(8,128)S(1)}, f32[4,32,32]{2,1,0:T(8,128)S(1)}) custom-call(bf16[8,2,512,128]{3,2,1,0:T(8,128)(2,1)S(1)} %get-tuple-element.52.refs_0_.refs_4_, bf16[8,2,512,128]{3,2,1,0:T(8,128)(2,1)S(1)} %get-tuple-element.53.refs_1_.refs_5_, bf16[8,2,128,512]{3,2,1,0:T(8,128)(2,1)S(1)} %get-tuple-element.54.refs_2_.refs_6_, ...), custom_call_target="tpu_custom_call" | custom-call | bytes 6000000 | tf_op jit(solution)/shard_map/right/pallas_call | solution.py:221
  76.7 0.1 collective-permute-start.23
  76.8 2.9 %factor.1.refs_4_.refs_9_ = f32[3,32,32]{2,1,0:T(8,128)S(1)} custom-call(f32[4,32,32]{2,1,0:T(8,128)S(1)} %get-tuple-element.63.g0, f32[4,32,32]{2,1,0:T(8,128)S(1)} %get-tuple-element.64.g1, f32[4,32,32]{2,1,0:T(8,128)S(1)} %get-tuple-element.65.g2, f32[4,32,32]{2,1,0:T(8,128)S(1)} %get-tuple-element.66.g3), custom_call_target="tpu_custom_call" | custom-call | bytes 12000000 | tf_op jit(solution)/shard_map/factor/pallas_call | solution.py:256
  79.7 1.7 %collective-permute-done.23 = f32[32,768]{1,0:T(8,128)S(1)} collective-permute-done((f32[32,768]{1,0:T(8,128)S(1)}, f32[32,768]{1,0:T(8,128)S(1)}, u32[]{:S(2)}, u32[]{:S(2)}) %collective-permute-start.23) | collective-permute-done | bytes 98336 | tf_op jit(solution)/shard_map/ppermute | solution.py:49
  81.5 0.1 collective-permute-start.24
  81.5 2.1 %left.2 = (f32[2,32,8192]{2,1,0:T(8,128)}, f32[32,4096]{1,0:T(8,128)}, bf16[8,2,640,128]{3,2,1,0:T(8,128)(2,1)S(1)}) custom-call(f32[4,32,640]{2,1,0:T(8,128)S(1)} %pad_maximum_fusion.refs_4_.refs_0_, f32[4,32,640]{2,1,0:T(8,128)S(1)} %collective-permute-done.10.refs_4_.refs_1_, f32[4,32,640]{2,1,0:T(8,128)S(1)} %pad_maximum_fusion.1.refs_5_.refs_2_, ...), custom_call_target="tpu_custom_call" | custom-call | bytes 6000000 | tf_op jit(solution)/shard_map/left/pallas_call | solution.py:304
  83.6 2.5 %collective-permute-done.24 = f32[32,768]{1,0:T(8,128)S(1)} collective-permute-done((f32[32,768]{1,0:T(8,128)S(1)}, f32[32,768]{1,0:T(8,128)S(1)}, u32[]{:S(2)}, u32[]{:S(2)}) %collective-permute-start.24) | collective-permute-done | bytes 98336 | tf_op jit(solution)/shard_map/ppermute | solution.py:49
  86.2 0.9 collective-permute-start.25
  87.1 2.1 %left.3 = (f32[2,32,8192]{2,1,0:T(8,128)}, f32[32,4096]{1,0:T(8,128)}, bf16[8,2,640,128]{3,2,1,0:T(8,128)(2,1)S(1)}) custom-call(f32[4,32,640]{2,1,0:T(8,128)S(1)} %collective-permute-done.9.refs_4_.refs_0_, f32[4,32,640]{2,1,0:T(8,128)S(1)} %collective-permute-done.21.refs_4_.refs_1_, ...), custom_call_target="tpu_custom_call", output_to_operand_aliasing={{0}: (5, {}), {1}: (6, {})} | custom-call | bytes 6000000 | tf_op jit(solution)/shard_map/left/pallas_call | solution.py:304
  89.2 2.9 %collective-permute-done.25 = f32[32,768]{1,0:T(8,128)S(1)} collective-permute-done((f32[32,768]{1,0:T(8,128)S(1)}, f32[32,768]{1,0:T(8,128)S(1)}, u32[]{:S(2)}, u32[]{:S(2)}) %collective-permute-start.25) | collective-permute-done | bytes 98336 | tf_op jit(solution)/shard_map/ppermute | solution.py:49
  92.1 3.3 %collective-permute-start.26 = (f32[32,768]{1,0:T(8,128)S(1)}, f32[32,768]{1,0:T(8,128)S(1)}, u32[]{:S(2)}, u32[]{:S(2)}) collective-permute-start(f32[32,768]{1,0:T(8,128)S(1)} %add.66), channel_id=1, source_target_pairs={{0,24},{1,97},{2,26},{3,99},{4,28},{5,101},{6,30},{7,103},{8,16},{... | collective-permute-start | bytes 294920 | tf_op jit(solution)/shard_map/ppermute | solution.py:49
  95.4 2.8 %collective-permute-done.26 = f32[32,768]{1,0:T(8,128)S(1)} collective-permute-done((f32[32,768]{1,0:T(8,128)S(1)}, f32[32,768]{1,0:T(8,128)S(1)}, u32[]{:S(2)}, u32[]{:S(2)}) %collective-permute-start.26) | collective-permute-done | bytes 98336 | tf_op jit(solution)/shard_map/ppermute | solution.py:49
  98.2 4.8 %errors.1 = (f32[2,32,128]{2,1,0:T(8,128)}, f32[32,512]{1,0:T(8,128)}, bf16[1,2,8192,128]{3,2,1,0:T(8,128)(2,1)}, bf16[1,4096,512]{2,1,0:T(8,128)(2,1)}) custom-call(bf16[8,2,512,128]{3,2,1,0:T(8,128)(2,1)S(1)} %get-tuple-element.47.refs_0_, bf16[8,2,512,128]{3,2,1,0:T(8,128)(2,1)S(1)} %get-tuple-element.48.refs_1_, ...), custom_call_target="tpu_custom_call" | custom-call | bytes 15000000 | tf_op jit(solution)/shard_map/errors/pallas_call | solution.py:362
  (25 shorter events, 0.3 us)
Async XLA Ops:
  6.8 6.3 %collective-permute-start = (f32[2,8,32,640]{3,2,1,0:T(8,128)S(1)}, f32[2,8,32,640]{3,2,1,0:T(8,128)S(1)}, u32[]{:S(2)}, u32[]{:S(2)}) collective-permute-start(f32[2,8,32,640]{3,2,1,0:T(8,128)S(1)} %get-tuple-element.46), channel_id=1, source_target_pairs={{0,1},{1,0},{2,3},{3,2},{4,5},{5,4},{6,7},{7,6},{8,9},{9,8},{10,11... | collective-permute-start | bytes 3932168 | tf_op jit(solution)/shard_map/ppermute | solution.py:49
  13.3 7.2 %collective-permute-start.11 = (f32[4,32,640]{2,1,0:T(8,128)S(1)}, f32[4,32,640]{2,1,0:T(8,128)S(1)}, u32[]{:S(2)}, u32[]{:S(2)}) collective-permute-start(f32[4,32,640]{2,1,0:T(8,128)S(1)} %get-tuple-element.86), channel_id=1, source_target_pairs={{0,32},{1,97},{2,34},{3,99},{4,36},{5,101},{6,38},{7,103},{8,40},{... | collective-permute-start | bytes 983048 | tf_op jit(solution)/shard_map/ppermute | solution.py:49
  15.1 7.1 %collective-permute-start.1 = (f32[4,32,640]{2,1,0:T(8,128)S(1)}, f32[4,32,640]{2,1,0:T(8,128)S(1)}, u32[]{:S(2)}, u32[]{:S(2)}) collective-permute-start(f32[4,32,640]{2,1,0:T(8,128)S(1)} %get-tuple-element.87), channel_id=1, source_target_pairs={{0,2},{1,7},{2,0},{3,5},{4,6},{5,3},{6,4},{7,1},{8,10},{9,15},{10,... | collective-permute-start | bytes 983048 | tf_op jit(solution)/shard_map/ppermute | solution.py:49
  22.2 5.4 %collective-permute-start.12 = (f32[2,32,640]{2,1,0:T(8,128)S(1)}, f32[2,32,640]{2,1,0:T(8,128)S(1)}, u32[]{:S(2)}, u32[]{:S(2)}) collective-permute-start(f32[2,32,640]{2,1,0:T(8,128)S(1)} %slice.77), channel_id=1, source_target_pairs={{0,8},{1,25},{2,10},{3,27},{4,12},{5,29},{6,14},{7,31},{8,0},{9,17... | collective-permute-start | bytes 491528 | tf_op jit(solution)/shard_map/ppermute | solution.py:49
  24.3 5.4 %collective-permute-start.2 = (f32[2,32,640]{2,1,0:T(8,128)S(1)}, f32[2,32,640]{2,1,0:T(8,128)S(1)}, u32[]{:S(2)}, u32[]{:S(2)}) collective-permute-start(f32[2,32,640]{2,1,0:T(8,128)S(1)} %slice.71), channel_id=1, source_target_pairs={{0,32},{1,97},{2,34},{3,99},{4,36},{5,101},{6,38},{7,103},{8,40},{... | collective-permute-start | bytes 491528 | tf_op jit(solution)/shard_map/ppermute | solution.py:49
  27.7 4.5 %collective-permute-start.13 = (f32[1,32,640]{2,1,0:T(8,128)S(1)}, f32[1,32,640]{2,1,0:T(8,128)S(1)}, u32[]{:S(2)}, u32[]{:S(2)}) collective-permute-start(f32[1,32,640]{2,1,0:T(8,128)S(1)} %slice.79), channel_id=1, source_target_pairs={{0,2},{1,7},{2,0},{3,5},{4,6},{5,3},{6,4},{7,1},{8,10},{9,15},{10,... | collective-permute-start | bytes 245768 | tf_op jit(solution)/shard_map/ppermute | solution.py:49
  29.7 4.8 %collective-permute-start.3 = (f32[1,32,640]{2,1,0:T(8,128)S(1)}, f32[1,32,640]{2,1,0:T(8,128)S(1)}, u32[]{:S(2)}, u32[]{:S(2)}) collective-permute-start(f32[1,32,640]{2,1,0:T(8,128)S(1)} %slice.73), channel_id=1, source_target_pairs={{0,8},{1,25},{2,10},{3,27},{4,12},{5,29},{6,14},{7,31},{8,0},{9,17... | collective-permute-start | bytes 245768 | tf_op jit(solution)/shard_map/ppermute | solution.py:49
  32.2 5.7 %collective-permute-start.14 = (f32[1,32,640]{2,1,0:T(8,128)S(1)}, f32[1,32,640]{2,1,0:T(8,128)S(1)}, u32[]{:S(2)}, u32[]{:S(2)}) collective-permute-start(f32[1,32,640]{2,1,0:T(8,128)S(1)} %slice_add_fusion.2), channel_id=1, source_target_pairs={{0,96},{1,33},{2,98},{3,35},{4,100},{5,37},{6,102},{7,39},{8,104},... | collective-permute-start | bytes 245768 | tf_op jit(solution)/shard_map/ppermute | solution.py:49
  34.5 7.6 %collective-permute-start.4 = (f32[1,32,640]{2,1,0:T(8,128)S(1)}, f32[1,32,640]{2,1,0:T(8,128)S(1)}, u32[]{:S(2)}, u32[]{:S(2)}) collective-permute-start(f32[1,32,640]{2,1,0:T(8,128)S(1)} %slice_add_fusion.3), channel_id=1, source_target_pairs={{0,6},{1,3},{2,4},{3,1},{4,2},{5,7},{6,0},{7,5},{8,14},{9,11},{10,... | collective-permute-start | bytes 245768 | tf_op jit(solution)/shard_map/ppermute | solution.py:49
  38.0 6.5 %collective-permute-start.15 = (f32[1,32,640]{2,1,0:T(8,128)S(1)}, f32[1,32,640]{2,1,0:T(8,128)S(1)}, u32[]{:S(2)}, u32[]{:S(2)}) collective-permute-start(f32[1,32,640]{2,1,0:T(8,128)S(1)} %add.61), channel_id=1, source_target_pairs={{0,24},{1,9},{2,26},{3,11},{4,28},{5,13},{6,30},{7,15},{8,16},{9,1... | collective-permute-start | bytes 245768 | tf_op jit(solution)/shard_map/ppermute | solution.py:49
  42.1 5.7 %collective-permute-start.5 = (f32[1,32,640]{2,1,0:T(8,128)S(1)}, f32[1,32,640]{2,1,0:T(8,128)S(1)}, u32[]{:S(2)}, u32[]{:S(2)}) collective-permute-start(f32[1,32,640]{2,1,0:T(8,128)S(1)} %add.55), channel_id=1, source_target_pairs={{0,96},{1,33},{2,98},{3,35},{4,100},{5,37},{6,102},{7,39},{8,104},... | collective-permute-start | bytes 245768 | tf_op jit(solution)/shard_map/ppermute | solution.py:49
  44.5 6.2 %collective-permute-start.16 = (f32[1,32,640]{2,1,0:T(8,128)S(1)}, f32[1,32,640]{2,1,0:T(8,128)S(1)}, u32[]{:S(2)}, u32[]{:S(2)}) collective-permute-start(f32[1,32,640]{2,1,0:T(8,128)S(1)} %add.62), channel_id=1, source_target_pairs={{0,6},{1,3},{2,4},{3,1},{4,2},{5,7},{6,0},{7,5},{8,14},{9,11},{10,... | collective-permute-start | bytes 245768 | tf_op jit(solution)/shard_map/ppermute | solution.py:49
  47.9 6.1 %collective-permute-start.6 = (f32[1,32,640]{2,1,0:T(8,128)S(1)}, f32[1,32,640]{2,1,0:T(8,128)S(1)}, u32[]{:S(2)}, u32[]{:S(2)}) collective-permute-start(f32[1,32,640]{2,1,0:T(8,128)S(1)} %add.56), channel_id=1, source_target_pairs={{0,24},{1,9},{2,26},{3,11},{4,28},{5,13},{6,30},{7,15},{8,16},{9,1... | collective-permute-start | bytes 245768 | tf_op jit(solution)/shard_map/ppermute | solution.py:49
  50.7 4.5 %collective-permute-start.17 = (f32[1,32,640]{2,1,0:T(8,128)S(1)}, f32[1,32,640]{2,1,0:T(8,128)S(1)}, u32[]{:S(2)}, u32[]{:S(2)}) collective-permute-start(f32[1,32,640]{2,1,0:T(8,128)S(1)} %add.63), channel_id=1, source_target_pairs={{0,2},{1,7},{2,0},{3,5},{4,6},{5,3},{6,4},{7,1},{8,10},{9,15},{10,... | collective-permute-start | bytes 245768 | tf_op jit(solution)/shard_map/ppermute | solution.py:49
  54.0 4.5 %collective-permute-start.7 = (f32[1,32,640]{2,1,0:T(8,128)S(1)}, f32[1,32,640]{2,1,0:T(8,128)S(1)}, u32[]{:S(2)}, u32[]{:S(2)}) collective-permute-start(f32[1,32,640]{2,1,0:T(8,128)S(1)} %add.57), channel_id=1, source_target_pairs={{0,8},{1,25},{2,10},{3,27},{4,12},{5,29},{6,14},{7,31},{8,0},{9,17... | collective-permute-start | bytes 245768 | tf_op jit(solution)/shard_map/ppermute | solution.py:49
  55.2 5.4 %collective-permute-start.18 = (f32[2,32,640]{2,1,0:T(8,128)S(1)}, f32[2,32,640]{2,1,0:T(8,128)S(1)}, u32[]{:S(2)}, u32[]{:S(2)}) collective-permute-start(f32[2,32,640]{2,1,0:T(8,128)S(1)} %pad_maximum_fusion.3), channel_id=1, source_target_pairs={{0,8},{1,25},{2,10},{3,27},{4,12},{5,29},{6,14},{7,31},{8,0},{9,17... | collective-permute-start | bytes 491528 | tf_op jit(solution)/shard_map/ppermute | solution.py:49
  58.5 5.4 %collective-permute-start.8 = (f32[2,32,640]{2,1,0:T(8,128)S(1)}, f32[2,32,640]{2,1,0:T(8,128)S(1)}, u32[]{:S(2)}, u32[]{:S(2)}) collective-permute-start(f32[2,32,640]{2,1,0:T(8,128)S(1)} %pad_maximum_fusion.2), channel_id=1, source_target_pairs={{0,32},{1,97},{2,34},{3,99},{4,36},{5,101},{6,38},{7,103},{8,40},{... | collective-permute-start | bytes 491528 | tf_op jit(solution)/shard_map/ppermute | solution.py:49
  60.7 6.1 %collective-permute-start.20 = (f32[4,32,640]{2,1,0:T(8,128)S(1)}, f32[4,32,640]{2,1,0:T(8,128)S(1)}, u32[]{:S(2)}, u32[]{:S(2)}) collective-permute-start(f32[4,32,640]{2,1,0:T(8,128)S(1)} %pad_maximum_fusion.1.refs_5_.refs_2_), channel_id=1, source_target_pairs={{0,1},{1,0},{2,3},{3,2},{4,5},{5,4},{6,7},{7,6},{8,9},{9,8},{10,11... | collective-permute-start | bytes 983048 | tf_op jit(solution)/shard_map/ppermute | solution.py:49
  63.9 2.8 %collective-permute-start.9 = (f32[4,32,640]{2,1,0:T(8,128)S(1)}, f32[4,32,640]{2,1,0:T(8,128)S(1)}, u32[]{:S(2)}, u32[]{:S(2)}) collective-permute-start(f32[4,32,640]{2,1,0:T(8,128)S(1)} %pad_maximum_fusion.refs_4_.refs_0_), channel_id=1, source_target_pairs={{0,1},{1,0},{2,3},{3,2},{4,5},{5,4},{6,7},{7,6},{8,9},{9,8},{10,11... | collective-permute-start | bytes 983048 | tf_op jit(solution)/shard_map/ppermute | solution.py:49
  64.0 7.2 %collective-permute-start.19 = (f32[4,32,640]{2,1,0:T(8,128)S(1)}, f32[4,32,640]{2,1,0:T(8,128)S(1)}, u32[]{:S(2)}, u32[]{:S(2)}) collective-permute-start(f32[4,32,640]{2,1,0:T(8,128)S(1)} %pad_maximum_fusion.1.refs_5_.refs_2_), channel_id=1, source_target_pairs={{0,32},{1,97},{2,34},{3,99},{4,36},{5,101},{6,38},{7,103},{8,40},{... | collective-permute-start | bytes 983048 | tf_op jit(solution)/shard_map/ppermute | solution.py:49
  64.1 7.3 %collective-permute-start.10 = (f32[4,32,640]{2,1,0:T(8,128)S(1)}, f32[4,32,640]{2,1,0:T(8,128)S(1)}, u32[]{:S(2)}, u32[]{:S(2)}) collective-permute-start(f32[4,32,640]{2,1,0:T(8,128)S(1)} %pad_maximum_fusion.refs_4_.refs_0_), channel_id=1, source_target_pairs={{0,2},{1,7},{2,0},{3,5},{4,6},{5,3},{6,4},{7,1},{8,10},{9,15},{10,... | collective-permute-start | bytes 983048 | tf_op jit(solution)/shard_map/ppermute | solution.py:49
  71.4 3.6 %collective-permute-start.21 = (f32[4,32,640]{2,1,0:T(8,128)S(1)}, f32[4,32,640]{2,1,0:T(8,128)S(1)}, u32[]{:S(2)}, u32[]{:S(2)}) collective-permute-start(f32[4,32,640]{2,1,0:T(8,128)S(1)} %collective-permute-done.10.refs_4_.refs_1_), channel_id=1, source_target_pairs={{0,1},{1,0},{2,3},{3,2},{4,5},{5,4},{6,7},{7,6},{8,9},{9,8},{10,11... | collective-permute-start | bytes 983048 | tf_op jit(solution)/shard_map/ppermute | solution.py:49
  73.8 1.7 %collective-permute-start.22 = (f32[4,32,640]{2,1,0:T(8,128)S(1)}, f32[4,32,640]{2,1,0:T(8,128)S(1)}, u32[]{:S(2)}, u32[]{:S(2)}) collective-permute-start(f32[4,32,640]{2,1,0:T(8,128)S(1)} %collective-permute-done.19.refs_5_.refs_3_), channel_id=1, source_target_pairs={{0,1},{1,0},{2,3},{3,2},{4,5},{5,4},{6,7},{7,6},{8,9},{9,8},{10,11... | collective-permute-start | bytes 983048 | tf_op jit(solution)/shard_map/ppermute | solution.py:49
  76.7 4.7 %collective-permute-start.23 = (f32[32,768]{1,0:T(8,128)S(1)}, f32[32,768]{1,0:T(8,128)S(1)}, u32[]{:S(2)}, u32[]{:S(2)}) collective-permute-start(f32[32,768]{1,0:T(8,128)S(1)} %get-tuple-element.62), channel_id=1, source_target_pairs={{0,32},{1,9},{2,34},{3,11},{4,36},{5,13},{6,38},{7,15},{8,40},{9,1... | collective-permute-start | bytes 294920 | tf_op jit(solution)/shard_map/ppermute | solution.py:49
  81.5 4.7 %collective-permute-start.24 = (f32[32,768]{1,0:T(8,128)S(1)}, f32[32,768]{1,0:T(8,128)S(1)}, u32[]{:S(2)}, u32[]{:S(2)}) collective-permute-start(f32[32,768]{1,0:T(8,128)S(1)} %add.64), channel_id=1, source_target_pairs={{0,8},{1,33},{2,10},{3,35},{4,12},{5,37},{6,14},{7,39},{8,0},{9,41... | collective-permute-start | bytes 294920 | tf_op jit(solution)/shard_map/ppermute | solution.py:49
  86.2 5.9 %collective-permute-start.25 = (f32[32,768]{1,0:T(8,128)S(1)}, f32[32,768]{1,0:T(8,128)S(1)}, u32[]{:S(2)}, u32[]{:S(2)}) collective-permute-start(f32[32,768]{1,0:T(8,128)S(1)} %add.65), channel_id=1, source_target_pairs={{0,96},{1,25},{2,98},{3,27},{4,100},{5,29},{6,102},{7,31},{8,104},... | collective-permute-start | bytes 294920 | tf_op jit(solution)/shard_map/ppermute | solution.py:49
  92.1 6.1 %collective-permute-start.26 = (f32[32,768]{1,0:T(8,128)S(1)}, f32[32,768]{1,0:T(8,128)S(1)}, u32[]{:S(2)}, u32[]{:S(2)}) collective-permute-start(f32[32,768]{1,0:T(8,128)S(1)} %add.66), channel_id=1, source_target_pairs={{0,24},{1,97},{2,26},{3,99},{4,28},{5,101},{6,30},{7,103},{8,16},{... | collective-permute-start | bytes 294920 | tf_op jit(solution)/shard_map/ppermute | solution.py:49

commit v4 on v3

v4 whole, which is shorter than its diff:
```python
import functools

import jax
import jax.numpy as jnp
from jax import lax
from jax.experimental import pallas as pl
from jax.experimental.pallas import tpu as pltpu
from jax.sharding import PartitionSpec as P

F32, BF16 = jnp.float32, jnp.bfloat16
ROWS, COLS = 8192, 128
OROWS, OCOLS = 4096, 512
RANK = 32
REPLICAS = 16
STEPS = 3
PARTS = 1 << STEPS
GROUP = PARTS // 2
CH = ROWS // (2 * PARTS)
OCH = OROWS // (4 * PARTS)
WIDE = CH + OCH
MIB = 1 << 20

X, Y, Z = 0, 1, 2


def other_turn(steps):
    return [(axis, 1 - turn) for axis, turn in steps]


FIRST = [(X, 0), (Y, 0), (Z, 0), (X, 1), (Y, 1), (Z, 1)]
SECOND = [(Y, 0), (Z, 0), (X, 0), (Y, 1), (Z, 1), (X, 1)]
CHAINS = ((FIRST, other_turn(FIRST)), (SECOND, other_turn(SECOND)))
RIGHT = ([(Y, 0), (Z, 0), (Y, 1), (Z, 1)], [(Z, 0), (Y, 0), (Z, 1), (Y, 1)])


def pairs(steps, k):
    out = []
    for i in range(128):
        q, core = [(i // 2) % 4, i // 32, (i // 8) % 4], i % 2
        axis, turn = steps[core][k]
        q[axis] ^= 3 if turn else 1
        out.append((i, ((q[1] * 4 + q[2]) * 4 + q[0]) * 2 + core))
    return out


CORES = [(i, i ^ 1) for i in range(128)]


def send(x, to):
    return lax.ppermute(x, ("dp", "mp"), to)


def group_of(chain, dh, d1):
    dp, mp = lax.axis_index("dp"), lax.axis_index("mp")
    q = (lax.div(mp, 2), lax.div(dp, 4), lax.rem(dp, 4))
    half = jnp.bitwise_xor(lax.rem(mp, 2), dh)

    def own(step):
        axis, turn = step
        high, low = lax.div(q[axis], 2), lax.rem(q[axis], 2)
        return high if turn else jnp.bitwise_xor(high, low)

    bits = [(1 - half) * own(CHAINS[chain][0][k]) + half * own(CHAINS[chain][1][k]) for k in range(STEPS)]
    return (2 * half + jnp.bitwise_xor(bits[0], d1)) * GROUP, 2 * bits[1] + bits[2]


def group_rows(chain, first):
    rows = pl.ds(pl.multiple_of(first * CH, CH), GROUP * CH)
    orows = pl.ds(pl.multiple_of(chain * (OROWS // 2) + first * OCH, OCH), GROUP * OCH)
    return rows, orows


def dot_nt(a, b):
    return lax.dot_general(a, b, (((1,), (1,)), ((), ())), preferred_element_type=F32)


def dot(a, b):
    return jnp.dot(a, b, preferred_element_type=F32)


def split2(a):
    high = a.astype(BF16)
    return high, (a - high.astype(F32)).astype(BF16)


def split3(a):
    high = a.astype(BF16)
    rest = a - high.astype(F32)
    mid = rest.astype(BF16)
    return high, mid, (rest - mid.astype(F32)).astype(BF16)


HBM = pl.BlockSpec(memory_space=pltpu.HBM)
VM = pl.BlockSpec(memory_space=pltpu.VMEM)


def cost(us):
    return pl.CostEstimate(flops=0, bytes_accessed=int(us * 3_000_000), transcendentals=0)


def loads(refs, bufs, sems, dh, d1):
    copies = []
    for chain in range(2):
        rows, orows = group_rows(chain, group_of(chain, dh, d1)[0])
        gkv, ekv, gout, eout = refs
        sources = (gkv.at[0, chain, rows, :], ekv.at[0, chain, rows, :], gout.at[0, orows, :], eout.at[0, orows, :])
        for n, (src, dst) in enumerate(zip(sources, bufs)):
            copies.append(pltpu.make_async_copy(src, dst.at[chain], sems.at[chain, n]))
    return copies


def part_kernel(here, then, *refs):
    refs = list(refs)
    take = lambda n: [refs.pop(0) for _ in range(n)]
    hbm, basis = take(4), take(2)
    loaded = here[2]
    bufs = take(4) if loaded else None
    refs = refs[here[3] :]
    outs = take(2)
    bufs = bufs or take(4)
    later = take(4) if then else None
    sems = refs[-1]
    now = [] if loaded else loads(hbm, bufs, sems.at[0], *here[:2])
    after = loads(hbm, later, sems.at[1], *then) if then else []
    if not loaded:
        split_kv, split_out, bkv, bout, bsems = refs[:5]
        first = [
            pltpu.make_async_copy(basis[0], bkv, bsems.at[0]),
            pltpu.make_async_copy(basis[1], bout, bsems.at[1]),
        ]
        for copy in first + now:
            copy.start()
        for copy in first:
            copy.wait()
        for a in range(2):
            b = jnp.concatenate(split3(bkv[a]), axis=0)
            split_kv[a] = jnp.concatenate([b, b], axis=1)
        split_out[...] = jnp.concatenate(split3(bout[...]), axis=0)
        basis = (split_kv, split_out)
    else:
        for copy in after:
            copy.start()
    kv = [basis[0][a] for a in range(2)]
    ob = basis[1][...]

    def fold(r):
        return r[:RANK] + (r[RANK : 2 * RANK] + r[2 * RANK :])

    bgkv, bekv, bgout, beout = bufs
    for chain in range(2):
        if now:
            for copy in now[4 * chain : 4 * chain + 4]:
                copy.wait()
            for copy in after[4 * chain : 4 * chain + 4]:
                copy.start()
        out = outs[chain]
        _, name = group_of(chain, *here[:2])
        for j in range(GROUP):
            rows, orows = slice(j * CH, (j + 1) * CH), slice(j * OCH, (j + 1) * OCH)
            both = jnp.concatenate([bgkv[chain, rows], bekv[chain, rows]], axis=1)
            i = jnp.bitwise_xor(name, j)
            out[i, :, :CH] = fold(dot_nt(kv[chain], both))
            out[i, :, CH:] = fold(dot_nt(ob, bgout[chain, orows]) + dot_nt(ob, beout[chain, orows]))
    for copy in after:
        copy.wait()


def part(here, then, args, basis, bufs=(), after=()):
    lead = jax.ShapeDtypeStruct((GROUP, RANK, WIDE), F32)
    kv = jax.ShapeDtypeStruct((2, GROUP * CH, COLS), BF16)
    out = jax.ShapeDtypeStruct((2, GROUP * OCH, OCOLS), BF16)
    n = (not bufs) + (then is not None)
    split = (jax.ShapeDtypeStruct((2, 3 * RANK, 2 * COLS), BF16), jax.ShapeDtypeStruct((3 * RANK, OCOLS), BF16))
    scratch = [pltpu.VMEM((2, RANK, COLS), F32), pltpu.VMEM((RANK, OCOLS), F32), pltpu.SemaphoreType.DMA((2,))]
    result = pl.pallas_call(
        functools.partial(part_kernel, (*here, bool(bufs), len(after)), then),
        out_shape=(lead, lead) + (kv, kv, out, out) * n + (() if bufs else split),
        in_specs=[HBM] * 4 + [VM if bufs else HBM] * 2 + [VM] * (len(bufs) + len(after)),
        out_specs=(VM,) * (2 + 4 * n + 2 * (not bufs)),
        scratch_shapes=([] if bufs else scratch) + [pltpu.SemaphoreType.DMA((2, 2, 4))],
        compiler_params=pltpu.CompilerParams(vmem_limit_bytes=14 * MIB),
        cost_estimate=cost(PART_US),
        name="part",
    )(*args, *basis, *bufs, *after)
    return result[:2], *[result[2 + 4 * i : 6 + 4 * i] for i in range(n)], *([] if bufs else [result[-2:]])


PART_US = 3


def tree(items):
    while len(items) > 1:
        items = [a + b for a, b in zip(items[::2], items[1::2])]
    return items[0]


def right_kernel(dh, d1, n_before, *refs):
    bgkv, bekv, bgout, beout, lead_a, lead_b = refs[:6]
    before = refs[6 : 6 + n_before]
    right, gram = refs[6 + n_before :]

    def fold(r):
        return r[:RANK] + r[RANK:]

    def square(parts):
        g = dot_nt(jnp.concatenate(parts, axis=0), jnp.concatenate(parts, axis=0))

        def at(i, j):
            return g[i * RANK : (i + 1) * RANK, j * RANK : (j + 1) * RANK]

        return at(0, 0) + ((at(0, 1) + at(1, 0)) + ((at(0, 2) + at(2, 0)) + at(1, 1)))

    sums = [0.0, 0.0, 0.0]
    grams = [[], [], [], []]
    for k, x in enumerate((lead_a, lead_b)):
        _, name = group_of(k, dh, d1)
        for j in range(GROUP):
            parts = split3(x[jnp.bitwise_xor(name, j)])
            kv, o = [p[:, :CH] for p in parts], [p[:, CH:] for p in parts]
            grams[k].append(square(kv))
            grams[2 + k].append(square(o))
            rows, orows = slice(j * CH, (j + 1) * CH), slice(j * OCH, (j + 1) * OCH)
            both = jnp.concatenate([bgkv[k, rows], bekv[k, rows]], axis=1)
            r = fold(dot(jnp.concatenate(kv[:2], axis=0), both))
            sums[k] += r[:, :COLS] + r[:, COLS:]
            two = jnp.concatenate(o[:2], axis=0)
            sums[2] += fold(dot(two, bgout[k, orows]) + dot(two, beout[k, orows]))
    for k in range(4):
        gram[k] = tree(grams[k])
    sums = jnp.concatenate(sums, axis=1)
    for other in before:
        sums += other[...]
    right[...] = sums


def right_part(dh, d1, bufs, lead, before=()):
    return pl.pallas_call(
        functools.partial(right_kernel, dh, d1, len(before)),
        out_shape=(
            jax.ShapeDtypeStruct((RANK, 2 * COLS + OCOLS), F32),
            jax.ShapeDtypeStruct((4, RANK, RANK), F32),
        ),
        in_specs=[VM] * (6 + len(before)),
        out_specs=(VM, VM),
        compiler_params=pltpu.CompilerParams(vmem_limit_bytes=20 * MIB),
        cost_estimate=cost(2),
        name="right",
    )(*bufs, *lead, *before)


def factor_kernel(g0, g1, g2, g3, out):
    row = lax.broadcasted_iota(jnp.int32, (RANK, 2 * RANK), 0)
    col = lax.broadcasted_iota(jnp.int32, (RANK, 2 * RANK), 1)
    eye = jnp.where(col == row + RANK, 1.0, 0.0).astype(F32)
    gram = [(g0[k] + g1[k]) + (g2[k] + g3[k]) for k in range(4)]
    gram[2] += gram[3]
    wide = [jnp.concatenate([gram[k], jnp.zeros((RANK, RANK), F32)], axis=1) + eye for k in range(3)]
    scale = [jnp.zeros((RANK, 1), F32)] * 3
    below = lax.broadcasted_iota(jnp.int32, (RANK, 1), 0)
    for i in range(RANK):
        for k in range(3):
            pivot = wide[k][i : i + 1, :]
            d = wide[k][i : i + 1, i : i + 1]
            scale[k] = jnp.where(below == i, lax.rsqrt(d), scale[k])
            factor = jnp.where(below > i, wide[k][:, i : i + 1] / d, 0.0)
            wide[k] = wide[k] - factor * pivot
    for k in range(3):
        out[k] = wide[k][:, RANK:] * scale[k]


def factor(grams):
    return pl.pallas_call(
        factor_kernel,
        out_shape=jax.ShapeDtypeStruct((3, RANK, RANK), F32),
        in_specs=[VM] * 4,
        out_specs=VM,
        compiler_params=pltpu.CompilerParams(vmem_limit_bytes=4 * MIB),
        cost_estimate=cost(4),
        name="factor",
    )(*grams)


def left_kernel(dh, *refs):
    a_own, a_got, b_own, b_got, w = refs[:5]
    left_kv, left_out, ortho, bkv, bout, sems = refs[-6:]
    weights = []
    for k in range(3):
        w1, w2, w3 = split3(w[k])
        weights.append(jnp.concatenate([w1, w1, w2, w1, w2, w3], axis=1))

    def apply(k, x):
        l1, l2, l3 = split3(x)
        return dot(weights[k], jnp.concatenate([l1, l2, l1, l3, l2, l1], axis=0))

    def packed(o):
        high = o.astype(BF16).astype(F32)
        rest = o - high
        return jnp.transpose(jnp.concatenate([high, rest, high, jnp.zeros_like(o)], axis=0)).astype(BF16)

    copies = []
    for d1 in range(2):
        for s, lead in enumerate(((a_own, a_got)[d1], (b_own, b_got)[d1])):
            first, name = group_of(s, dh, d1)
            for j in range(GROUP):
                x = lead[jnp.bitwise_xor(name, j)]
                o_kv = apply(s, x[:, :CH])
                o_out = apply(2, x[:, CH:])
                bkv[d1, s, :, j * CH : (j + 1) * CH] = o_kv * (ROWS**0.5)
                bout[d1, s, :, j * OCH : (j + 1) * OCH] = o_out * (OROWS**0.5)
                ortho[d1, s, j, :CH] = packed(o_kv)
                ortho[d1, s, j, CH:] = packed(o_out)
            rows, orows = group_rows(s, first)
            copies.append(pltpu.make_async_copy(bkv.at[d1, s], left_kv.at[s, :, rows], sems.at[d1, s, 0]))
            copies.append(pltpu.make_async_copy(bout.at[d1, s], left_out.at[:, orows], sems.at[d1, s, 1]))
            copies[-2].start()
            copies[-1].start()
    for copy in copies:
        copy.wait()


def left_part(dh, lead, w, before=()):
    return pl.pallas_call(
        functools.partial(left_kernel, dh),
        out_shape=(
            jax.ShapeDtypeStruct((2, RANK, ROWS), F32),
            jax.ShapeDtypeStruct((RANK, OROWS), F32),
            jax.ShapeDtypeStruct((2, 2, GROUP, WIDE, 128), BF16),
        ),
        in_specs=[VM] * 5 + [HBM] * len(before),
        out_specs=(HBM, HBM, VM),
        scratch_shapes=[
            pltpu.VMEM((2, 2, RANK, GROUP * CH), F32),
            pltpu.VMEM((2, 2, RANK, GROUP * OCH), F32),
            pltpu.SemaphoreType.DMA((2, 2, 2)),
        ],
        input_output_aliases={5: 0, 6: 1} if before else {},
        compiler_params=pltpu.CompilerParams(vmem_limit_bytes=16 * MIB),
        cost_estimate=cost(2),
        name="left",
    )(*lead, w, *before)


def error_kernel(*refs):
    total, w, ortho = refs[16], refs[17], refs[18:20]
    right_kv, right_out, new_kv, new_out, nkv, nout, nsems = refs[20:]
    packed = []
    for k, (at, n) in enumerate(((0, COLS), (COLS, COLS), (2 * COLS, OCOLS))):
        w1, w2, w3 = split3(w[k])
        r1, r2, r3 = split3(total[:, at : at + n] * (1.0 / REPLICAS))
        right = dot(
            jnp.concatenate([w1, w1, w2, w1, w2, w3], axis=1),
            jnp.concatenate([r1, r2, r1, r3, r2, r1], axis=0),
        )
        if k < 2:
            right_kv[k] = right
        else:
            right_out[...] = right
        high, low = split2(right)
        packed.append(jnp.concatenate([high, high, low, jnp.zeros_like(high)], axis=0))
    stores = []
    for g in range(4):
        dh, d1 = g // 2, g % 2
        bgkv, bekv, bgout, beout = refs[4 * g : 4 * g + 4]
        for s in range(2):
            for j in range(GROUP):
                rows, orows = slice(j * CH, (j + 1) * CH), slice(j * OCH, (j + 1) * OCH)
                merged = bgkv[s, rows].astype(F32) + bekv[s, rows].astype(F32)
                nkv[g, s, rows] = (merged - dot(ortho[dh][d1, s, j, :CH], packed[s])).astype(BF16)
                merged = bgout[s, orows].astype(F32) + beout[s, orows].astype(F32)
                nout[g, s, orows] = (merged - dot(ortho[dh][d1, s, j, CH:], packed[2])).astype(BF16)
            rows, orows = group_rows(s, group_of(s, dh, d1)[0])
            stores.append(pltpu.make_async_copy(nkv.at[g, s], new_kv.at[0, s, rows, :], nsems.at[g, s, 0]))
            stores.append(pltpu.make_async_copy(nout.at[g, s], new_out.at[0, orows, :], nsems.at[g, s, 1]))
            stores[-2].start()
            stores[-1].start()
    for copy in stores:
        copy.wait()


def errors(bufs, total, w, ortho):
    return pl.pallas_call(
        error_kernel,
        out_shape=(
            jax.ShapeDtypeStruct((2, RANK, COLS), F32),
            jax.ShapeDtypeStruct((RANK, OCOLS), F32),
            jax.ShapeDtypeStruct((1, 2, ROWS, COLS), BF16),
            jax.ShapeDtypeStruct((1, OROWS, OCOLS), BF16),
        ),
        in_specs=[VM] * 20,
        out_specs=(VM, VM, HBM, HBM),
        scratch_shapes=[
            pltpu.VMEM((4, 2, GROUP * CH, COLS), BF16),
            pltpu.VMEM((4, 2, GROUP * OCH, OCOLS), BF16),
            pltpu.SemaphoreType.DMA((4, 2, 2)),
        ],
        compiler_params=pltpu.CompilerParams(vmem_limit_bytes=24 * MIB),
        cost_estimate=cost(5),
        name="errors",
    )(*bufs, total, w, *ortho)


def on_device(grad_kv, error_kv, grad_out, error_out, basis_kv, basis_out):
    args = (grad_kv, error_kv, grad_out, error_out, jnp.swapaxes(basis_kv, 1, 2), basis_out.T)
    *args, bkv, bout = [pltpu.with_memory_space_constraint(x, pltpu.HBM) for x in args]
    far, bufs_far1, bufs_near1, basis = part((1, 1), (0, 1), args, (bkv, bout))
    far = [send(x, CORES) for x in far]
    near, bufs_far0 = part((0, 1), (1, 0), args, basis, bufs_near1)
    sent = [x + y for x, y in zip(near, far)]
    got = [send(x, pairs(CHAINS[s], 0)) for s, x in enumerate(sent)]
    far, bufs_near0 = part((1, 0), (0, 0), args, basis, bufs_far0, sent)
    far = [send(x, CORES) for x in far]
    (near,) = part((0, 0), None, args, basis, bufs_near0, got[1:])
    both = [(x + y) + z for x, y, z in zip(near, far, got)]

    for k in range(1, 2 * STEPS):
        for s in range(2):
            x = both[s]
            if k < STEPS:
                n = x.shape[0] // 2
                both[s] = x[:n] + send(x[n:], pairs(CHAINS[s], k))
            else:
                both[s] = x + send(x, pairs(CHAINS[s], k))
    for k in reversed(range(1, STEPS)):
        both = [jnp.concatenate([x, send(x, pairs(CHAINS[s], k))]) for s, x in enumerate(both)]
    own0 = both
    own1 = [send(x, pairs(CHAINS[s], 0)) for s, x in enumerate(both)]
    other0 = [send(x, CORES) for x in own0]
    sum1, gram1 = right_part(0, 0, bufs_near0, own0)
    sum2, gram2 = right_part(1, 0, bufs_far0, other0)
    own1, sum1, sum2 = lax.optimization_barrier((own1, sum1, sum2))
    other1 = [send(x, CORES) for x in own1]
    sum3, gram3 = right_part(0, 1, bufs_near1, own1)
    total, gram4 = right_part(1, 1, bufs_far1, other1, (sum1, sum2, sum3))
    own = (own0[0], own1[0], own0[1], own1[1])
    other = (other0[0], other1[0], other0[1], other1[1])
    w = factor((gram1, gram3, gram2, gram4))
    total = total + send(total, pairs(RIGHT, 0))
    total, w = lax.optimization_barrier((total, w))
    *left, ortho_own = left_part(0, own, w)
    total = total + send(total, pairs(RIGHT, 1))
    total, left = lax.optimization_barrier((total, left))
    left_kv, left_out, ortho_other = left_part(1, other, w, left)
    total = total + send(total, pairs(RIGHT, 2))
    total, ortho_other = lax.optimization_barrier((total, ortho_other))
    total = total + send(total, pairs(RIGHT, 3))
    right_kv, right_out, new_kv, new_out = errors(
        (*bufs_near0, *bufs_near1, *bufs_far0, *bufs_far1), total, w, (ortho_own, ortho_other)
    )
    return (
        jnp.swapaxes(left_kv, 1, 2),
        left_out.T,
        jnp.swapaxes(right_kv, 1, 2),
        right_out.T,
        new_kv,
        new_out,
    )


def solution(mesh):
    placed = (
        P("dp", None, None, "mp"),
        P("dp", None, None, "mp"),
        P("dp", None, "mp"),
        P("dp", None, "mp"),
        P(None, "mp", None),
        P("mp", None),
    )
    return jax.shard_map(
        on_device,
        mesh=mesh,
        in_specs=placed,
        out_specs=(
            P(),
            P(),
            P(None, "mp", None),
            P("mp", None),
            P("dp", None, None, "mp"),
            P("dp", None, "mp"),
        ),
        check_vma=False,
    )
```

time: 104 us -> 100 us (0.962)
  starting transfers between devices: 36.3 us -> 30.1 us
  waiting for transfers between devices: 36.1 us -> 38.5 us
    ppermute x27 -> x30, starting transfers between devices: 36.3 us -> 30.1 us  [send(): return lax.ppermute(x, ('dp', 'mp'), to)]
    ppermute x27 -> x30, waiting for transfers between devices: 36.1 us -> 38.5 us  [send(): return lax.ppermute(x, ('dp', 'mp'), to)]
    pallas_call x6 -> x8, Pallas kernels: 17.3 us -> 18.6 us  [the longest x4 13.6 us: part(): pl.pallas_call(functools.partial(part_kernel, (*here, bool(bufs), len(aft...]
  transfers between devices with their start and end apart: 27 -> 30, of which waited for: 20 -> 19; matrix products, arithmetic and copies ran while one was open for 0% -> 0% of each run, Pallas kernels for 16% -> 19%
where the time goes in v4:
time: 100 us
  waiting for transfers between devices  38.5 us (38%)
  Pallas kernels  30.1 us (30%)
  starting transfers between devices  30.1 us (30%)
  between operations  1.11 us (1%)
    ppermute x30, waiting for transfers between devices, send(): return lax.ppermute(x, ('dp', 'mp'), to)  38.5 us
    ppermute x30, starting transfers between devices, send(): return lax.ppermute(x, ('dp', 'mp'), to)  30.1 us
    pallas_call x4, Pallas kernels, part(): pl.pallas_call(functools.partial(part_kernel, (*here, bool(bufs), len(aft...  13.6 us
    pallas_call x4, Pallas kernels, right_part(): pl.pallas_call(functools.partial(right_kernel, dh, d1, len(before)), out_...  5.01 us
    pallas_call x1, Pallas kernels, errors(): pl.pallas_call(error_kernel, out_shape=(jax.ShapeDtypeStruct((2, RANK, CO...  4.68 us
    pallas_call x2, Pallas kernels, left_part(): pl.pallas_call(functools.partial(left_kernel, dh), out_shape=(jax.ShapeDt...  3.91 us
    pallas_call x1, Pallas kernels, factor(): pl.pallas_call(factor_kernel, out_shape=jax.ShapeDtypeStruct((3, RANK, RA...  2.87 us
  transfers between devices with their start and end apart: 30, of which 19 were waited for; matrix products, arithmetic and copies ran while one was open for 0% of the time, Pallas kernels for 19%

profile of v4, /device:TPU:0, one launch (start us, length us, event | category | flops | bytes accessed | tf_op | source)
XLA Modules:
  0.0 100.2 jit_solution(3201225443613194735)
XLA Ops:
  0.6 5.2 %part.4 = (f32[4,32,640]{2,1,0:T(8,128)S(1)}, f32[4,32,640]{2,1,0:T(8,128)S(1)}, bf16[2,2048,128]{2,1,0:T(8,128)(2,1)S(1)}, bf16[2,2048,128]{2,1,0:T(8,128)(2,1)...) custom-call(bf16[1,2,8192,128]{3,2,1,0:T(8,128)(2,1)} %refs_0_.7, ...), custom_call_target="tpu_custom_call" | custom-call | bytes 9000000 | tf_op jit(solution)/shard_map/part/pallas_call | solution.py:175
  5.8 0.1 collective-permute-start.1
  5.9 0.5 collective-permute-start
  6.4 3.5 %part.5 = (f32[4,32,640]{2,1,0:T(8,128)S(1)}, f32[4,32,640]{2,1,0:T(8,128)S(1)}, bf16[2,2048,128]{2,1,0:T(8,128)(2,1)S(1)}, bf16[2,2048,128]{2,1,0:T(8,128)(2,1)...) custom-call(bf16[1,2,8192,128]{3,2,1,0:T(8,128)(2,1)} %refs_0_.7, ...), custom_call_target="tpu_custom_call" | custom-call | bytes 9000000 | tf_op jit(solution)/shard_map/part/pallas_call | solution.py:175
  10.0 1.7 %collective-permute-start.2 = (f32[4,32,640]{2,1,0:T(8,128)S(1)}, f32[4,32,640]{2,1,0:T(8,128)S(1)}, u32[]{:S(2)}, u32[]{:S(2)}) collective-permute-start(f32[4,32,640]{2,1,0:T(8,128)S(1)} %add.61.refs_11_), channel_id=1, source_target_pairs={{0,32},{1,97},{2,34},{3,99},{4,36},{5,101},{6,38},{7,103},{8,40},{... | collective-permute-start | bytes 983048 | tf_op jit(solution)/shard_map/ppermute | solution.py:50
  11.8 1.6 %collective-permute-start.4 = (f32[4,32,640]{2,1,0:T(8,128)S(1)}, f32[4,32,640]{2,1,0:T(8,128)S(1)}, u32[]{:S(2)}, u32[]{:S(2)}) collective-permute-start(f32[4,32,640]{2,1,0:T(8,128)S(1)} %add.60.refs_10_), channel_id=1, source_target_pairs={{0,2},{1,7},{2,0},{3,5},{4,6},{5,3},{6,4},{7,1},{8,10},{9,15},{10,... | collective-permute-start | bytes 983048 | tf_op jit(solution)/shard_map/ppermute | solution.py:50
  13.3 3.5 %part.6 = (f32[4,32,640]{2,1,0:T(8,128)S(1)}, f32[4,32,640]{2,1,0:T(8,128)S(1)}, bf16[2,2048,128]{2,1,0:T(8,128)(2,1)S(1)}, bf16[2,2048,128]{2,1,0:T(8,128)(2,1)...) custom-call(bf16[1,2,8192,128]{3,2,1,0:T(8,128)(2,1)} %refs_0_.7, ...), custom_call_target="tpu_custom_call" | custom-call | bytes 9000000 | tf_op jit(solution)/shard_map/part/pallas_call | solution.py:175
  16.8 2.3 %collective-permute-start.3 = (f32[4,32,640]{2,1,0:T(8,128)S(1)}, f32[4,32,640]{2,1,0:T(8,128)S(1)}, u32[]{:S(2)}, u32[]{:S(2)}) collective-permute-start(f32[4,32,640]{2,1,0:T(8,128)S(1)} %get-tuple-element.80), channel_id=1, source_target_pairs={{0,1},{1,0},{2,3},{3,2},{4,5},{5,4},{6,7},{7,6},{8,9},{9,8},{10,11... | collective-permute-start | bytes 983048 | tf_op jit(solution)/shard_map/ppermute | solution.py:50
  19.1 0.1 collective-permute-start.14
  19.2 1.5 %part.7 = (f32[4,32,640]{2,1,0:T(8,128)S(1)}, f32[4,32,640]{2,1,0:T(8,128)S(1)}) custom-call(bf16[1,2,8192,128]{3,2,1,0:T(8,128)(2,1)} %refs_0_.7, bf16[1,2,8192,128]{3,2,1,0:T(8,128)(2,1)} %refs_1_.7, bf16[1,4096,512]{2,1,0:T(8,128)(2,1)} %refs_2_.7, bf16[1,4096,512]{2,1,0:T(8,128)(2,1)} %refs_3_.7, bf16[2,96,256]{2,1,0:T(8,128)(2,1)S(1)} %get-tuple-element.61.refs_4_, ...), custom_call_target="tpu_custom_call" | custom-call | bytes 9000000 | tf_op jit(solution)/shard_map/part/pallas_call | solution.py:175
  20.7 0.1 add_add_fusion.1
  20.8 0.2 collective-permute-start.5
  21.0 0.1 add_add_fusion
  21.1 2.0 %collective-permute-start.15 = (f32[2,32,640]{2,1,0:T(8,128)S(1)}, f32[2,32,640]{2,1,0:T(8,128)S(1)}, u32[]{:S(2)}, u32[]{:S(2)}) collective-permute-start(f32[2,32,640]{2,1,0:T(8,128)S(1)} %slice.37), channel_id=1, source_target_pairs={{0,8},{1,25},{2,10},{3,27},{4,12},{5,29},{6,14},{7,31},{8,0},{9,17... | collective-permute-start | bytes 491528 | tf_op jit(solution)/shard_map/ppermute | solution.py:50
  23.1 3.1 %collective-permute-done.5 = f32[2,32,640]{2,1,0:T(8,128)S(1)} collective-permute-done((f32[2,32,640]{2,1,0:T(8,128)S(1)}, f32[2,32,640]{2,1,0:T(8,128)S(1)}, u32[]{:S(2)}, u32[]{:S(2)}) %collective-permute-start.5) | collective-permute-done | bytes 163872 | tf_op jit(solution)/shard_map/ppermute | solution.py:50
  26.3 2.0 %collective-permute-start.6 = (f32[1,32,640]{2,1,0:T(8,128)S(1)}, f32[1,32,640]{2,1,0:T(8,128)S(1)}, u32[]{:S(2)}, u32[]{:S(2)}) collective-permute-start(f32[1,32,640]{2,1,0:T(8,128)S(1)} %slice.35), channel_id=1, source_target_pairs={{0,8},{1,25},{2,10},{3,27},{4,12},{5,29},{6,14},{7,31},{8,0},{9,17... | collective-permute-start | bytes 245768 | tf_op jit(solution)/shard_map/ppermute | solution.py:50
  28.3 0.3 collective-permute-start.16
  28.6 2.2 %collective-permute-done.6 = f32[1,32,640]{2,1,0:T(8,128)S(1)} collective-permute-done((f32[1,32,640]{2,1,0:T(8,128)S(1)}, f32[1,32,640]{2,1,0:T(8,128)S(1)}, u32[]{:S(2)}, u32[]{:S(2)}) %collective-permute-start.6) | collective-permute-done | bytes 81952 | tf_op jit(solution)/shard_map/ppermute | solution.py:50
  30.8 1.0 %collective-permute-start.7 = (f32[1,32,640]{2,1,0:T(8,128)S(1)}, f32[1,32,640]{2,1,0:T(8,128)S(1)}, u32[]{:S(2)}, u32[]{:S(2)}) collective-permute-start(f32[1,32,640]{2,1,0:T(8,128)S(1)} %slice_add_fusion.3), channel_id=1, source_target_pairs={{0,6},{1,3},{2,4},{3,1},{4,2},{5,7},{6,0},{7,5},{8,14},{9,11},{10,... | collective-permute-start | bytes 245768 | tf_op jit(solution)/shard_map/ppermute | solution.py:50
  31.8 1.0 %collective-permute-done.16 = f32[1,32,640]{2,1,0:T(8,128)S(1)} collective-permute-done((f32[1,32,640]{2,1,0:T(8,128)S(1)}, f32[1,32,640]{2,1,0:T(8,128)S(1)}, u32[]{:S(2)}, u32[]{:S(2)}) %collective-permute-start.16) | collective-permute-done | bytes 81952 | tf_op jit(solution)/shard_map/ppermute | solution.py:50
  32.8 1.9 %collective-permute-start.17 = (f32[1,32,640]{2,1,0:T(8,128)S(1)}, f32[1,32,640]{2,1,0:T(8,128)S(1)}, u32[]{:S(2)}, u32[]{:S(2)}) collective-permute-start(f32[1,32,640]{2,1,0:T(8,128)S(1)} %slice_add_fusion.2), channel_id=1, source_target_pairs={{0,96},{1,33},{2,98},{3,35},{4,100},{5,37},{6,102},{7,39},{8,104},... | collective-permute-start | bytes 245768 | tf_op jit(solution)/shard_map/ppermute | solution.py:50
  34.7 1.8 %collective-permute-done.7 = f32[1,32,640]{2,1,0:T(8,128)S(1)} collective-permute-done((f32[1,32,640]{2,1,0:T(8,128)S(1)}, f32[1,32,640]{2,1,0:T(8,128)S(1)}, u32[]{:S(2)}, u32[]{:S(2)}) %collective-permute-start.7) | collective-permute-done | bytes 81952 | tf_op jit(solution)/shard_map/ppermute | solution.py:50
  36.5 1.1 %collective-permute-start.8 = (f32[1,32,640]{2,1,0:T(8,128)S(1)}, f32[1,32,640]{2,1,0:T(8,128)S(1)}, u32[]{:S(2)}, u32[]{:S(2)}) collective-permute-start(f32[1,32,640]{2,1,0:T(8,128)S(1)} %add.66), channel_id=1, source_target_pairs={{0,96},{1,33},{2,98},{3,35},{4,100},{5,37},{6,102},{7,39},{8,104},... | collective-permute-start | bytes 245768 | tf_op jit(solution)/shard_map/ppermute | solution.py:50
  37.6 1.0 collective-permute-done.17
  38.6 3.2 %collective-permute-start.18 = (f32[1,32,640]{2,1,0:T(8,128)S(1)}, f32[1,32,640]{2,1,0:T(8,128)S(1)}, u32[]{:S(2)}, u32[]{:S(2)}) collective-permute-start(f32[1,32,640]{2,1,0:T(8,128)S(1)} %add.73), channel_id=1, source_target_pairs={{0,24},{1,9},{2,26},{3,11},{4,28},{5,13},{6,30},{7,15},{8,16},{9,1... | collective-permute-start | bytes 245768 | tf_op jit(solution)/shard_map/ppermute | solution.py:50
  41.7 0.5 collective-permute-done.8
  42.3 4.1 %collective-permute-start.9 = (f32[1,32,640]{2,1,0:T(8,128)S(1)}, f32[1,32,640]{2,1,0:T(8,128)S(1)}, u32[]{:S(2)}, u32[]{:S(2)}) collective-permute-start(f32[1,32,640]{2,1,0:T(8,128)S(1)} %add.67), channel_id=1, source_target_pairs={{0,24},{1,9},{2,26},{3,11},{4,28},{5,13},{6,30},{7,15},{8,16},{9,1... | collective-permute-start | bytes 245768 | tf_op jit(solution)/shard_map/ppermute | solution.py:50
  46.4 1.0 %collective-permute-start.19 = (f32[1,32,640]{2,1,0:T(8,128)S(1)}, f32[1,32,640]{2,1,0:T(8,128)S(1)}, u32[]{:S(2)}, u32[]{:S(2)}) collective-permute-start(f32[1,32,640]{2,1,0:T(8,128)S(1)} %add.74), channel_id=1, source_target_pairs={{0,6},{1,3},{2,4},{3,1},{4,2},{5,7},{6,0},{7,5},{8,14},{9,11},{10,... | collective-permute-start | bytes 245768 | tf_op jit(solution)/shard_map/ppermute | solution.py:50
  47.5 1.4 %collective-permute-done.9 = f32[1,32,640]{2,1,0:T(8,128)S(1)} collective-permute-done((f32[1,32,640]{2,1,0:T(8,128)S(1)}, f32[1,32,640]{2,1,0:T(8,128)S(1)}, u32[]{:S(2)}, u32[]{:S(2)}) %collective-permute-start.9) | collective-permute-done | bytes 81952 | tf_op jit(solution)/shard_map/ppermute | solution.py:50
  48.8 0.1 collective-permute-start.10
  48.9 3.2 %collective-permute-done.19 = f32[1,32,640]{2,1,0:T(8,128)S(1)} collective-permute-done((f32[1,32,640]{2,1,0:T(8,128)S(1)}, f32[1,32,640]{2,1,0:T(8,128)S(1)}, u32[]{:S(2)}, u32[]{:S(2)}) %collective-permute-start.19) | collective-permute-done | bytes 81952 | tf_op jit(solution)/shard_map/ppermute | solution.py:50
  52.2 0.1 collective-permute-start.20
  52.3 1.1 %collective-permute-done.10 = f32[1,32,640]{2,1,0:T(8,128)S(1)} collective-permute-done((f32[1,32,640]{2,1,0:T(8,128)S(1)}, f32[1,32,640]{2,1,0:T(8,128)S(1)}, u32[]{:S(2)}, u32[]{:S(2)}) %collective-permute-start.10) | collective-permute-done | bytes 81952 | tf_op jit(solution)/shard_map/ppermute | solution.py:50
  53.4 0.1 collective-permute-start.11
  53.5 3.2 %collective-permute-done.20 = f32[1,32,640]{2,1,0:T(8,128)S(1)} collective-permute-done((f32[1,32,640]{2,1,0:T(8,128)S(1)}, f32[1,32,640]{2,1,0:T(8,128)S(1)}, u32[]{:S(2)}, u32[]{:S(2)}) %collective-permute-start.20) | collective-permute-done | bytes 81952 | tf_op jit(solution)/shard_map/ppermute | solution.py:50
  56.7 0.1 collective-permute-start.21
  56.8 2.0 %collective-permute-done.11 = f32[2,32,640]{2,1,0:T(8,128)S(1)} collective-permute-done((f32[2,32,640]{2,1,0:T(8,128)S(1)}, f32[2,32,640]{2,1,0:T(8,128)S(1)}, u32[]{:S(2)}, u32[]{:S(2)}) %collective-permute-start.11) | collective-permute-done | bytes 163872 | tf_op jit(solution)/shard_map/ppermute | solution.py:50
  58.8 0.1 collective-permute-start.12
  58.9 3.2 %collective-permute-done.21 = f32[2,32,640]{2,1,0:T(8,128)S(1)} collective-permute-done((f32[2,32,640]{2,1,0:T(8,128)S(1)}, f32[2,32,640]{2,1,0:T(8,128)S(1)}, u32[]{:S(2)}, u32[]{:S(2)}) %collective-permute-start.21) | collective-permute-done | bytes 163872 | tf_op jit(solution)/shard_map/ppermute | solution.py:50
  62.1 0.1 collective-permute-start.23
  62.2 0.1 collective-permute-start.13
  62.3 0.3 collective-permute-start.22
  62.6 1.3 %right.4 = (f32[32,768]{1,0:T(8,128)S(1)}, f32[4,32,32]{2,1,0:T(8,128)S(1)}) custom-call(bf16[2,2048,128]{2,1,0:T(8,128)(2,1)S(1)} %get-tuple-element.75.refs_6_.refs_0_, bf16[2,2048,128]{2,1,0:T(8,128)(2,1)S(1)} %get-tuple-element.76.refs_7_.refs_1_, bf16[2,512,512]{2,1,0:T(8,128)(2,1)S(1)} %get-tuple-element.77.refs_8_.refs_2_, ...), custom_call_target="tpu_custom_call" | custom-call | bytes 6000000 | tf_op jit(solution)/shard_map/right/pallas_call | solution.py:237
  63.9 1.3 %right.5 = (f32[32,768]{1,0:T(8,128)S(1)}, f32[4,32,32]{2,1,0:T(8,128)S(1)}) custom-call(bf16[2,2048,128]{2,1,0:T(8,128)(2,1)S(1)} %get-tuple-element.67.refs_6_.refs_0_.refs_8_, bf16[2,2048,128]{2,1,0:T(8,128)(2,1)S(1)} %get-tuple-element.68.refs_7_.refs_1_.refs_9_, bf16[2,512,512]{2,1,0:T(8,128)(2,1)S(1)} %get-tuple-element.69.refs_8_.refs_2_.refs_10_, ...), custom_call_target="tpu_custom_call" | custom-call | bytes 6000000 | tf_op jit(solution)/shard_map/right/pallas_call | solution.py:237
  65.1 4.2 %collective-permute-done.13.refs_4_.refs_1_ = f32[4,32,640]{2,1,0:T(8,128)S(1)} collective-permute-done((f32[4,32,640]{2,1,0:T(8,128)S(1)}, f32[4,32,640]{2,1,0:T(8,128)S(1)}, u32[]{:S(2)}, u32[]{:S(2)}) %collective-permute-start.13) | collective-permute-done | bytes 327712 | tf_op jit(solution)/shard_map/ppermute | solution.py:50
  69.4 0.3 collective-permute-done.22.refs_5_.refs_3_
  69.6 1.5 %collective-permute-start.24 = (f32[4,32,640]{2,1,0:T(8,128)S(1)}, f32[4,32,640]{2,1,0:T(8,128)S(1)}, u32[]{:S(2)}, u32[]{:S(2)}) collective-permute-start(f32[4,32,640]{2,1,0:T(8,128)S(1)} %collective-permute-done.13.refs_4_.refs_1_), channel_id=1, source_target_pairs={{0,1},{1,0},{2,3},{3,2},{4,5},{5,4},{6,7},{7,6},{8,9},{9,8},{10,11... | collective-permute-start | bytes 983048 | tf_op jit(solution)/shard_map/ppermute | solution.py:50
  71.2 0.0 collective-permute-start.25
  71.2 1.2 %right.6 = (f32[32,768]{1,0:T(8,128)S(1)}, f32[4,32,32]{2,1,0:T(8,128)S(1)}) custom-call(bf16[2,2048,128]{2,1,0:T(8,128)(2,1)S(1)} %get-tuple-element.63.refs_6_.refs_0_.refs_4_, bf16[2,2048,128]{2,1,0:T(8,128)(2,1)S(1)} %get-tuple-element.64.refs_7_.refs_1_.refs_5_, bf16[2,512,512]{2,1,0:T(8,128)(2,1)S(1)} %get-tuple-element.65.refs_8_.refs_2_.refs_6_, ...), custom_call_target="tpu_custom_call" | custom-call | bytes 6000000 | tf_op jit(solution)/shard_map/right/pallas_call | solution.py:237
  72.4 0.0 collective-permute-done.24.refs_4_.refs_1_
  72.4 0.5 collective-permute-done.25.refs_5_.refs_3_
  72.9 1.3 %right.7 = (f32[32,768]{1,0:T(8,128)S(1)}, f32[4,32,32]{2,1,0:T(8,128)S(1)}) custom-call(bf16[2,2048,128]{2,1,0:T(8,128)(2,1)S(1)} %get-tuple-element.87.refs_0_.refs_12_, bf16[2,2048,128]{2,1,0:T(8,128)(2,1)S(1)} %get-tuple-element.88.refs_1_.refs_13_, bf16[2,512,512]{2,1,0:T(8,128)(2,1)S(1)} %get-tuple-element.89.refs_2_.refs_14_, ...), custom_call_target="tpu_custom_call" | custom-call | bytes 6000000 | tf_op jit(solution)/shard_map/right/pallas_call | solution.py:237
  74.1 0.1 collective-permute-start.26
  74.2 2.9 %factor.1.refs_4_.refs_17_ = f32[3,32,32]{2,1,0:T(8,128)S(1)} custom-call(f32[4,32,32]{2,1,0:T(8,128)S(1)} %get-tuple-element.95.g0, f32[4,32,32]{2,1,0:T(8,128)S(1)} %get-tuple-element.96.g1, f32[4,32,32]{2,1,0:T(8,128)S(1)} %get-tuple-element.97.g2, f32[4,32,32]{2,1,0:T(8,128)S(1)} %get-tuple-element.98.g3), custom_call_target="tpu_custom_call" | custom-call | bytes 12000000 | tf_op jit(solution)/shard_map/factor/pallas_call | solution.py:272
  77.1 1.7 %collective-permute-done.26 = f32[32,768]{1,0:T(8,128)S(1)} collective-permute-done((f32[32,768]{1,0:T(8,128)S(1)}, f32[32,768]{1,0:T(8,128)S(1)}, u32[]{:S(2)}, u32[]{:S(2)}) %collective-permute-start.26) | collective-permute-done | bytes 98336 | tf_op jit(solution)/shard_map/ppermute | solution.py:50
  78.8 0.1 collective-permute-start.27
  78.9 2.0 %left.2 = (f32[2,32,8192]{2,1,0:T(8,128)}, f32[32,4096]{1,0:T(8,128)}, bf16[2,2,4,640,128]{4,3,2,1,0:T(8,128)(2,1)S(1)}) custom-call(f32[4,32,640]{2,1,0:T(8,128)S(1)} %pad_maximum_fusion.refs_4_.refs_0_, f32[4,32,640]{2,1,0:T(8,128)S(1)} %collective-permute-done.13.refs_4_.refs_1_, f32[4,32,640]{2,1,0:T(8,128)S(1)} %pad_maximum_fusion.1.refs_5_.refs_2_, ...), custom_call_target="tpu_custom_call" | custom-call | bytes 6000000 | tf_op jit(solution)/shard_map/left/pallas_call | solution.py:322
  80.9 2.6 %collective-permute-done.27 = f32[32,768]{1,0:T(8,128)S(1)} collective-permute-done((f32[32,768]{1,0:T(8,128)S(1)}, f32[32,768]{1,0:T(8,128)S(1)}, u32[]{:S(2)}, u32[]{:S(2)}) %collective-permute-start.27) | collective-permute-done | bytes 98336 | tf_op jit(solution)/shard_map/ppermute | solution.py:50
  83.6 2.2 %collective-permute-start.28 = (f32[32,768]{1,0:T(8,128)S(1)}, f32[32,768]{1,0:T(8,128)S(1)}, u32[]{:S(2)}, u32[]{:S(2)}) collective-permute-start(f32[32,768]{1,0:T(8,128)S(1)} %add.77), channel_id=1, source_target_pairs={{0,96},{1,25},{2,98},{3,27},{4,100},{5,29},{6,102},{7,31},{8,104},... | collective-permute-start | bytes 294920 | tf_op jit(solution)/shard_map/ppermute | solution.py:50
  85.8 2.0 %left.3 = (f32[2,32,8192]{2,1,0:T(8,128)}, f32[32,4096]{1,0:T(8,128)}, bf16[2,2,4,640,128]{4,3,2,1,0:T(8,128)(2,1)S(1)}) custom-call(f32[4,32,640]{2,1,0:T(8,128)S(1)} %collective-permute-done.12.refs_4_.refs_0_, f32[4,32,640]{2,1,0:T(8,128)S(1)} %collective-permute-done.24.refs_4_.refs_1_, ...), custom_call_target="tpu_custom_call", output_to_operand_aliasing={{0}: (5, {}), {1}: (6, {})} | custom-call | bytes 6000000 | tf_op jit(solution)/shard_map/left/pallas_call | solution.py:322
  87.7 1.7 %collective-permute-done.28 = f32[32,768]{1,0:T(8,128)S(1)} collective-permute-done((f32[32,768]{1,0:T(8,128)S(1)}, f32[32,768]{1,0:T(8,128)S(1)}, u32[]{:S(2)}, u32[]{:S(2)}) %collective-permute-start.28) | collective-permute-done | bytes 98336 | tf_op jit(solution)/shard_map/ppermute | solution.py:50
  89.5 2.2 %collective-permute-start.29 = (f32[32,768]{1,0:T(8,128)S(1)}, f32[32,768]{1,0:T(8,128)S(1)}, u32[]{:S(2)}, u32[]{:S(2)}) collective-permute-start(f32[32,768]{1,0:T(8,128)S(1)} %add.78), channel_id=1, source_target_pairs={{0,24},{1,97},{2,26},{3,99},{4,28},{5,101},{6,30},{7,103},{8,16},{... | collective-permute-start | bytes 294920 | tf_op jit(solution)/shard_map/ppermute | solution.py:50
  91.7 3.7 %collective-permute-done.29 = f32[32,768]{1,0:T(8,128)S(1)} collective-permute-done((f32[32,768]{1,0:T(8,128)S(1)}, f32[32,768]{1,0:T(8,128)S(1)}, u32[]{:S(2)}, u32[]{:S(2)}) %collective-permute-start.29) | collective-permute-done | bytes 98336 | tf_op jit(solution)/shard_map/ppermute | solution.py:50
  95.4 4.7 %errors.1 = (f32[2,32,128]{2,1,0:T(8,128)}, f32[32,512]{1,0:T(8,128)}, bf16[1,2,8192,128]{3,2,1,0:T(8,128)(2,1)}, bf16[1,4096,512]{2,1,0:T(8,128)(2,1)}) custom-call(bf16[2,2048,128]{2,1,0:T(8,128)(2,1)S(1)} %get-tuple-element.75.refs_6_.refs_0_, bf16[2,2048,128]{2,1,0:T(8,128)(2,1)S(1)} %get-tuple-element.76.refs_7_.refs_1_, ...), custom_call_target="tpu_custom_call" | custom-call | bytes 15000000 | tf_op jit(solution)/shard_map/errors/pallas_call | solution.py:381
  (34 shorter events, 0.4 us)
Async XLA Ops:
  5.8 4.1 %collective-permute-start.1 = (f32[4,32,640]{2,1,0:T(8,128)S(1)}, f32[4,32,640]{2,1,0:T(8,128)S(1)}, u32[]{:S(2)}, u32[]{:S(2)}) collective-permute-start(f32[4,32,640]{2,1,0:T(8,128)S(1)} %get-tuple-element.74), channel_id=1, source_target_pairs={{0,1},{1,0},{2,3},{3,2},{4,5},{5,4},{6,7},{7,6},{8,9},{9,8},{10,11... | collective-permute-start | bytes 983048 | tf_op jit(solution)/shard_map/ppermute | solution.py:50
  5.9 5.8 %collective-permute-start = (f32[4,32,640]{2,1,0:T(8,128)S(1)}, f32[4,32,640]{2,1,0:T(8,128)S(1)}, u32[]{:S(2)}, u32[]{:S(2)}) collective-permute-start(f32[4,32,640]{2,1,0:T(8,128)S(1)} %get-tuple-element.72), channel_id=1, source_target_pairs={{0,1},{1,0},{2,3},{3,2},{4,5},{5,4},{6,7},{7,6},{8,9},{9,8},{10,11... | collective-permute-start | bytes 983048 | tf_op jit(solution)/shard_map/ppermute | solution.py:50
  10.0 9.3 %collective-permute-start.2 = (f32[4,32,640]{2,1,0:T(8,128)S(1)}, f32[4,32,640]{2,1,0:T(8,128)S(1)}, u32[]{:S(2)}, u32[]{:S(2)}) collective-permute-start(f32[4,32,640]{2,1,0:T(8,128)S(1)} %add.61.refs_11_), channel_id=1, source_target_pairs={{0,32},{1,97},{2,34},{3,99},{4,36},{5,101},{6,38},{7,103},{8,40},{... | collective-permute-start | bytes 983048 | tf_op jit(solution)/shard_map/ppermute | solution.py:50
  11.8 9.0 %collective-permute-start.4 = (f32[4,32,640]{2,1,0:T(8,128)S(1)}, f32[4,32,640]{2,1,0:T(8,128)S(1)}, u32[]{:S(2)}, u32[]{:S(2)}) collective-permute-start(f32[4,32,640]{2,1,0:T(8,128)S(1)} %add.60.refs_10_), channel_id=1, source_target_pairs={{0,2},{1,7},{2,0},{3,5},{4,6},{5,3},{6,4},{7,1},{8,10},{9,15},{10,... | collective-permute-start | bytes 983048 | tf_op jit(solution)/shard_map/ppermute | solution.py:50
  16.8 3.9 %collective-permute-start.3 = (f32[4,32,640]{2,1,0:T(8,128)S(1)}, f32[4,32,640]{2,1,0:T(8,128)S(1)}, u32[]{:S(2)}, u32[]{:S(2)}) collective-permute-start(f32[4,32,640]{2,1,0:T(8,128)S(1)} %get-tuple-element.80), channel_id=1, source_target_pairs={{0,1},{1,0},{2,3},{3,2},{4,5},{5,4},{6,7},{7,6},{8,9},{9,8},{10,11... | collective-permute-start | bytes 983048 | tf_op jit(solution)/shard_map/ppermute | solution.py:50
  19.1 1.9 %collective-permute-start.14 = (f32[4,32,640]{2,1,0:T(8,128)S(1)}, f32[4,32,640]{2,1,0:T(8,128)S(1)}, u32[]{:S(2)}, u32[]{:S(2)}) collective-permute-start(f32[4,32,640]{2,1,0:T(8,128)S(1)} %get-tuple-element.82), channel_id=1, source_target_pairs={{0,1},{1,0},{2,3},{3,2},{4,5},{5,4},{6,7},{7,6},{8,9},{9,8},{10,11... | collective-permute-start | bytes 983048 | tf_op jit(solution)/shard_map/ppermute | solution.py:50
  20.8 5.4 %collective-permute-start.5 = (f32[2,32,640]{2,1,0:T(8,128)S(1)}, f32[2,32,640]{2,1,0:T(8,128)S(1)}, u32[]{:S(2)}, u32[]{:S(2)}) collective-permute-start(f32[2,32,640]{2,1,0:T(8,128)S(1)} %slice.33), channel_id=1, source_target_pairs={{0,32},{1,97},{2,34},{3,99},{4,36},{5,101},{6,38},{7,103},{8,40},{... | collective-permute-start | bytes 491528 | tf_op jit(solution)/shard_map/ppermute | solution.py:50
  21.1 7.1 %collective-permute-start.15 = (f32[2,32,640]{2,1,0:T(8,128)S(1)}, f32[2,32,640]{2,1,0:T(8,128)S(1)}, u32[]{:S(2)}, u32[]{:S(2)}) collective-permute-start(f32[2,32,640]{2,1,0:T(8,128)S(1)} %slice.37), channel_id=1, source_target_pairs={{0,8},{1,25},{2,10},{3,27},{4,12},{5,29},{6,14},{7,31},{8,0},{9,17... | collective-permute-start | bytes 491528 | tf_op jit(solution)/shard_map/ppermute | solution.py:50
  26.3 4.5 %collective-permute-start.6 = (f32[1,32,640]{2,1,0:T(8,128)S(1)}, f32[1,32,640]{2,1,0:T(8,128)S(1)}, u32[]{:S(2)}, u32[]{:S(2)}) collective-permute-start(f32[1,32,640]{2,1,0:T(8,128)S(1)} %slice.35), channel_id=1, source_target_pairs={{0,8},{1,25},{2,10},{3,27},{4,12},{5,29},{6,14},{7,31},{8,0},{9,17... | collective-permute-start | bytes 245768 | tf_op jit(solution)/shard_map/ppermute | solution.py:50
  28.3 4.5 %collective-permute-start.16 = (f32[1,32,640]{2,1,0:T(8,128)S(1)}, f32[1,32,640]{2,1,0:T(8,128)S(1)}, u32[]{:S(2)}, u32[]{:S(2)}) collective-permute-start(f32[1,32,640]{2,1,0:T(8,128)S(1)} %slice.39), channel_id=1, source_target_pairs={{0,2},{1,7},{2,0},{3,5},{4,6},{5,3},{6,4},{7,1},{8,10},{9,15},{10,... | collective-permute-start | bytes 245768 | tf_op jit(solution)/shard_map/ppermute | solution.py:50
  30.8 5.7 %collective-permute-start.7 = (f32[1,32,640]{2,1,0:T(8,128)S(1)}, f32[1,32,640]{2,1,0:T(8,128)S(1)}, u32[]{:S(2)}, u32[]{:S(2)}) collective-permute-start(f32[1,32,640]{2,1,0:T(8,128)S(1)} %slice_add_fusion.3), channel_id=1, source_target_pairs={{0,6},{1,3},{2,4},{3,1},{4,2},{5,7},{6,0},{7,5},{8,14},{9,11},{10,... | collective-permute-start | bytes 245768 | tf_op jit(solution)/shard_map/ppermute | solution.py:50
  32.8 5.7 %collective-permute-start.17 = (f32[1,32,640]{2,1,0:T(8,128)S(1)}, f32[1,32,640]{2,1,0:T(8,128)S(1)}, u32[]{:S(2)}, u32[]{:S(2)}) collective-permute-start(f32[1,32,640]{2,1,0:T(8,128)S(1)} %slice_add_fusion.2), channel_id=1, source_target_pairs={{0,96},{1,33},{2,98},{3,35},{4,100},{5,37},{6,102},{7,39},{8,104},... | collective-permute-start | bytes 245768 | tf_op jit(solution)/shard_map/ppermute | solution.py:50
  36.5 5.7 %collective-permute-start.8 = (f32[1,32,640]{2,1,0:T(8,128)S(1)}, f32[1,32,640]{2,1,0:T(8,128)S(1)}, u32[]{:S(2)}, u32[]{:S(2)}) collective-permute-start(f32[1,32,640]{2,1,0:T(8,128)S(1)} %add.66), channel_id=1, source_target_pairs={{0,96},{1,33},{2,98},{3,35},{4,100},{5,37},{6,102},{7,39},{8,104},... | collective-permute-start | bytes 245768 | tf_op jit(solution)/shard_map/ppermute | solution.py:50
  38.6 7.8 %collective-permute-start.18 = (f32[1,32,640]{2,1,0:T(8,128)S(1)}, f32[1,32,640]{2,1,0:T(8,128)S(1)}, u32[]{:S(2)}, u32[]{:S(2)}) collective-permute-start(f32[1,32,640]{2,1,0:T(8,128)S(1)} %add.73), channel_id=1, source_target_pairs={{0,24},{1,9},{2,26},{3,11},{4,28},{5,13},{6,30},{7,15},{8,16},{9,1... | collective-permute-start | bytes 245768 | tf_op jit(solution)/shard_map/ppermute | solution.py:50
  42.3 6.5 %collective-permute-start.9 = (f32[1,32,640]{2,1,0:T(8,128)S(1)}, f32[1,32,640]{2,1,0:T(8,128)S(1)}, u32[]{:S(2)}, u32[]{:S(2)}) collective-permute-start(f32[1,32,640]{2,1,0:T(8,128)S(1)} %add.67), channel_id=1, source_target_pairs={{0,24},{1,9},{2,26},{3,11},{4,28},{5,13},{6,30},{7,15},{8,16},{9,1... | collective-permute-start | bytes 245768 | tf_op jit(solution)/shard_map/ppermute | solution.py:50
  46.4 5.7 %collective-permute-start.19 = (f32[1,32,640]{2,1,0:T(8,128)S(1)}, f32[1,32,640]{2,1,0:T(8,128)S(1)}, u32[]{:S(2)}, u32[]{:S(2)}) collective-permute-start(f32[1,32,640]{2,1,0:T(8,128)S(1)} %add.74), channel_id=1, source_target_pairs={{0,6},{1,3},{2,4},{3,1},{4,2},{5,7},{6,0},{7,5},{8,14},{9,11},{10,... | collective-permute-start | bytes 245768 | tf_op jit(solution)/shard_map/ppermute | solution.py:50
  48.8 4.5 %collective-permute-start.10 = (f32[1,32,640]{2,1,0:T(8,128)S(1)}, f32[1,32,640]{2,1,0:T(8,128)S(1)}, u32[]{:S(2)}, u32[]{:S(2)}) collective-permute-start(f32[1,32,640]{2,1,0:T(8,128)S(1)} %add.68), channel_id=1, source_target_pairs={{0,8},{1,25},{2,10},{3,27},{4,12},{5,29},{6,14},{7,31},{8,0},{9,17... | collective-permute-start | bytes 245768 | tf_op jit(solution)/shard_map/ppermute | solution.py:50
  52.2 4.5 %collective-permute-start.20 = (f32[1,32,640]{2,1,0:T(8,128)S(1)}, f32[1,32,640]{2,1,0:T(8,128)S(1)}, u32[]{:S(2)}, u32[]{:S(2)}) collective-permute-start(f32[1,32,640]{2,1,0:T(8,128)S(1)} %add.75), channel_id=1, source_target_pairs={{0,2},{1,7},{2,0},{3,5},{4,6},{5,3},{6,4},{7,1},{8,10},{9,15},{10,... | collective-permute-start | bytes 245768 | tf_op jit(solution)/shard_map/ppermute | solution.py:50
  53.4 5.4 %collective-permute-start.11 = (f32[2,32,640]{2,1,0:T(8,128)S(1)}, f32[2,32,640]{2,1,0:T(8,128)S(1)}, u32[]{:S(2)}, u32[]{:S(2)}) collective-permute-start(f32[2,32,640]{2,1,0:T(8,128)S(1)} %pad_maximum_fusion.2), channel_id=1, source_target_pairs={{0,32},{1,97},{2,34},{3,99},{4,36},{5,101},{6,38},{7,103},{8,40},{... | collective-permute-start | bytes 491528 | tf_op jit(solution)/shard_map/ppermute | solution.py:50
  56.7 5.4 %collective-permute-start.21 = (f32[2,32,640]{2,1,0:T(8,128)S(1)}, f32[2,32,640]{2,1,0:T(8,128)S(1)}, u32[]{:S(2)}, u32[]{:S(2)}) collective-permute-start(f32[2,32,640]{2,1,0:T(8,128)S(1)} %pad_maximum_fusion.3), channel_id=1, source_target_pairs={{0,8},{1,25},{2,10},{3,27},{4,12},{5,29},{6,14},{7,31},{8,0},{9,17... | collective-permute-start | bytes 491528 | tf_op jit(solution)/shard_map/ppermute | solution.py:50
  58.8 5.1 %collective-permute-start.12 = (f32[4,32,640]{2,1,0:T(8,128)S(1)}, f32[4,32,640]{2,1,0:T(8,128)S(1)}, u32[]{:S(2)}, u32[]{:S(2)}) collective-permute-start(f32[4,32,640]{2,1,0:T(8,128)S(1)} %pad_maximum_fusion.refs_4_.refs_0_), channel_id=1, source_target_pairs={{0,1},{1,0},{2,3},{3,2},{4,5},{5,4},{6,7},{7,6},{8,9},{9,8},{10,11... | collective-permute-start | bytes 983048 | tf_op jit(solution)/shard_map/ppermute | solution.py:50
  62.1 1.7 %collective-permute-start.23 = (f32[4,32,640]{2,1,0:T(8,128)S(1)}, f32[4,32,640]{2,1,0:T(8,128)S(1)}, u32[]{:S(2)}, u32[]{:S(2)}) collective-permute-start(f32[4,32,640]{2,1,0:T(8,128)S(1)} %pad_maximum_fusion.1.refs_5_.refs_2_), channel_id=1, source_target_pairs={{0,1},{1,0},{2,3},{3,2},{4,5},{5,4},{6,7},{7,6},{8,9},{9,8},{10,11... | collective-permute-start | bytes 983048 | tf_op jit(solution)/shard_map/ppermute | solution.py:50
  62.2 7.2 %collective-permute-start.13 = (f32[4,32,640]{2,1,0:T(8,128)S(1)}, f32[4,32,640]{2,1,0:T(8,128)S(1)}, u32[]{:S(2)}, u32[]{:S(2)}) collective-permute-start(f32[4,32,640]{2,1,0:T(8,128)S(1)} %pad_maximum_fusion.refs_4_.refs_0_), channel_id=1, source_target_pairs={{0,2},{1,7},{2,0},{3,5},{4,6},{5,3},{6,4},{7,1},{8,10},{9,15},{10,... | collective-permute-start | bytes 983048 | tf_op jit(solution)/shard_map/ppermute | solution.py:50
  62.3 7.3 %collective-permute-start.22 = (f32[4,32,640]{2,1,0:T(8,128)S(1)}, f32[4,32,640]{2,1,0:T(8,128)S(1)}, u32[]{:S(2)}, u32[]{:S(2)}) collective-permute-start(f32[4,32,640]{2,1,0:T(8,128)S(1)} %pad_maximum_fusion.1.refs_5_.refs_2_), channel_id=1, source_target_pairs={{0,32},{1,97},{2,34},{3,99},{4,36},{5,101},{6,38},{7,103},{8,40},{... | collective-permute-start | bytes 983048 | tf_op jit(solution)/shard_map/ppermute | solution.py:50
  69.6 2.8 %collective-permute-start.24 = (f32[4,32,640]{2,1,0:T(8,128)S(1)}, f32[4,32,640]{2,1,0:T(8,128)S(1)}, u32[]{:S(2)}, u32[]{:S(2)}) collective-permute-start(f32[4,32,640]{2,1,0:T(8,128)S(1)} %collective-permute-done.13.refs_4_.refs_1_), channel_id=1, source_target_pairs={{0,1},{1,0},{2,3},{3,2},{4,5},{5,4},{6,7},{7,6},{8,9},{9,8},{10,11... | collective-permute-start | bytes 983048 | tf_op jit(solution)/shard_map/ppermute | solution.py:50
  71.2 1.7 %collective-permute-start.25 = (f32[4,32,640]{2,1,0:T(8,128)S(1)}, f32[4,32,640]{2,1,0:T(8,128)S(1)}, u32[]{:S(2)}, u32[]{:S(2)}) collective-permute-start(f32[4,32,640]{2,1,0:T(8,128)S(1)} %collective-permute-done.22.refs_5_.refs_3_), channel_id=1, source_target_pairs={{0,1},{1,0},{2,3},{3,2},{4,5},{5,4},{6,7},{7,6},{8,9},{9,8},{10,11... | collective-permute-start | bytes 983048 | tf_op jit(solution)/shard_map/ppermute | solution.py:50
  74.1 4.7 %collective-permute-start.26 = (f32[32,768]{1,0:T(8,128)S(1)}, f32[32,768]{1,0:T(8,128)S(1)}, u32[]{:S(2)}, u32[]{:S(2)}) collective-permute-start(f32[32,768]{1,0:T(8,128)S(1)} %get-tuple-element.94), channel_id=1, source_target_pairs={{0,32},{1,9},{2,34},{3,11},{4,36},{5,13},{6,38},{7,15},{8,40},{9,1... | collective-permute-start | bytes 294920 | tf_op jit(solution)/shard_map/ppermute | solution.py:50
  78.8 4.7 %collective-permute-start.27 = (f32[32,768]{1,0:T(8,128)S(1)}, f32[32,768]{1,0:T(8,128)S(1)}, u32[]{:S(2)}, u32[]{:S(2)}) collective-permute-start(f32[32,768]{1,0:T(8,128)S(1)} %add.76), channel_id=1, source_target_pairs={{0,8},{1,33},{2,10},{3,35},{4,12},{5,37},{6,14},{7,39},{8,0},{9,41... | collective-permute-start | bytes 294920 | tf_op jit(solution)/shard_map/ppermute | solution.py:50
  83.6 5.9 %collective-permute-start.28 = (f32[32,768]{1,0:T(8,128)S(1)}, f32[32,768]{1,0:T(8,128)S(1)}, u32[]{:S(2)}, u32[]{:S(2)}) collective-permute-start(f32[32,768]{1,0:T(8,128)S(1)} %add.77), channel_id=1, source_target_pairs={{0,96},{1,25},{2,98},{3,27},{4,100},{5,29},{6,102},{7,31},{8,104},... | collective-permute-start | bytes 294920 | tf_op jit(solution)/shard_map/ppermute | solution.py:50
  89.5 5.9 %collective-permute-start.29 = (f32[32,768]{1,0:T(8,128)S(1)}, f32[32,768]{1,0:T(8,128)S(1)}, u32[]{:S(2)}, u32[]{:S(2)}) collective-permute-start(f32[32,768]{1,0:T(8,128)S(1)} %add.78), channel_id=1, source_target_pairs={{0,24},{1,97},{2,26},{3,99},{4,28},{5,101},{6,30},{7,103},{8,16},{... | collective-permute-start | bytes 294920 | tf_op jit(solution)/shard_map/ppermute | solution.py:50

commit v5 on v4

--- a/solution.py
+++ b/solution.py
@@ -98,94 +98,99 @@
     return pl.CostEstimate(flops=0, bytes_accessed=int(us * 3_000_000), transcendentals=0)
 
 
-def loads(refs, bufs, sems, dh, d1):
-    copies = []
-    for chain in range(2):
-        rows, orows = group_rows(chain, group_of(chain, dh, d1)[0])
-        gkv, ekv, gout, eout = refs
-        sources = (gkv.at[0, chain, rows, :], ekv.at[0, chain, rows, :], gout.at[0, orows, :], eout.at[0, orows, :])
-        for n, (src, dst) in enumerate(zip(sources, bufs)):
-            copies.append(pltpu.make_async_copy(src, dst.at[chain], sems.at[chain, n]))
-    return copies
-
-
-def part_kernel(here, then, *refs):
+KV_ROWS = jax.ShapeDtypeStruct((GROUP * CH, COLS), BF16)
+OUT_ROWS = jax.ShapeDtypeStruct((GROUP * OCH, OCOLS), BF16)
+ROW_SHAPES = [KV_ROWS, KV_ROWS, OUT_ROWS, OUT_ROWS]
+
+
+def loads(refs, bufs, sems, chain, group):
+    rows, orows = group_rows(chain, group_of(chain, *group)[0])
+    gkv, ekv, gout, eout = refs
+    sources = (gkv.at[0, chain, rows, :], ekv.at[0, chain, rows, :], gout.at[0, orows, :], eout.at[0, orows, :])
+    return [pltpu.make_async_copy(src, dst, sems.at[n]) for n, (src, dst) in enumerate(zip(sources, bufs))]
+
+
+def part_kernel(group, given, ahead, n_after, first, *refs):
     refs = list(refs)
     take = lambda n: [refs.pop(0) for _ in range(n)]
     hbm, basis = take(4), take(2)
-    loaded = here[2]
-    bufs = take(4) if loaded else None
-    refs = refs[here[3] :]
+    bufs = {chain: take(4) for chain in given}
+    take(n_after)
     outs = take(2)
-    bufs = bufs or take(4)
-    later = take(4) if then else None
+    here = [chain for chain in range(2) if chain not in given]
+    for chain in here:
+        bufs[chain] = take(4)
+    later = [take(4) for _ in ahead]
     sems = refs[-1]
-    now = [] if loaded else loads(hbm, bufs, sems.at[0], *here[:2])
-    after = loads(hbm, later, sems.at[1], *then) if then else []
-    if not loaded:
+    now = {chain: loads(hbm, bufs[chain], sems.at[chain], chain, group) for chain in here}
+    after = [c for n, (chain, g) in enumerate(ahead) for c in loads(hbm, later[n], sems.at[2 + n], chain, g)]
+    if first:
         split_kv, split_out, bkv, bout, bsems = refs[:5]
-        first = [
+        copies = [
             pltpu.make_async_copy(basis[0], bkv, bsems.at[0]),
             pltpu.make_async_copy(basis[1], bout, bsems.at[1]),
         ]
-        for copy in first + now:
+        for copy in copies:
             copy.start()
-        for copy in first:
+    for chain in here:
+        for copy in now[chain]:
+            copy.start()
+    if not first:
+        for copy in after:
+            copy.start()
+    if first:
+        for copy in copies:
             copy.wait()
         for a in range(2):
             b = jnp.concatenate(split3(bkv[a]), axis=0)
             split_kv[a] = jnp.concatenate([b, b], axis=1)
         split_out[...] = jnp.concatenate(split3(bout[...]), axis=0)
         basis = (split_kv, split_out)
-    else:
-        for copy in after:
-            copy.start()
-    kv = [basis[0][a] for a in range(2)]
-    ob = basis[1][...]
 
     def fold(r):
         return r[:RANK] + (r[RANK : 2 * RANK] + r[2 * RANK :])
 
-    bgkv, bekv, bgout, beout = bufs
-    for chain in range(2):
-        if now:
-            for copy in now[4 * chain : 4 * chain + 4]:
-                copy.wait()
-            for copy in after[4 * chain : 4 * chain + 4]:
+    for chain in [*given, *here]:
+        for copy in now.get(chain, []):
+            copy.wait()
+        if first and chain == here[0]:
+            for copy in after:
                 copy.start()
-        out = outs[chain]
-        _, name = group_of(chain, *here[:2])
+        gkv, ekv, gout, eout = bufs[chain]
+        _, name = group_of(chain, *group)
         for j in range(GROUP):
             rows, orows = slice(j * CH, (j + 1) * CH), slice(j * OCH, (j + 1) * OCH)
-            both = jnp.concatenate([bgkv[chain, rows], bekv[chain, rows]], axis=1)
             i = jnp.bitwise_xor(name, j)
-            out[i, :, :CH] = fold(dot_nt(kv[chain], both))
-            out[i, :, CH:] = fold(dot_nt(ob, bgout[chain, orows]) + dot_nt(ob, beout[chain, orows]))
+            both = jnp.concatenate([gkv[rows], ekv[rows]], axis=1)
+            outs[chain][i, :, :CH] = fold(dot_nt(basis[0][chain], both))
+            outs[chain][i, :, CH:] = fold(dot_nt(basis[1][...], gout[orows]) + dot_nt(basis[1][...], eout[orows]))
     for copy in after:
         copy.wait()
 
 
-def part(here, then, args, basis, bufs=(), after=()):
-    lead = jax.ShapeDtypeStruct((GROUP, RANK, WIDE), F32)
-    kv = jax.ShapeDtypeStruct((2, GROUP * CH, COLS), BF16)
-    out = jax.ShapeDtypeStruct((2, GROUP * OCH, OCOLS), BF16)
-    n = (not bufs) + (then is not None)
-    split = (jax.ShapeDtypeStruct((2, 3 * RANK, 2 * COLS), BF16), jax.ShapeDtypeStruct((3 * RANK, OCOLS), BF16))
-    scratch = [pltpu.VMEM((2, RANK, COLS), F32), pltpu.VMEM((RANK, OCOLS), F32), pltpu.SemaphoreType.DMA((2,))]
+def part(group, args, basis, bufs, ahead=(), after=(), first=False):
+    given = [chain for chain in range(2) if (chain, group) in bufs]
+    loaded = [(chain, group) for chain in range(2) if chain not in given] + list(ahead)
+    shapes = [jax.ShapeDtypeStruct((GROUP, RANK, WIDE), F32)] * 2 + ROW_SHAPES * len(loaded)
+    scratch = [pltpu.SemaphoreType.DMA((2 + len(ahead), 4))]
+    if first:
+        shapes.append(jax.ShapeDtypeStruct((2, 3 * RANK, 2 * COLS), BF16))
+        shapes.append(jax.ShapeDtypeStruct((3 * RANK, OCOLS), BF16))
+        scratch = [pltpu.VMEM((2, RANK, COLS), F32), pltpu.VMEM((RANK, OCOLS), F32), pltpu.SemaphoreType.DMA((2,))] + scratch
+    operands = [x for chain in given for x in bufs[chain, group]]
     result = pl.pallas_call(
-        functools.partial(part_kernel, (*here, bool(bufs), len(after)), then),
-        out_shape=(lead, lead) + (kv, kv, out, out) * n + (() if bufs else split),
-        in_specs=[HBM] * 4 + [VM if bufs else HBM] * 2 + [VM] * (len(bufs) + len(after)),
-        out_specs=(VM,) * (2 + 4 * n + 2 * (not bufs)),
-        scratch_shapes=([] if bufs else scratch) + [pltpu.SemaphoreType.DMA((2, 2, 4))],
-        compiler_params=pltpu.CompilerParams(vmem_limit_bytes=14 * MIB),
-        cost_estimate=cost(PART_US),
+        functools.partial(part_kernel, group, given, ahead, len(after), first),
+        out_shape=shapes,
+        in_specs=[HBM] * 4 + [HBM if first else VM] * 2 + [VM] * (len(operands) + len(after)),
+        out_specs=[VM] * len(shapes),
+        scratch_shapes=scratch,
+        compiler_params=pltpu.CompilerParams(vmem_limit_bytes=16 * MIB),
+        cost_estimate=cost(3),
         name="part",
-    )(*args, *basis, *bufs, *after)
-    return result[:2], *[result[2 + 4 * i : 6 + 4 * i] for i in range(n)], *([] if bufs else [result[-2:]])
-
-
-PART_US = 3
+    )(*args, *basis, *operands, *after)
+    for n, key in enumerate(loaded):
+        bufs[key] = tuple(result[2 + 4 * n : 6 + 4 * n])
+    return result[:2], result[2 + 4 * len(loaded) :]
 
 
 def tree(items):
@@ -194,10 +199,11 @@
     return items[0]
 
 
-def right_kernel(dh, d1, n_before, *refs):
-    bgkv, bekv, bgout, beout, lead_a, lead_b = refs[:6]
-    before = refs[6 : 6 + n_before]
-    right, gram = refs[6 + n_before :]
+def right_kernel(chain, group, n_before, last, *refs):
+    bufs, x = refs[:4], refs[4]
+    before = refs[5 : 5 + n_before]
+    keys = refs[5 + n_before] if last else None
+    right, gram = refs[-2:]
 
     def fold(r):
         return r[:RANK] + r[RANK:]
@@ -210,50 +216,58 @@
 
         return at(0, 0) + ((at(0, 1) + at(1, 0)) + ((at(0, 2) + at(2, 0)) + at(1, 1)))
 
-    sums = [0.0, 0.0, 0.0]
-    grams = [[], [], [], []]
-    for k, x in enumerate((lead_a, lead_b)):
-        _, name = group_of(k, dh, d1)
-        for j in range(GROUP):
-            parts = split3(x[jnp.bitwise_xor(name, j)])
-            kv, o = [p[:, :CH] for p in parts], [p[:, CH:] for p in parts]
-            grams[k].append(square(kv))
-            grams[2 + k].append(square(o))
-            rows, orows = slice(j * CH, (j + 1) * CH), slice(j * OCH, (j + 1) * OCH)
-            both = jnp.concatenate([bgkv[k, rows], bekv[k, rows]], axis=1)
-            r = fold(dot(jnp.concatenate(kv[:2], axis=0), both))
-            sums[k] += r[:, :COLS] + r[:, COLS:]
-            two = jnp.concatenate(o[:2], axis=0)
-            sums[2] += fold(dot(two, bgout[k, orows]) + dot(two, beout[k, orows]))
-    for k in range(4):
+    sums = [0.0, 0.0]
+    grams = [[], []]
+    _, name = group_of(chain, *group)
+    for j in range(GROUP):
+        parts = split3(x[jnp.bitwise_xor(name, j)])
+        rows, orows = slice(j * CH, (j + 1) * CH), slice(j * OCH, (j + 1) * OCH)
+        kv, o = [p[:, :CH] for p in parts], [p[:, CH:] for p in parts]
+        grams[0].append(square(kv))
+        grams[1].append(square(o))
+        both = jnp.concatenate([bufs[0][rows], bufs[1][rows]], axis=1)
+        r = fold(dot(jnp.concatenate(kv[:2], axis=0), both))
+        sums[0] += r[:, :COLS] + r[:, COLS:]
+        two = jnp.concatenate(o[:2], axis=0)
+        sums[1] += fold(dot(two, bufs[2][orows]) + dot(two, bufs[3][orows]))
+    for k in range(2):
         gram[k] = tree(grams[k])
     sums = jnp.concatenate(sums, axis=1)
     for other in before:
         sums += other[...]
-    right[...] = sums
-
-
-def right_part(dh, d1, bufs, lead, before=()):
+    if last:
+        right[:, :COLS] = keys[:, :COLS]
+        right[:, COLS : 2 * COLS] = sums[:, :COLS]
+        right[:, 2 * COLS :] = keys[:, COLS:] + sums[:, COLS:]
+    else:
+        right[...] = sums
+
+
+def right_part(chain, group, bufs, lead, before=(), keys=None):
+    last = keys is not None
+    width = 2 * COLS + OCOLS if last else COLS + OCOLS
+    operands = (*bufs[chain, group], lead, *before, *([keys] if last else []))
     return pl.pallas_call(
-        functools.partial(right_kernel, dh, d1, len(before)),
+        functools.partial(right_kernel, chain, group, len(before), last),
         out_shape=(
-            jax.ShapeDtypeStruct((RANK, 2 * COLS + OCOLS), F32),
-            jax.ShapeDtypeStruct((4, RANK, RANK), F32),
+            jax.ShapeDtypeStruct((RANK, width), F32),
+            jax.ShapeDtypeStruct((2, RANK, RANK), F32),
         ),
-        in_specs=[VM] * (6 + len(before)),
+        in_specs=[VM] * len(operands),
         out_specs=(VM, VM),
-        compiler_params=pltpu.CompilerParams(vmem_limit_bytes=20 * MIB),
-        cost_estimate=cost(2),
+        compiler_params=pltpu.CompilerParams(vmem_limit_bytes=16 * MIB),
+        cost_estimate=cost(1),
         name="right",
-    )(*bufs, *lead, *before)
-
-
-def factor_kernel(g0, g1, g2, g3, out):
+    )(*operands)
+
+
+def factor_kernel(a0, a1, a2, a3, b0, b1, b2, b3, out):
     row = lax.broadcasted_iota(jnp.int32, (RANK, 2 * RANK), 0)
     col = lax.broadcasted_iota(jnp.int32, (RANK, 2 * RANK), 1)
     eye = jnp.where(col == row + RANK, 1.0, 0.0).astype(F32)
-    gram = [(g0[k] + g1[k]) + (g2[k] + g3[k]) for k in range(4)]
-    gram[2] += gram[3]
+    keys, outs_a = [(a0[k] + a1[k]) + (a2[k] + a3[k]) for k in range(2)]
+    values, outs_b = [(b0[k] + b1[k]) + (b2[k] + b3[k]) for k in range(2)]
+    gram = [keys, values, outs_a + outs_b]
     wide = [jnp.concatenate([gram[k], jnp.zeros((RANK, RANK), F32)], axis=1) + eye for k in range(3)]
     scale = [jnp.zeros((RANK, 1), F32)] * 3
     below = lax.broadcasted_iota(jnp.int32, (RANK, 1), 0)
@@ -272,7 +286,7 @@
     return pl.pallas_call(
         factor_kernel,
         out_shape=jax.ShapeDtypeStruct((3, RANK, RANK), F32),
-        in_specs=[VM] * 4,
+        in_specs=[VM] * 8,
         out_specs=VM,
         compiler_params=pltpu.CompilerParams(vmem_limit_bytes=4 * MIB),
         cost_estimate=cost(4),
@@ -341,8 +355,8 @@
 
 
 def error_kernel(*refs):
-    total, w, ortho = refs[16], refs[17], refs[18:20]
-    right_kv, right_out, new_kv, new_out, nkv, nout, nsems = refs[20:]
+    total, w, ortho = refs[32], refs[33], refs[34:36]
+    right_kv, right_out, new_kv, new_out, nkv, nout, nsems = refs[36:]
     packed = []
     for k, (at, n) in enumerate(((0, COLS), (COLS, COLS), (2 * COLS, OCOLS))):
         w1, w2, w3 = split3(w[k])
@@ -358,16 +372,15 @@
         high, low = split2(right)
         packed.append(jnp.concatenate([high, high, low, jnp.zeros_like(high)], axis=0))
     stores = []
-    for g in range(4):
-        dh, d1 = g // 2, g % 2
-        bgkv, bekv, bgout, beout = refs[4 * g : 4 * g + 4]
+    for g, (dh, d1) in enumerate(GROUPS):
         for s in range(2):
+            gkv, ekv, gout, eout = refs[8 * g + 4 * s : 8 * g + 4 * s + 4]
             for j in range(GROUP):
-                rows, orows = slice(j * CH, (j + 1) * CH), slice(j * OCH, (j + 1) * OCH)
-                merged = bgkv[s, rows].astype(F32) + bekv[s, rows].astype(F32)
-                nkv[g, s, rows] = (merged - dot(ortho[dh][d1, s, j, :CH], packed[s])).astype(BF16)
-                merged = bgout[s, orows].astype(F32) + beout[s, orows].astype(F32)
-                nout[g, s, orows] = (merged - dot(ortho[dh][d1, s, j, CH:], packed[2])).astype(BF16)
+                at, oat = slice(j * CH, (j + 1) * CH), slice(j * OCH, (j + 1) * OCH)
+                merged = gkv[at].astype(F32) + ekv[at].astype(F32)
+                nkv[g, s, at] = (merged - dot(ortho[dh][d1, s, j, :CH], packed[s])).astype(BF16)
+                merged = gout[oat].astype(F32) + eout[oat].astype(F32)
+                nout[g, s, oat] = (merged - dot(ortho[dh][d1, s, j, CH:], packed[2])).astype(BF16)
             rows, orows = group_rows(s, group_of(s, dh, d1)[0])
             stores.append(pltpu.make_async_copy(nkv.at[g, s], new_kv.at[0, s, rows, :], nsems.at[g, s, 0]))
             stores.append(pltpu.make_async_copy(nout.at[g, s], new_out.at[0, orows, :], nsems.at[g, s, 1]))
@@ -377,7 +390,11 @@
         copy.wait()
 
 
+GROUPS = ((0, 0), (0, 1), (1, 0), (1, 1))
+
+
 def errors(bufs, total, w, ortho):
+    bufs = [x for group in GROUPS for chain in range(2) for x in bufs[chain, group]]
     return pl.pallas_call(
         error_kernel,
         out_shape=(
@@ -386,7 +403,7 @@
             jax.ShapeDtypeStruct((1, 2, ROWS, COLS), BF16),
             jax.ShapeDtypeStruct((1, OROWS, OCOLS), BF16),
         ),
-        in_specs=[VM] * 20,
+        in_specs=[VM] * 36,
         out_specs=(VM, VM, HBM, HBM),
         scratch_shapes=[
             pltpu.VMEM((4, 2, GROUP * CH, COLS), BF16),
@@ -402,14 +419,16 @@
 def on_device(grad_kv, error_kv, grad_out, error_out, basis_kv, basis_out):
     args = (grad_kv, error_kv, grad_out, error_out, jnp.swapaxes(basis_kv, 1, 2), basis_out.T)
     *args, bkv, bout = [pltpu.with_memory_space_constraint(x, pltpu.HBM) for x in args]
-    far, bufs_far1, bufs_near1, basis = part((1, 1), (0, 1), args, (bkv, bout))
+    near0, near1, far0, far1 = GROUPS
+    bufs = {}
+    far, basis = part(far1, args, (bkv, bout), bufs, [(0, near1)], first=True)
     far = [send(x, CORES) for x in far]
-    near, bufs_far0 = part((0, 1), (1, 0), args, basis, bufs_near1)
+    near, _ = part(near1, args, basis, bufs, [(0, far0)])
     sent = [x + y for x, y in zip(near, far)]
     got = [send(x, pairs(CHAINS[s], 0)) for s, x in enumerate(sent)]
-    far, bufs_near0 = part((1, 0), (0, 0), args, basis, bufs_far0, sent)
+    far, _ = part(far0, args, basis, bufs, [(0, near0), (1, near0)], after=sent)
     far = [send(x, CORES) for x in far]
-    (near,) = part((0, 0), None, args, basis, bufs_near0, got[1:])
+    near, _ = part(near0, args, basis, bufs, after=got[1:])
     both = [(x + y) + z for x, y, z in zip(near, far, got)]
 
     for k in range(1, 2 * STEPS):
@@ -425,15 +444,18 @@
     own0 = both
     own1 = [send(x, pairs(CHAINS[s], 0)) for s, x in enumerate(both)]
     other0 = [send(x, CORES) for x in own0]
-    sum1, gram1 = right_part(0, 0, bufs_near0, own0)
-    sum2, gram2 = right_part(1, 0, bufs_far0, other0)
-    own1, sum1, sum2 = lax.optimization_barrier((own1, sum1, sum2))
-    other1 = [send(x, CORES) for x in own1]
-    sum3, gram3 = right_part(0, 1, bufs_near1, own1)
-    total, gram4 = right_part(1, 1, bufs_far1, other1, (sum1, sum2, sum3))
+    other1, grams, total = [], [], None
+    for s in range(2):
+        sum1, gram1 = right_part(s, near0, bufs, own0[s])
+        sum2, gram2 = right_part(s, far0, bufs, other0[s])
+        own1[s], sum1, sum2 = lax.optimization_barrier((own1[s], sum1, sum2))
+        other1.append(send(own1[s], CORES))
+        sum3, gram3 = right_part(s, near1, bufs, own1[s])
+        total, gram4 = right_part(s, far1, bufs, other1[s], (sum1, sum2, sum3), total)
+        grams += [gram1, gram3, gram2, gram4]
     own = (own0[0], own1[0], own0[1], own1[1])
     other = (other0[0], other1[0], other0[1], other1[1])
-    w = factor((gram1, gram3, gram2, gram4))
+    w = factor(grams)
     total = total + send(total, pairs(RIGHT, 0))
     total, w = lax.optimization_barrier((total, w))
     *left, ortho_own = left_part(0, own, w)
@@ -443,9 +465,7 @@
     total = total + send(total, pairs(RIGHT, 2))
     total, ortho_other = lax.optimization_barrier((total, ortho_other))
     total = total + send(total, pairs(RIGHT, 3))
-    right_kv, right_out, new_kv, new_out = errors(
-        (*bufs_near0, *bufs_near1, *bufs_far0, *bufs_far1), total, w, (ortho_own, ortho_other)
-    )
+    right_kv, right_out, new_kv, new_out = errors(bufs, total, w, (ortho_own, ortho_other))
     return (
         jnp.swapaxes(left_kv, 1, 2),
         left_out.T,

time: 100 us -> 97.5 us (0.975)
  starting transfers between devices: 30.1 us -> 27.6 us
    ppermute x30, starting transfers between devices: 30.1 us -> 27.6 us  [send(): return lax.ppermute(x, ('dp', 'mp'), to)]
    pallas_call x8 -> x12, Pallas kernels: 18.6 us -> 17.7 us  [the longest x4 11.7 us: part(): pl.pallas_call(functools.partial(part_kernel, group, given, ahead, len(af...]
  transfers between devices with their start and end apart: 30 -> 30, of which waited for: 19 -> 18; matrix products, arithmetic and copies ran while one was open for 0% -> 0% of each run, Pallas kernels for 19% -> 21%
where the time goes in v5:
time: 97.5 us; the launch traced here: 97.3 us
  waiting for transfers between devices  38.9 us (40%)
  Pallas kernels  29.2 us (30%)
  starting transfers between devices  27.6 us (28%)
  between operations  1.1 us (1%)
    ppermute x30, waiting for transfers between devices, send(): return lax.ppermute(x, ('dp', 'mp'), to)  38.9 us
    ppermute x30, starting transfers between devices, send(): return lax.ppermute(x, ('dp', 'mp'), to)  27.6 us
    pallas_call x4, Pallas kernels, part(): pl.pallas_call(functools.partial(part_kernel, group, given, ahead, len(af...  11.7 us
    pallas_call x8, Pallas kernels, right_part(): pl.pallas_call(functools.partial(right_kernel, chain, group, len(before),...  6.07 us
    pallas_call x1, Pallas kernels, errors(): pl.pallas_call(error_kernel, out_shape=(jax.ShapeDtypeStruct((2, RANK, CO...  4.72 us
    pallas_call x2, Pallas kernels, left_part(): pl.pallas_call(functools.partial(left_kernel, dh), out_shape=(jax.ShapeDt...  3.9 us
    pallas_call x1, Pallas kernels, factor(): pl.pallas_call(factor_kernel, out_shape=jax.ShapeDtypeStruct((3, RANK, RA...  2.87 us
  transfers between devices with their start and end apart: 30, of which 18 were waited for; matrix products, arithmetic and copies ran while one was open for 0% of the time, Pallas kernels for 21%

profile of v5, /device:TPU:0, one launch (start us, length us, event | category | flops | bytes accessed | tf_op | source)
XLA Modules:
  0.0 97.3 jit_solution(9772710351765887855)
XLA Ops:
  0.6 3.8 %part.4 = (f32[4,32,640]{2,1,0:T(8,128)S(1)}, f32[4,32,640]{2,1,0:T(8,128)S(1)}, bf16[2048,128]{1,0:T(8,128)(2,1)S(1)}, bf16[2048,128]{1,0:T(8,128)(2,1)S(1)}, b...) custom-call(bf16[1,2,8192,128]{3,2,1,0:T(8,128)(2,1)} %refs_0_.7, ...), custom_call_target="tpu_custom_call" | custom-call | bytes 9000000 | tf_op jit(solution)/shard_map/part/pallas_call | solution.py:181
  4.4 0.1 collective-permute-start.1
  4.5 0.5 collective-permute-start
  5.0 3.0 %part.5 = (f32[4,32,640]{2,1,0:T(8,128)S(1)}, f32[4,32,640]{2,1,0:T(8,128)S(1)}, bf16[2048,128]{1,0:T(8,128)(2,1)S(1)}, bf16[2048,128]{1,0:T(8,128)(2,1)S(1)}, b...) custom-call(bf16[1,2,8192,128]{3,2,1,0:T(8,128)(2,1)} %refs_0_.7, ...), custom_call_target="tpu_custom_call" | custom-call | bytes 9000000 | tf_op jit(solution)/shard_map/part/pallas_call | solution.py:181
  8.0 1.7 %collective-permute-start.2 = (f32[4,32,640]{2,1,0:T(8,128)S(1)}, f32[4,32,640]{2,1,0:T(8,128)S(1)}, u32[]{:S(2)}, u32[]{:S(2)}) collective-permute-start(f32[4,32,640]{2,1,0:T(8,128)S(1)} %add.61.refs_11_), channel_id=1, source_target_pairs={{0,32},{1,97},{2,34},{3,99},{4,36},{5,101},{6,38},{7,103},{8,40},{... | collective-permute-start | bytes 983048 | tf_op jit(solution)/shard_map/ppermute | solution.py:50
  9.8 1.6 %collective-permute-start.4 = (f32[4,32,640]{2,1,0:T(8,128)S(1)}, f32[4,32,640]{2,1,0:T(8,128)S(1)}, u32[]{:S(2)}, u32[]{:S(2)}) collective-permute-start(f32[4,32,640]{2,1,0:T(8,128)S(1)} %add.60.refs_10_), channel_id=1, source_target_pairs={{0,2},{1,7},{2,0},{3,5},{4,6},{5,3},{6,4},{7,1},{8,10},{9,15},{10,... | collective-permute-start | bytes 983048 | tf_op jit(solution)/shard_map/ppermute | solution.py:50
  11.4 3.5 %part.6 = (f32[4,32,640]{2,1,0:T(8,128)S(1)}, f32[4,32,640]{2,1,0:T(8,128)S(1)}, bf16[2048,128]{1,0:T(8,128)(2,1)S(1)}, bf16[2048,128]{1,0:T(8,128)(2,1)S(1)}, b...) custom-call(bf16[1,2,8192,128]{3,2,1,0:T(8,128)(2,1)} %refs_0_.7, ...), custom_call_target="tpu_custom_call" | custom-call | bytes 9000000 | tf_op jit(solution)/shard_map/part/pallas_call | solution.py:181
  14.9 2.3 %collective-permute-start.3 = (f32[4,32,640]{2,1,0:T(8,128)S(1)}, f32[4,32,640]{2,1,0:T(8,128)S(1)}, u32[]{:S(2)}, u32[]{:S(2)}) collective-permute-start(f32[4,32,640]{2,1,0:T(8,128)S(1)} %get-tuple-element.110), channel_id=1, source_target_pairs={{0,1},{1,0},{2,3},{3,2},{4,5},{5,4},{6,7},{7,6},{8,9},{9,8},{10,11... | collective-permute-start | bytes 983048 | tf_op jit(solution)/shard_map/ppermute | solution.py:50
  17.2 0.1 collective-permute-start.15
  17.3 1.4 %part.7 = (f32[4,32,640]{2,1,0:T(8,128)S(1)}, f32[4,32,640]{2,1,0:T(8,128)S(1)}) custom-call(bf16[1,2,8192,128]{3,2,1,0:T(8,128)(2,1)} %refs_0_.7, bf16[1,2,8192,128]{3,2,1,0:T(8,128)(2,1)} %refs_1_.7, bf16[1,4096,512]{2,1,0:T(8,128)(2,1)} %refs_2_.7, bf16[1,4096,512]{2,1,0:T(8,128)(2,1)} %refs_3_.7, bf16[2,96,256]{2,1,0:T(8,128)(2,1)S(1)} %get-tuple-element.87.refs_4_, ...), custom_call_target="tpu_custom_call" | custom-call | bytes 9000000 | tf_op jit(solution)/shard_map/part/pallas_call | solution.py:181
  18.8 0.1 add_add_fusion.1
  18.8 0.2 collective-permute-start.5
  19.1 0.1 add_add_fusion
  19.1 2.0 %collective-permute-start.16 = (f32[2,32,640]{2,1,0:T(8,128)S(1)}, f32[2,32,640]{2,1,0:T(8,128)S(1)}, u32[]{:S(2)}, u32[]{:S(2)}) collective-permute-start(f32[2,32,640]{2,1,0:T(8,128)S(1)} %slice.37), channel_id=1, source_target_pairs={{0,8},{1,25},{2,10},{3,27},{4,12},{5,29},{6,14},{7,31},{8,0},{9,17... | collective-permute-start | bytes 491528 | tf_op jit(solution)/shard_map/ppermute | solution.py:50
  21.1 3.1 %collective-permute-done.5 = f32[2,32,640]{2,1,0:T(8,128)S(1)} collective-permute-done((f32[2,32,640]{2,1,0:T(8,128)S(1)}, f32[2,32,640]{2,1,0:T(8,128)S(1)}, u32[]{:S(2)}, u32[]{:S(2)}) %collective-permute-start.5) | collective-permute-done | bytes 163872 | tf_op jit(solution)/shard_map/ppermute | solution.py:50
  24.3 2.0 %collective-permute-start.6 = (f32[1,32,640]{2,1,0:T(8,128)S(1)}, f32[1,32,640]{2,1,0:T(8,128)S(1)}, u32[]{:S(2)}, u32[]{:S(2)}) collective-permute-start(f32[1,32,640]{2,1,0:T(8,128)S(1)} %slice.35), channel_id=1, source_target_pairs={{0,8},{1,25},{2,10},{3,27},{4,12},{5,29},{6,14},{7,31},{8,0},{9,17... | collective-permute-start | bytes 245768 | tf_op jit(solution)/shard_map/ppermute | solution.py:50
  26.3 0.3 collective-permute-start.17
  26.6 2.2 %collective-permute-done.6 = f32[1,32,640]{2,1,0:T(8,128)S(1)} collective-permute-done((f32[1,32,640]{2,1,0:T(8,128)S(1)}, f32[1,32,640]{2,1,0:T(8,128)S(1)}, u32[]{:S(2)}, u32[]{:S(2)}) %collective-permute-start.6) | collective-permute-done | bytes 81952 | tf_op jit(solution)/shard_map/ppermute | solution.py:50
  28.8 1.1 %collective-permute-start.7 = (f32[1,32,640]{2,1,0:T(8,128)S(1)}, f32[1,32,640]{2,1,0:T(8,128)S(1)}, u32[]{:S(2)}, u32[]{:S(2)}) collective-permute-start(f32[1,32,640]{2,1,0:T(8,128)S(1)} %slice_add_fusion.3), channel_id=1, source_target_pairs={{0,6},{1,3},{2,4},{3,1},{4,2},{5,7},{6,0},{7,5},{8,14},{9,11},{10,... | collective-permute-start | bytes 245768 | tf_op jit(solution)/shard_map/ppermute | solution.py:50
  29.9 1.0 %collective-permute-done.17 = f32[1,32,640]{2,1,0:T(8,128)S(1)} collective-permute-done((f32[1,32,640]{2,1,0:T(8,128)S(1)}, f32[1,32,640]{2,1,0:T(8,128)S(1)}, u32[]{:S(2)}, u32[]{:S(2)}) %collective-permute-start.17) | collective-permute-done | bytes 81952 | tf_op jit(solution)/shard_map/ppermute | solution.py:50
  30.9 1.9 %collective-permute-start.18 = (f32[1,32,640]{2,1,0:T(8,128)S(1)}, f32[1,32,640]{2,1,0:T(8,128)S(1)}, u32[]{:S(2)}, u32[]{:S(2)}) collective-permute-start(f32[1,32,640]{2,1,0:T(8,128)S(1)} %slice_add_fusion.2), channel_id=1, source_target_pairs={{0,96},{1,33},{2,98},{3,35},{4,100},{5,37},{6,102},{7,39},{8,104},... | collective-permute-start | bytes 245768 | tf_op jit(solution)/shard_map/ppermute | solution.py:50
  32.7 1.8 %collective-permute-done.7 = f32[1,32,640]{2,1,0:T(8,128)S(1)} collective-permute-done((f32[1,32,640]{2,1,0:T(8,128)S(1)}, f32[1,32,640]{2,1,0:T(8,128)S(1)}, u32[]{:S(2)}, u32[]{:S(2)}) %collective-permute-start.7) | collective-permute-done | bytes 81952 | tf_op jit(solution)/shard_map/ppermute | solution.py:50
  34.6 1.0 %collective-permute-start.8 = (f32[1,32,640]{2,1,0:T(8,128)S(1)}, f32[1,32,640]{2,1,0:T(8,128)S(1)}, u32[]{:S(2)}, u32[]{:S(2)}) collective-permute-start(f32[1,32,640]{2,1,0:T(8,128)S(1)} %add.66), channel_id=1, source_target_pairs={{0,96},{1,33},{2,98},{3,35},{4,100},{5,37},{6,102},{7,39},{8,104},... | collective-permute-start | bytes 245768 | tf_op jit(solution)/shard_map/ppermute | solution.py:50
  35.6 1.0 %collective-permute-done.18 = f32[1,32,640]{2,1,0:T(8,128)S(1)} collective-permute-done((f32[1,32,640]{2,1,0:T(8,128)S(1)}, f32[1,32,640]{2,1,0:T(8,128)S(1)}, u32[]{:S(2)}, u32[]{:S(2)}) %collective-permute-start.18) | collective-permute-done | bytes 81952 | tf_op jit(solution)/shard_map/ppermute | solution.py:50
  36.6 3.1 %collective-permute-start.19 = (f32[1,32,640]{2,1,0:T(8,128)S(1)}, f32[1,32,640]{2,1,0:T(8,128)S(1)}, u32[]{:S(2)}, u32[]{:S(2)}) collective-permute-start(f32[1,32,640]{2,1,0:T(8,128)S(1)} %add.73), channel_id=1, source_target_pairs={{0,24},{1,9},{2,26},{3,11},{4,28},{5,13},{6,30},{7,15},{8,16},{9,1... | collective-permute-start | bytes 245768 | tf_op jit(solution)/shard_map/ppermute | solution.py:50
  39.8 0.5 collective-permute-done.8
  40.3 4.1 %collective-permute-start.9 = (f32[1,32,640]{2,1,0:T(8,128)S(1)}, f32[1,32,640]{2,1,0:T(8,128)S(1)}, u32[]{:S(2)}, u32[]{:S(2)}) collective-permute-start(f32[1,32,640]{2,1,0:T(8,128)S(1)} %add.67), channel_id=1, source_target_pairs={{0,24},{1,9},{2,26},{3,11},{4,28},{5,13},{6,30},{7,15},{8,16},{9,1... | collective-permute-start | bytes 245768 | tf_op jit(solution)/shard_map/ppermute | solution.py:50
  44.4 1.1 %collective-permute-start.20 = (f32[1,32,640]{2,1,0:T(8,128)S(1)}, f32[1,32,640]{2,1,0:T(8,128)S(1)}, u32[]{:S(2)}, u32[]{:S(2)}) collective-permute-start(f32[1,32,640]{2,1,0:T(8,128)S(1)} %add.74), channel_id=1, source_target_pairs={{0,6},{1,3},{2,4},{3,1},{4,2},{5,7},{6,0},{7,5},{8,14},{9,11},{10,... | collective-permute-start | bytes 245768 | tf_op jit(solution)/shard_map/ppermute | solution.py:50
  45.5 1.3 %collective-permute-done.9 = f32[1,32,640]{2,1,0:T(8,128)S(1)} collective-permute-done((f32[1,32,640]{2,1,0:T(8,128)S(1)}, f32[1,32,640]{2,1,0:T(8,128)S(1)}, u32[]{:S(2)}, u32[]{:S(2)}) %collective-permute-start.9) | collective-permute-done | bytes 81952 | tf_op jit(solution)/shard_map/ppermute | solution.py:50
  46.9 0.1 collective-permute-start.10
  46.9 3.2 %collective-permute-done.20 = f32[1,32,640]{2,1,0:T(8,128)S(1)} collective-permute-done((f32[1,32,640]{2,1,0:T(8,128)S(1)}, f32[1,32,640]{2,1,0:T(8,128)S(1)}, u32[]{:S(2)}, u32[]{:S(2)}) %collective-permute-start.20) | collective-permute-done | bytes 81952 | tf_op jit(solution)/shard_map/ppermute | solution.py:50
  50.2 0.1 collective-permute-start.21
  50.3 1.1 %collective-permute-done.10 = f32[1,32,640]{2,1,0:T(8,128)S(1)} collective-permute-done((f32[1,32,640]{2,1,0:T(8,128)S(1)}, f32[1,32,640]{2,1,0:T(8,128)S(1)}, u32[]{:S(2)}, u32[]{:S(2)}) %collective-permute-start.10) | collective-permute-done | bytes 81952 | tf_op jit(solution)/shard_map/ppermute | solution.py:50
  51.4 0.1 collective-permute-start.11
  51.5 3.2 %collective-permute-done.21 = f32[1,32,640]{2,1,0:T(8,128)S(1)} collective-permute-done((f32[1,32,640]{2,1,0:T(8,128)S(1)}, f32[1,32,640]{2,1,0:T(8,128)S(1)}, u32[]{:S(2)}, u32[]{:S(2)}) %collective-permute-start.21) | collective-permute-done | bytes 81952 | tf_op jit(solution)/shard_map/ppermute | solution.py:50
  54.7 0.1 collective-permute-start.22
  54.8 2.0 %collective-permute-done.11 = f32[2,32,640]{2,1,0:T(8,128)S(1)} collective-permute-done((f32[2,32,640]{2,1,0:T(8,128)S(1)}, f32[2,32,640]{2,1,0:T(8,128)S(1)}, u32[]{:S(2)}, u32[]{:S(2)}) %collective-permute-start.11) | collective-permute-done | bytes 163872 | tf_op jit(solution)/shard_map/ppermute | solution.py:50
  56.8 1.0 %collective-permute-start.13 = (f32[4,32,640]{2,1,0:T(8,128)S(1)}, f32[4,32,640]{2,1,0:T(8,128)S(1)}, u32[]{:S(2)}, u32[]{:S(2)}) collective-permute-start(f32[4,32,640]{2,1,0:T(8,128)S(1)} %pad_maximum_fusion.refs_4_.refs_0_), channel_id=1, source_target_pairs={{0,2},{1,7},{2,0},{3,5},{4,6},{5,3},{6,4},{7,1},{8,10},{9,15},{10,... | collective-permute-start | bytes 983048 | tf_op jit(solution)/shard_map/ppermute | solution.py:50
  57.8 2.3 %collective-permute-done.22 = f32[2,32,640]{2,1,0:T(8,128)S(1)} collective-permute-done((f32[2,32,640]{2,1,0:T(8,128)S(1)}, f32[2,32,640]{2,1,0:T(8,128)S(1)}, u32[]{:S(2)}, u32[]{:S(2)}) %collective-permute-start.22) | collective-permute-done | bytes 163872 | tf_op jit(solution)/shard_map/ppermute | solution.py:50
  60.1 0.1 collective-permute-start.23
  60.2 0.3 collective-permute-start.24
  60.5 0.8 right.10
  61.3 0.8 right.8
  62.0 0.8 right.9
  62.8 1.2 %collective-permute-done.13.refs_4_.refs_1_ = f32[4,32,640]{2,1,0:T(8,128)S(1)} collective-permute-done((f32[4,32,640]{2,1,0:T(8,128)S(1)}, f32[4,32,640]{2,1,0:T(8,128)S(1)}, u32[]{:S(2)}, u32[]{:S(2)}) %collective-permute-start.13) | collective-permute-done | bytes 327712 | tf_op jit(solution)/shard_map/ppermute | solution.py:50
  64.0 0.7 right.11
  64.7 2.8 %collective-permute-done.24.refs_4_.refs_3_ = f32[4,32,640]{2,1,0:T(8,128)S(1)} collective-permute-done((f32[4,32,640]{2,1,0:T(8,128)S(1)}, f32[4,32,640]{2,1,0:T(8,128)S(1)}, u32[]{:S(2)}, u32[]{:S(2)}) %collective-permute-start.24) | collective-permute-done | bytes 327712 | tf_op jit(solution)/shard_map/ppermute | solution.py:50
  67.6 0.3 collective-permute-start.25
  67.9 0.7 right.13
  68.6 0.8 right.12
  69.4 0.8 right.14
  70.2 0.8 right.15
  70.9 0.1 collective-permute-start.26
  71.0 2.9 %factor.1.refs_4_.refs_33_ = f32[3,32,32]{2,1,0:T(8,128)S(1)} custom-call(f32[2,32,32]{2,1,0:T(8,128)S(1)} %get-tuple-element.143.a0, f32[2,32,32]{2,1,0:T(8,128)S(1)} %get-tuple-element.144.a1, f32[2,32,32]{2,1,0:T(8,128)S(1)} %get-tuple-element.145.a2, f32[2,32,32]{2,1,0:T(8,128)S(1)} %get-tuple-element.146.a3, f32[2,32,32]{2,1,0:T(8,128)S(1)} %get-tuple-element.147.b0, ...), custom_call_target="tpu_custom_call" | custom-call | bytes 12000000 | tf_op jit(solution)/shard_map/factor/pallas_call | solution.py:286
  73.9 1.7 %collective-permute-done.26 = f32[32,768]{1,0:T(8,128)S(1)} collective-permute-done((f32[32,768]{1,0:T(8,128)S(1)}, f32[32,768]{1,0:T(8,128)S(1)}, u32[]{:S(2)}, u32[]{:S(2)}) %collective-permute-start.26) | collective-permute-done | bytes 98336 | tf_op jit(solution)/shard_map/ppermute | solution.py:50
  75.6 0.1 collective-permute-start.27
  75.7 2.0 %left.2 = (f32[2,32,8192]{2,1,0:T(8,128)}, f32[32,4096]{1,0:T(8,128)}, bf16[2,2,4,640,128]{4,3,2,1,0:T(8,128)(2,1)S(1)}) custom-call(f32[4,32,640]{2,1,0:T(8,128)S(1)} %pad_maximum_fusion.refs_4_.refs_0_, f32[4,32,640]{2,1,0:T(8,128)S(1)} %collective-permute-done.13.refs_4_.refs_1_, f32[4,32,640]{2,1,0:T(8,128)S(1)} %pad_maximum_fusion.1.refs_4_.refs_2_, ...), custom_call_target="tpu_custom_call" | custom-call | bytes 6000000 | tf_op jit(solution)/shard_map/left/pallas_call | solution.py:336
  77.7 2.6 %collective-permute-done.27 = f32[32,768]{1,0:T(8,128)S(1)} collective-permute-done((f32[32,768]{1,0:T(8,128)S(1)}, f32[32,768]{1,0:T(8,128)S(1)}, u32[]{:S(2)}, u32[]{:S(2)}) %collective-permute-start.27) | collective-permute-done | bytes 98336 | tf_op jit(solution)/shard_map/ppermute | solution.py:50
  80.3 1.0 %collective-permute-start.28 = (f32[32,768]{1,0:T(8,128)S(1)}, f32[32,768]{1,0:T(8,128)S(1)}, u32[]{:S(2)}, u32[]{:S(2)}) collective-permute-start(f32[32,768]{1,0:T(8,128)S(1)} %add.77), channel_id=1, source_target_pairs={{0,96},{1,25},{2,98},{3,27},{4,100},{5,29},{6,102},{7,31},{8,104},... | collective-permute-start | bytes 294920 | tf_op jit(solution)/shard_map/ppermute | solution.py:50
  81.4 2.0 %left.3 = (f32[2,32,8192]{2,1,0:T(8,128)}, f32[32,4096]{1,0:T(8,128)}, bf16[2,2,4,640,128]{4,3,2,1,0:T(8,128)(2,1)S(1)}) custom-call(f32[4,32,640]{2,1,0:T(8,128)S(1)} %collective-permute-done.12.refs_4_.refs_0_, f32[4,32,640]{2,1,0:T(8,128)S(1)} %collective-permute-done.14.refs_4_.refs_1_, ...), custom_call_target="tpu_custom_call", output_to_operand_aliasing={{0}: (5, {}), {1}: (6, {})} | custom-call | bytes 6000000 | tf_op jit(solution)/shard_map/left/pallas_call | solution.py:336
  83.3 2.9 %collective-permute-done.28 = f32[32,768]{1,0:T(8,128)S(1)} collective-permute-done((f32[32,768]{1,0:T(8,128)S(1)}, f32[32,768]{1,0:T(8,128)S(1)}, u32[]{:S(2)}, u32[]{:S(2)}) %collective-permute-start.28) | collective-permute-done | bytes 98336 | tf_op jit(solution)/shard_map/ppermute | solution.py:50
  86.3 1.3 %collective-permute-start.29 = (f32[32,768]{1,0:T(8,128)S(1)}, f32[32,768]{1,0:T(8,128)S(1)}, u32[]{:S(2)}, u32[]{:S(2)}) collective-permute-start(f32[32,768]{1,0:T(8,128)S(1)} %add.78), channel_id=1, source_target_pairs={{0,24},{1,97},{2,26},{3,99},{4,28},{5,101},{6,30},{7,103},{8,16},{... | collective-permute-start | bytes 294920 | tf_op jit(solution)/shard_map/ppermute | solution.py:50
  87.5 4.9 %collective-permute-done.29 = f32[32,768]{1,0:T(8,128)S(1)} collective-permute-done((f32[32,768]{1,0:T(8,128)S(1)}, f32[32,768]{1,0:T(8,128)S(1)}, u32[]{:S(2)}, u32[]{:S(2)}) %collective-permute-start.29) | collective-permute-done | bytes 98336 | tf_op jit(solution)/shard_map/ppermute | solution.py:50
  92.4 4.7 %errors.1 = (f32[2,32,128]{2,1,0:T(8,128)}, f32[32,512]{1,0:T(8,128)}, bf16[1,2,8192,128]{3,2,1,0:T(8,128)(2,1)}, bf16[1,4096,512]{2,1,0:T(8,128)(2,1)}) custom-call(bf16[2048,128]{1,0:T(8,128)(2,1)S(1)} %get-tuple-element.101.refs_6_.refs_0_, bf16[2048,128]{1,0:T(8,128)(2,1)S(1)} %get-tuple-element.102.refs_7_.refs_1_, ...), custom_call_target="tpu_custom_call" | custom-call | bytes 15000000 | tf_op jit(solution)/shard_map/errors/pallas_call | solution.py:398
  (38 shorter events, 0.4 us)
Async XLA Ops:
  4.4 3.6 %collective-permute-start.1 = (f32[4,32,640]{2,1,0:T(8,128)S(1)}, f32[4,32,640]{2,1,0:T(8,128)S(1)}, u32[]{:S(2)}, u32[]{:S(2)}) collective-permute-start(f32[4,32,640]{2,1,0:T(8,128)S(1)} %get-tuple-element.100), channel_id=1, source_target_pairs={{0,1},{1,0},{2,3},{3,2},{4,5},{5,4},{6,7},{7,6},{8,9},{9,8},{10,11... | collective-permute-start | bytes 983048 | tf_op jit(solution)/shard_map/ppermute | solution.py:50
  4.5 5.3 %collective-permute-start = (f32[4,32,640]{2,1,0:T(8,128)S(1)}, f32[4,32,640]{2,1,0:T(8,128)S(1)}, u32[]{:S(2)}, u32[]{:S(2)}) collective-permute-start(f32[4,32,640]{2,1,0:T(8,128)S(1)} %get-tuple-element.98), channel_id=1, source_target_pairs={{0,1},{1,0},{2,3},{3,2},{4,5},{5,4},{6,7},{7,6},{8,9},{9,8},{10,11... | collective-permute-start | bytes 983048 | tf_op jit(solution)/shard_map/ppermute | solution.py:50
  8.0 9.3 %collective-permute-start.2 = (f32[4,32,640]{2,1,0:T(8,128)S(1)}, f32[4,32,640]{2,1,0:T(8,128)S(1)}, u32[]{:S(2)}, u32[]{:S(2)}) collective-permute-start(f32[4,32,640]{2,1,0:T(8,128)S(1)} %add.61.refs_11_), channel_id=1, source_target_pairs={{0,32},{1,97},{2,34},{3,99},{4,36},{5,101},{6,38},{7,103},{8,40},{... | collective-permute-start | bytes 983048 | tf_op jit(solution)/shard_map/ppermute | solution.py:50
  9.8 8.9 %collective-permute-start.4 = (f32[4,32,640]{2,1,0:T(8,128)S(1)}, f32[4,32,640]{2,1,0:T(8,128)S(1)}, u32[]{:S(2)}, u32[]{:S(2)}) collective-permute-start(f32[4,32,640]{2,1,0:T(8,128)S(1)} %add.60.refs_10_), channel_id=1, source_target_pairs={{0,2},{1,7},{2,0},{3,5},{4,6},{5,3},{6,4},{7,1},{8,10},{9,15},{10,... | collective-permute-start | bytes 983048 | tf_op jit(solution)/shard_map/ppermute | solution.py:50
  14.9 3.8 %collective-permute-start.3 = (f32[4,32,640]{2,1,0:T(8,128)S(1)}, f32[4,32,640]{2,1,0:T(8,128)S(1)}, u32[]{:S(2)}, u32[]{:S(2)}) collective-permute-start(f32[4,32,640]{2,1,0:T(8,128)S(1)} %get-tuple-element.110), channel_id=1, source_target_pairs={{0,1},{1,0},{2,3},{3,2},{4,5},{5,4},{6,7},{7,6},{8,9},{9,8},{10,11... | collective-permute-start | bytes 983048 | tf_op jit(solution)/shard_map/ppermute | solution.py:50
  17.2 1.8 %collective-permute-start.15 = (f32[4,32,640]{2,1,0:T(8,128)S(1)}, f32[4,32,640]{2,1,0:T(8,128)S(1)}, u32[]{:S(2)}, u32[]{:S(2)}) collective-permute-start(f32[4,32,640]{2,1,0:T(8,128)S(1)} %get-tuple-element.115), channel_id=1, source_target_pairs={{0,1},{1,0},{2,3},{3,2},{4,5},{5,4},{6,7},{7,6},{8,9},{9,8},{10,11... | collective-permute-start | bytes 983048 | tf_op jit(solution)/shard_map/ppermute | solution.py:50
  18.8 5.4 %collective-permute-start.5 = (f32[2,32,640]{2,1,0:T(8,128)S(1)}, f32[2,32,640]{2,1,0:T(8,128)S(1)}, u32[]{:S(2)}, u32[]{:S(2)}) collective-permute-start(f32[2,32,640]{2,1,0:T(8,128)S(1)} %slice.33), channel_id=1, source_target_pairs={{0,32},{1,97},{2,34},{3,99},{4,36},{5,101},{6,38},{7,103},{8,40},{... | collective-permute-start | bytes 491528 | tf_op jit(solution)/shard_map/ppermute | solution.py:50
  19.1 7.1 %collective-permute-start.16 = (f32[2,32,640]{2,1,0:T(8,128)S(1)}, f32[2,32,640]{2,1,0:T(8,128)S(1)}, u32[]{:S(2)}, u32[]{:S(2)}) collective-permute-start(f32[2,32,640]{2,1,0:T(8,128)S(1)} %slice.37), channel_id=1, source_target_pairs={{0,8},{1,25},{2,10},{3,27},{4,12},{5,29},{6,14},{7,31},{8,0},{9,17... | collective-permute-start | bytes 491528 | tf_op jit(solution)/shard_map/ppermute | solution.py:50
  24.3 4.5 %collective-permute-start.6 = (f32[1,32,640]{2,1,0:T(8,128)S(1)}, f32[1,32,640]{2,1,0:T(8,128)S(1)}, u32[]{:S(2)}, u32[]{:S(2)}) collective-permute-start(f32[1,32,640]{2,1,0:T(8,128)S(1)} %slice.35), channel_id=1, source_target_pairs={{0,8},{1,25},{2,10},{3,27},{4,12},{5,29},{6,14},{7,31},{8,0},{9,17... | collective-permute-start | bytes 245768 | tf_op jit(solution)/shard_map/ppermute | solution.py:50
  26.3 4.5 %collective-permute-start.17 = (f32[1,32,640]{2,1,0:T(8,128)S(1)}, f32[1,32,640]{2,1,0:T(8,128)S(1)}, u32[]{:S(2)}, u32[]{:S(2)}) collective-permute-start(f32[1,32,640]{2,1,0:T(8,128)S(1)} %slice.39), channel_id=1, source_target_pairs={{0,2},{1,7},{2,0},{3,5},{4,6},{5,3},{6,4},{7,1},{8,10},{9,15},{10,... | collective-permute-start | bytes 245768 | tf_op jit(solution)/shard_map/ppermute | solution.py:50
  28.8 5.7 %collective-permute-start.7 = (f32[1,32,640]{2,1,0:T(8,128)S(1)}, f32[1,32,640]{2,1,0:T(8,128)S(1)}, u32[]{:S(2)}, u32[]{:S(2)}) collective-permute-start(f32[1,32,640]{2,1,0:T(8,128)S(1)} %slice_add_fusion.3), channel_id=1, source_target_pairs={{0,6},{1,3},{2,4},{3,1},{4,2},{5,7},{6,0},{7,5},{8,14},{9,11},{10,... | collective-permute-start | bytes 245768 | tf_op jit(solution)/shard_map/ppermute | solution.py:50
  30.9 5.7 %collective-permute-start.18 = (f32[1,32,640]{2,1,0:T(8,128)S(1)}, f32[1,32,640]{2,1,0:T(8,128)S(1)}, u32[]{:S(2)}, u32[]{:S(2)}) collective-permute-start(f32[1,32,640]{2,1,0:T(8,128)S(1)} %slice_add_fusion.2), channel_id=1, source_target_pairs={{0,96},{1,33},{2,98},{3,35},{4,100},{5,37},{6,102},{7,39},{8,104},... | collective-permute-start | bytes 245768 | tf_op jit(solution)/shard_map/ppermute | solution.py:50
  34.6 5.7 %collective-permute-start.8 = (f32[1,32,640]{2,1,0:T(8,128)S(1)}, f32[1,32,640]{2,1,0:T(8,128)S(1)}, u32[]{:S(2)}, u32[]{:S(2)}) collective-permute-start(f32[1,32,640]{2,1,0:T(8,128)S(1)} %add.66), channel_id=1, source_target_pairs={{0,96},{1,33},{2,98},{3,35},{4,100},{5,37},{6,102},{7,39},{8,104},... | collective-permute-start | bytes 245768 | tf_op jit(solution)/shard_map/ppermute | solution.py:50
  36.6 7.8 %collective-permute-start.19 = (f32[1,32,640]{2,1,0:T(8,128)S(1)}, f32[1,32,640]{2,1,0:T(8,128)S(1)}, u32[]{:S(2)}, u32[]{:S(2)}) collective-permute-start(f32[1,32,640]{2,1,0:T(8,128)S(1)} %add.73), channel_id=1, source_target_pairs={{0,24},{1,9},{2,26},{3,11},{4,28},{5,13},{6,30},{7,15},{8,16},{9,1... | collective-permute-start | bytes 245768 | tf_op jit(solution)/shard_map/ppermute | solution.py:50
  40.3 6.5 %collective-permute-start.9 = (f32[1,32,640]{2,1,0:T(8,128)S(1)}, f32[1,32,640]{2,1,0:T(8,128)S(1)}, u32[]{:S(2)}, u32[]{:S(2)}) collective-permute-start(f32[1,32,640]{2,1,0:T(8,128)S(1)} %add.67), channel_id=1, source_target_pairs={{0,24},{1,9},{2,26},{3,11},{4,28},{5,13},{6,30},{7,15},{8,16},{9,1... | collective-permute-start | bytes 245768 | tf_op jit(solution)/shard_map/ppermute | solution.py:50
  44.4 5.7 %collective-permute-start.20 = (f32[1,32,640]{2,1,0:T(8,128)S(1)}, f32[1,32,640]{2,1,0:T(8,128)S(1)}, u32[]{:S(2)}, u32[]{:S(2)}) collective-permute-start(f32[1,32,640]{2,1,0:T(8,128)S(1)} %add.74), channel_id=1, source_target_pairs={{0,6},{1,3},{2,4},{3,1},{4,2},{5,7},{6,0},{7,5},{8,14},{9,11},{10,... | collective-permute-start | bytes 245768 | tf_op jit(solution)/shard_map/ppermute | solution.py:50
  46.9 4.5 %collective-permute-start.10 = (f32[1,32,640]{2,1,0:T(8,128)S(1)}, f32[1,32,640]{2,1,0:T(8,128)S(1)}, u32[]{:S(2)}, u32[]{:S(2)}) collective-permute-start(f32[1,32,640]{2,1,0:T(8,128)S(1)} %add.68), channel_id=1, source_target_pairs={{0,8},{1,25},{2,10},{3,27},{4,12},{5,29},{6,14},{7,31},{8,0},{9,17... | collective-permute-start | bytes 245768 | tf_op jit(solution)/shard_map/ppermute | solution.py:50
  50.2 4.5 %collective-permute-start.21 = (f32[1,32,640]{2,1,0:T(8,128)S(1)}, f32[1,32,640]{2,1,0:T(8,128)S(1)}, u32[]{:S(2)}, u32[]{:S(2)}) collective-permute-start(f32[1,32,640]{2,1,0:T(8,128)S(1)} %add.75), channel_id=1, source_target_pairs={{0,2},{1,7},{2,0},{3,5},{4,6},{5,3},{6,4},{7,1},{8,10},{9,15},{10,... | collective-permute-start | bytes 245768 | tf_op jit(solution)/shard_map/ppermute | solution.py:50
  51.4 5.4 %collective-permute-start.11 = (f32[2,32,640]{2,1,0:T(8,128)S(1)}, f32[2,32,640]{2,1,0:T(8,128)S(1)}, u32[]{:S(2)}, u32[]{:S(2)}) collective-permute-start(f32[2,32,640]{2,1,0:T(8,128)S(1)} %pad_maximum_fusion.2), channel_id=1, source_target_pairs={{0,32},{1,97},{2,34},{3,99},{4,36},{5,101},{6,38},{7,103},{8,40},{... | collective-permute-start | bytes 491528 | tf_op jit(solution)/shard_map/ppermute | solution.py:50
  54.7 5.4 %collective-permute-start.22 = (f32[2,32,640]{2,1,0:T(8,128)S(1)}, f32[2,32,640]{2,1,0:T(8,128)S(1)}, u32[]{:S(2)}, u32[]{:S(2)}) collective-permute-start(f32[2,32,640]{2,1,0:T(8,128)S(1)} %pad_maximum_fusion.3), channel_id=1, source_target_pairs={{0,8},{1,25},{2,10},{3,27},{4,12},{5,29},{6,14},{7,31},{8,0},{9,17... | collective-permute-start | bytes 491528 | tf_op jit(solution)/shard_map/ppermute | solution.py:50
  56.8 7.2 %collective-permute-start.13 = (f32[4,32,640]{2,1,0:T(8,128)S(1)}, f32[4,32,640]{2,1,0:T(8,128)S(1)}, u32[]{:S(2)}, u32[]{:S(2)}) collective-permute-start(f32[4,32,640]{2,1,0:T(8,128)S(1)} %pad_maximum_fusion.refs_4_.refs_0_), channel_id=1, source_target_pairs={{0,2},{1,7},{2,0},{3,5},{4,6},{5,3},{6,4},{7,1},{8,10},{9,15},{10,... | collective-permute-start | bytes 983048 | tf_op jit(solution)/shard_map/ppermute | solution.py:50
  57.8 4.2 %collective-permute-start.12 = (f32[4,32,640]{2,1,0:T(8,128)S(1)}, f32[4,32,640]{2,1,0:T(8,128)S(1)}, u32[]{:S(2)}, u32[]{:S(2)}) collective-permute-start(f32[4,32,640]{2,1,0:T(8,128)S(1)} %pad_maximum_fusion.refs_4_.refs_0_), channel_id=1, source_target_pairs={{0,1},{1,0},{2,3},{3,2},{4,5},{5,4},{6,7},{7,6},{8,9},{9,8},{10,11... | collective-permute-start | bytes 983048 | tf_op jit(solution)/shard_map/ppermute | solution.py:50
  60.1 3.8 %collective-permute-start.23 = (f32[4,32,640]{2,1,0:T(8,128)S(1)}, f32[4,32,640]{2,1,0:T(8,128)S(1)}, u32[]{:S(2)}, u32[]{:S(2)}) collective-permute-start(f32[4,32,640]{2,1,0:T(8,128)S(1)} %pad_maximum_fusion.1.refs_4_.refs_2_), channel_id=1, source_target_pairs={{0,1},{1,0},{2,3},{3,2},{4,5},{5,4},{6,7},{7,6},{8,9},{9,8},{10,11... | collective-permute-start | bytes 983048 | tf_op jit(solution)/shard_map/ppermute | solution.py:50
  60.2 7.3 %collective-permute-start.24 = (f32[4,32,640]{2,1,0:T(8,128)S(1)}, f32[4,32,640]{2,1,0:T(8,128)S(1)}, u32[]{:S(2)}, u32[]{:S(2)}) collective-permute-start(f32[4,32,640]{2,1,0:T(8,128)S(1)} %pad_maximum_fusion.1.refs_4_.refs_2_), channel_id=1, source_target_pairs={{0,32},{1,97},{2,34},{3,99},{4,36},{5,101},{6,38},{7,103},{8,40},{... | collective-permute-start | bytes 983048 | tf_op jit(solution)/shard_map/ppermute | solution.py:50
  64.0 5.4 %collective-permute-start.14 = (f32[4,32,640]{2,1,0:T(8,128)S(1)}, f32[4,32,640]{2,1,0:T(8,128)S(1)}, u32[]{:S(2)}, u32[]{:S(2)}) collective-permute-start(f32[4,32,640]{2,1,0:T(8,128)S(1)} %collective-permute-done.13.refs_4_.refs_1_), channel_id=1, source_target_pairs={{0,1},{1,0},{2,3},{3,2},{4,5},{5,4},{6,7},{7,6},{8,9},{9,8},{10,11... | collective-permute-start | bytes 983048 | tf_op jit(solution)/shard_map/ppermute | solution.py:50
  67.6 2.6 %collective-permute-start.25 = (f32[4,32,640]{2,1,0:T(8,128)S(1)}, f32[4,32,640]{2,1,0:T(8,128)S(1)}, u32[]{:S(2)}, u32[]{:S(2)}) collective-permute-start(f32[4,32,640]{2,1,0:T(8,128)S(1)} %collective-permute-done.24.refs_4_.refs_3_), channel_id=1, source_target_pairs={{0,1},{1,0},{2,3},{3,2},{4,5},{5,4},{6,7},{7,6},{8,9},{9,8},{10,11... | collective-permute-start | bytes 983048 | tf_op jit(solution)/shard_map/ppermute | solution.py:50
  70.9 4.7 %collective-permute-start.26 = (f32[32,768]{1,0:T(8,128)S(1)}, f32[32,768]{1,0:T(8,128)S(1)}, u32[]{:S(2)}, u32[]{:S(2)}) collective-permute-start(f32[32,768]{1,0:T(8,128)S(1)} %get-tuple-element.142), channel_id=1, source_target_pairs={{0,32},{1,9},{2,34},{3,11},{4,36},{5,13},{6,38},{7,15},{8,40},{9,1... | collective-permute-start | bytes 294920 | tf_op jit(solution)/shard_map/ppermute | solution.py:50
  75.6 4.7 %collective-permute-start.27 = (f32[32,768]{1,0:T(8,128)S(1)}, f32[32,768]{1,0:T(8,128)S(1)}, u32[]{:S(2)}, u32[]{:S(2)}) collective-permute-start(f32[32,768]{1,0:T(8,128)S(1)} %add.76), channel_id=1, source_target_pairs={{0,8},{1,33},{2,10},{3,35},{4,12},{5,37},{6,14},{7,39},{8,0},{9,41... | collective-permute-start | bytes 294920 | tf_op jit(solution)/shard_map/ppermute | solution.py:50
  80.3 5.9 %collective-permute-start.28 = (f32[32,768]{1,0:T(8,128)S(1)}, f32[32,768]{1,0:T(8,128)S(1)}, u32[]{:S(2)}, u32[]{:S(2)}) collective-permute-start(f32[32,768]{1,0:T(8,128)S(1)} %add.77), channel_id=1, source_target_pairs={{0,96},{1,25},{2,98},{3,27},{4,100},{5,29},{6,102},{7,31},{8,104},... | collective-permute-start | bytes 294920 | tf_op jit(solution)/shard_map/ppermute | solution.py:50
  86.3 6.1 %collective-permute-start.29 = (f32[32,768]{1,0:T(8,128)S(1)}, f32[32,768]{1,0:T(8,128)S(1)}, u32[]{:S(2)}, u32[]{:S(2)}) collective-permute-start(f32[32,768]{1,0:T(8,128)S(1)} %add.78), channel_id=1, source_target_pairs={{0,24},{1,97},{2,26},{3,99},{4,28},{5,101},{6,30},{7,103},{8,16},{... | collective-permute-start | bytes 294920 | tf_op jit(solution)/shard_map/ppermute | solution.py:50

commit v6 on v5

--- a/solution.py
+++ b/solution.py
@@ -243,10 +243,10 @@
         right[...] = sums
 
 
-def right_part(chain, group, bufs, lead, before=(), keys=None):
+def right_part(chain, group, bufs, lead, before=(), keys=None, after=()):
     last = keys is not None
     width = 2 * COLS + OCOLS if last else COLS + OCOLS
-    operands = (*bufs[chain, group], lead, *before, *([keys] if last else []))
+    operands = (*bufs[chain, group], lead, *before, *([keys] if last else []), *after)
     return pl.pallas_call(
         functools.partial(right_kernel, chain, group, len(before), last),
         out_shape=(
@@ -448,9 +448,12 @@
     for s in range(2):
         sum1, gram1 = right_part(s, near0, bufs, own0[s])
         sum2, gram2 = right_part(s, far0, bufs, other0[s])
-        own1[s], sum1, sum2 = lax.optimization_barrier((own1[s], sum1, sum2))
+        if s == 0:
+            own1[s], sum1, sum2 = lax.optimization_barrier((own1[s], sum1, sum2))
+        else:
+            own1[s], sum1, sum2, sum3 = lax.optimization_barrier((own1[s], sum1, sum2, sum3))
         other1.append(send(own1[s], CORES))
-        sum3, gram3 = right_part(s, near1, bufs, own1[s])
+        sum3, gram3 = right_part(s, near1, bufs, own1[s], after=() if s == 0 else (total,))
         total, gram4 = right_part(s, far1, bufs, other1[s], (sum1, sum2, sum3), total)
         grams += [gram1, gram3, gram2, gram4]
     own = (own0[0], own1[0], own0[1], own1[1])

time: 97.5 us -> 96.7 us (level)
  waiting for transfers between devices: 38.9 us -> 37.2 us
    ppermute x30, waiting for transfers between devices: 38.9 us -> 37.2 us  [send(): return lax.ppermute(x, ('dp', 'mp'), to)]
where the time goes in v6:
time: 96.7 us; the launch traced here: 96.5 us
  waiting for transfers between devices  37.2 us (38%)
  Pallas kernels  29.2 us (30%)
  starting transfers between devices  28.5 us (29%)
  between operations  1.11 us (1%)
    ppermute x30, waiting for transfers between devices, send(): return lax.ppermute(x, ('dp', 'mp'), to)  37.2 us
    ppermute x30, starting transfers between devices, send(): return lax.ppermute(x, ('dp', 'mp'), to)  28.5 us
    pallas_call x4, Pallas kernels, part(): pl.pallas_call(functools.partial(part_kernel, group, given, ahead, len(af...  11.7 us
    pallas_call x8, Pallas kernels, right_part(): pl.pallas_call(functools.partial(right_kernel, chain, group, len(before),...  6.07 us
    pallas_call x1, Pallas kernels, errors(): pl.pallas_call(error_kernel, out_shape=(jax.ShapeDtypeStruct((2, RANK, CO...  4.72 us
    pallas_call x2, Pallas kernels, left_part(): pl.pallas_call(functools.partial(left_kernel, dh), out_shape=(jax.ShapeDt...  3.91 us
    pallas_call x1, Pallas kernels, factor(): pl.pallas_call(factor_kernel, out_shape=jax.ShapeDtypeStruct((3, RANK, RA...  2.87 us
  transfers between devices with their start and end apart: 30, of which 18 were waited for; matrix products, arithmetic and copies ran while one was open for 0% of the time, Pallas kernels for 21%

profile of v6, /device:TPU:0, one launch (start us, length us, event | category | flops | bytes accessed | tf_op | source)
XLA Modules:
  0.0 96.5 jit_solution(13676487128740469864)
XLA Ops:
  0.6 3.8 %part.4 = (f32[4,32,640]{2,1,0:T(8,128)S(1)}, f32[4,32,640]{2,1,0:T(8,128)S(1)}, bf16[2048,128]{1,0:T(8,128)(2,1)S(1)}, bf16[2048,128]{1,0:T(8,128)(2,1)S(1)}, b...) custom-call(bf16[1,2,8192,128]{3,2,1,0:T(8,128)(2,1)} %refs_0_.7, ...), custom_call_target="tpu_custom_call" | custom-call | bytes 9000000 | tf_op jit(solution)/shard_map/part/pallas_call | solution.py:181
  4.4 0.1 collective-permute-start.1
  4.5 0.5 collective-permute-start
  5.0 3.0 %part.5 = (f32[4,32,640]{2,1,0:T(8,128)S(1)}, f32[4,32,640]{2,1,0:T(8,128)S(1)}, bf16[2048,128]{1,0:T(8,128)(2,1)S(1)}, bf16[2048,128]{1,0:T(8,128)(2,1)S(1)}, b...) custom-call(bf16[1,2,8192,128]{3,2,1,0:T(8,128)(2,1)} %refs_0_.7, ...), custom_call_target="tpu_custom_call" | custom-call | bytes 9000000 | tf_op jit(solution)/shard_map/part/pallas_call | solution.py:181
  8.0 1.7 %collective-permute-start.2 = (f32[4,32,640]{2,1,0:T(8,128)S(1)}, f32[4,32,640]{2,1,0:T(8,128)S(1)}, u32[]{:S(2)}, u32[]{:S(2)}) collective-permute-start(f32[4,32,640]{2,1,0:T(8,128)S(1)} %add.61.refs_11_), channel_id=1, source_target_pairs={{0,32},{1,97},{2,34},{3,99},{4,36},{5,101},{6,38},{7,103},{8,40},{... | collective-permute-start | bytes 983048 | tf_op jit(solution)/shard_map/ppermute | solution.py:50
  9.8 1.6 %collective-permute-start.4 = (f32[4,32,640]{2,1,0:T(8,128)S(1)}, f32[4,32,640]{2,1,0:T(8,128)S(1)}, u32[]{:S(2)}, u32[]{:S(2)}) collective-permute-start(f32[4,32,640]{2,1,0:T(8,128)S(1)} %add.60.refs_10_), channel_id=1, source_target_pairs={{0,2},{1,7},{2,0},{3,5},{4,6},{5,3},{6,4},{7,1},{8,10},{9,15},{10,... | collective-permute-start | bytes 983048 | tf_op jit(solution)/shard_map/ppermute | solution.py:50
  11.4 3.5 %part.6 = (f32[4,32,640]{2,1,0:T(8,128)S(1)}, f32[4,32,640]{2,1,0:T(8,128)S(1)}, bf16[2048,128]{1,0:T(8,128)(2,1)S(1)}, bf16[2048,128]{1,0:T(8,128)(2,1)S(1)}, b...) custom-call(bf16[1,2,8192,128]{3,2,1,0:T(8,128)(2,1)} %refs_0_.7, ...), custom_call_target="tpu_custom_call" | custom-call | bytes 9000000 | tf_op jit(solution)/shard_map/part/pallas_call | solution.py:181
  14.9 2.3 %collective-permute-start.3 = (f32[4,32,640]{2,1,0:T(8,128)S(1)}, f32[4,32,640]{2,1,0:T(8,128)S(1)}, u32[]{:S(2)}, u32[]{:S(2)}) collective-permute-start(f32[4,32,640]{2,1,0:T(8,128)S(1)} %get-tuple-element.110), channel_id=1, source_target_pairs={{0,1},{1,0},{2,3},{3,2},{4,5},{5,4},{6,7},{7,6},{8,9},{9,8},{10,11... | collective-permute-start | bytes 983048 | tf_op jit(solution)/shard_map/ppermute | solution.py:50
  17.2 0.1 collective-permute-start.15
  17.3 1.4 %part.7 = (f32[4,32,640]{2,1,0:T(8,128)S(1)}, f32[4,32,640]{2,1,0:T(8,128)S(1)}) custom-call(bf16[1,2,8192,128]{3,2,1,0:T(8,128)(2,1)} %refs_0_.7, bf16[1,2,8192,128]{3,2,1,0:T(8,128)(2,1)} %refs_1_.7, bf16[1,4096,512]{2,1,0:T(8,128)(2,1)} %refs_2_.7, bf16[1,4096,512]{2,1,0:T(8,128)(2,1)} %refs_3_.7, bf16[2,96,256]{2,1,0:T(8,128)(2,1)S(1)} %get-tuple-element.87.refs_4_, ...), custom_call_target="tpu_custom_call" | custom-call | bytes 9000000 | tf_op jit(solution)/shard_map/part/pallas_call | solution.py:181
  18.8 0.1 add_add_fusion.1
  18.8 0.2 collective-permute-start.5
  19.1 2.0 %collective-permute-start.16 = (f32[2,32,640]{2,1,0:T(8,128)S(1)}, f32[2,32,640]{2,1,0:T(8,128)S(1)}, u32[]{:S(2)}, u32[]{:S(2)}) collective-permute-start(f32[2,32,640]{2,1,0:T(8,128)S(1)} %slice.37), channel_id=1, source_target_pairs={{0,8},{1,25},{2,10},{3,27},{4,12},{5,29},{6,14},{7,31},{8,0},{9,17... | collective-permute-start | bytes 491528 | tf_op jit(solution)/shard_map/ppermute | solution.py:50
  21.1 3.1 %collective-permute-done.5 = f32[2,32,640]{2,1,0:T(8,128)S(1)} collective-permute-done((f32[2,32,640]{2,1,0:T(8,128)S(1)}, f32[2,32,640]{2,1,0:T(8,128)S(1)}, u32[]{:S(2)}, u32[]{:S(2)}) %collective-permute-start.5) | collective-permute-done | bytes 163872 | tf_op jit(solution)/shard_map/ppermute | solution.py:50
  24.3 2.0 %collective-permute-start.6 = (f32[1,32,640]{2,1,0:T(8,128)S(1)}, f32[1,32,640]{2,1,0:T(8,128)S(1)}, u32[]{:S(2)}, u32[]{:S(2)}) collective-permute-start(f32[1,32,640]{2,1,0:T(8,128)S(1)} %slice.35), channel_id=1, source_target_pairs={{0,8},{1,25},{2,10},{3,27},{4,12},{5,29},{6,14},{7,31},{8,0},{9,17... | collective-permute-start | bytes 245768 | tf_op jit(solution)/shard_map/ppermute | solution.py:50
  26.3 0.3 collective-permute-start.17
  26.6 2.2 %collective-permute-done.6 = f32[1,32,640]{2,1,0:T(8,128)S(1)} collective-permute-done((f32[1,32,640]{2,1,0:T(8,128)S(1)}, f32[1,32,640]{2,1,0:T(8,128)S(1)}, u32[]{:S(2)}, u32[]{:S(2)}) %collective-permute-start.6) | collective-permute-done | bytes 81952 | tf_op jit(solution)/shard_map/ppermute | solution.py:50
  28.8 1.1 %collective-permute-start.7 = (f32[1,32,640]{2,1,0:T(8,128)S(1)}, f32[1,32,640]{2,1,0:T(8,128)S(1)}, u32[]{:S(2)}, u32[]{:S(2)}) collective-permute-start(f32[1,32,640]{2,1,0:T(8,128)S(1)} %slice_add_fusion.3), channel_id=1, source_target_pairs={{0,6},{1,3},{2,4},{3,1},{4,2},{5,7},{6,0},{7,5},{8,14},{9,11},{10,... | collective-permute-start | bytes 245768 | tf_op jit(solution)/shard_map/ppermute | solution.py:50
  29.9 1.0 %collective-permute-done.17 = f32[1,32,640]{2,1,0:T(8,128)S(1)} collective-permute-done((f32[1,32,640]{2,1,0:T(8,128)S(1)}, f32[1,32,640]{2,1,0:T(8,128)S(1)}, u32[]{:S(2)}, u32[]{:S(2)}) %collective-permute-start.17) | collective-permute-done | bytes 81952 | tf_op jit(solution)/shard_map/ppermute | solution.py:50
  30.9 1.9 %collective-permute-start.18 = (f32[1,32,640]{2,1,0:T(8,128)S(1)}, f32[1,32,640]{2,1,0:T(8,128)S(1)}, u32[]{:S(2)}, u32[]{:S(2)}) collective-permute-start(f32[1,32,640]{2,1,0:T(8,128)S(1)} %slice_add_fusion.2), channel_id=1, source_target_pairs={{0,96},{1,33},{2,98},{3,35},{4,100},{5,37},{6,102},{7,39},{8,104},... | collective-permute-start | bytes 245768 | tf_op jit(solution)/shard_map/ppermute | solution.py:50
  32.7 1.8 %collective-permute-done.7 = f32[1,32,640]{2,1,0:T(8,128)S(1)} collective-permute-done((f32[1,32,640]{2,1,0:T(8,128)S(1)}, f32[1,32,640]{2,1,0:T(8,128)S(1)}, u32[]{:S(2)}, u32[]{:S(2)}) %collective-permute-start.7) | collective-permute-done | bytes 81952 | tf_op jit(solution)/shard_map/ppermute | solution.py:50
  34.6 1.0 %collective-permute-start.8 = (f32[1,32,640]{2,1,0:T(8,128)S(1)}, f32[1,32,640]{2,1,0:T(8,128)S(1)}, u32[]{:S(2)}, u32[]{:S(2)}) collective-permute-start(f32[1,32,640]{2,1,0:T(8,128)S(1)} %add.66), channel_id=1, source_target_pairs={{0,96},{1,33},{2,98},{3,35},{4,100},{5,37},{6,102},{7,39},{8,104},... | collective-permute-start | bytes 245768 | tf_op jit(solution)/shard_map/ppermute | solution.py:50
  35.6 1.0 %collective-permute-done.18 = f32[1,32,640]{2,1,0:T(8,128)S(1)} collective-permute-done((f32[1,32,640]{2,1,0:T(8,128)S(1)}, f32[1,32,640]{2,1,0:T(8,128)S(1)}, u32[]{:S(2)}, u32[]{:S(2)}) %collective-permute-start.18) | collective-permute-done | bytes 81952 | tf_op jit(solution)/shard_map/ppermute | solution.py:50
  36.6 3.1 %collective-permute-start.19 = (f32[1,32,640]{2,1,0:T(8,128)S(1)}, f32[1,32,640]{2,1,0:T(8,128)S(1)}, u32[]{:S(2)}, u32[]{:S(2)}) collective-permute-start(f32[1,32,640]{2,1,0:T(8,128)S(1)} %add.73), channel_id=1, source_target_pairs={{0,24},{1,9},{2,26},{3,11},{4,28},{5,13},{6,30},{7,15},{8,16},{9,1... | collective-permute-start | bytes 245768 | tf_op jit(solution)/shard_map/ppermute | solution.py:50
  39.8 0.5 collective-permute-done.8
  40.3 4.1 %collective-permute-start.9 = (f32[1,32,640]{2,1,0:T(8,128)S(1)}, f32[1,32,640]{2,1,0:T(8,128)S(1)}, u32[]{:S(2)}, u32[]{:S(2)}) collective-permute-start(f32[1,32,640]{2,1,0:T(8,128)S(1)} %add.67), channel_id=1, source_target_pairs={{0,24},{1,9},{2,26},{3,11},{4,28},{5,13},{6,30},{7,15},{8,16},{9,1... | collective-permute-start | bytes 245768 | tf_op jit(solution)/shard_map/ppermute | solution.py:50
  44.4 1.1 %collective-permute-start.20 = (f32[1,32,640]{2,1,0:T(8,128)S(1)}, f32[1,32,640]{2,1,0:T(8,128)S(1)}, u32[]{:S(2)}, u32[]{:S(2)}) collective-permute-start(f32[1,32,640]{2,1,0:T(8,128)S(1)} %add.74), channel_id=1, source_target_pairs={{0,6},{1,3},{2,4},{3,1},{4,2},{5,7},{6,0},{7,5},{8,14},{9,11},{10,... | collective-permute-start | bytes 245768 | tf_op jit(solution)/shard_map/ppermute | solution.py:50
  45.5 1.3 %collective-permute-done.9 = f32[1,32,640]{2,1,0:T(8,128)S(1)} collective-permute-done((f32[1,32,640]{2,1,0:T(8,128)S(1)}, f32[1,32,640]{2,1,0:T(8,128)S(1)}, u32[]{:S(2)}, u32[]{:S(2)}) %collective-permute-start.9) | collective-permute-done | bytes 81952 | tf_op jit(solution)/shard_map/ppermute | solution.py:50
  46.9 0.1 collective-permute-start.10
  46.9 3.2 %collective-permute-done.20 = f32[1,32,640]{2,1,0:T(8,128)S(1)} collective-permute-done((f32[1,32,640]{2,1,0:T(8,128)S(1)}, f32[1,32,640]{2,1,0:T(8,128)S(1)}, u32[]{:S(2)}, u32[]{:S(2)}) %collective-permute-start.20) | collective-permute-done | bytes 81952 | tf_op jit(solution)/shard_map/ppermute | solution.py:50
  50.2 0.1 collective-permute-start.21
  50.3 1.1 %collective-permute-done.10 = f32[1,32,640]{2,1,0:T(8,128)S(1)} collective-permute-done((f32[1,32,640]{2,1,0:T(8,128)S(1)}, f32[1,32,640]{2,1,0:T(8,128)S(1)}, u32[]{:S(2)}, u32[]{:S(2)}) %collective-permute-start.10) | collective-permute-done | bytes 81952 | tf_op jit(solution)/shard_map/ppermute | solution.py:50
  51.4 0.1 collective-permute-start.11
  51.5 3.2 %collective-permute-done.21 = f32[1,32,640]{2,1,0:T(8,128)S(1)} collective-permute-done((f32[1,32,640]{2,1,0:T(8,128)S(1)}, f32[1,32,640]{2,1,0:T(8,128)S(1)}, u32[]{:S(2)}, u32[]{:S(2)}) %collective-permute-start.21) | collective-permute-done | bytes 81952 | tf_op jit(solution)/shard_map/ppermute | solution.py:50
  54.7 0.1 collective-permute-start.22
  54.8 2.0 %collective-permute-done.11 = f32[2,32,640]{2,1,0:T(8,128)S(1)} collective-permute-done((f32[2,32,640]{2,1,0:T(8,128)S(1)}, f32[2,32,640]{2,1,0:T(8,128)S(1)}, u32[]{:S(2)}, u32[]{:S(2)}) %collective-permute-start.11) | collective-permute-done | bytes 163872 | tf_op jit(solution)/shard_map/ppermute | solution.py:50
  56.8 1.0 %collective-permute-start.13 = (f32[4,32,640]{2,1,0:T(8,128)S(1)}, f32[4,32,640]{2,1,0:T(8,128)S(1)}, u32[]{:S(2)}, u32[]{:S(2)}) collective-permute-start(f32[4,32,640]{2,1,0:T(8,128)S(1)} %pad_maximum_fusion.refs_4_.refs_0_), channel_id=1, source_target_pairs={{0,2},{1,7},{2,0},{3,5},{4,6},{5,3},{6,4},{7,1},{8,10},{9,15},{10,... | collective-permute-start | bytes 983048 | tf_op jit(solution)/shard_map/ppermute | solution.py:50
  57.8 2.3 %collective-permute-done.22 = f32[2,32,640]{2,1,0:T(8,128)S(1)} collective-permute-done((f32[2,32,640]{2,1,0:T(8,128)S(1)}, f32[2,32,640]{2,1,0:T(8,128)S(1)}, u32[]{:S(2)}, u32[]{:S(2)}) %collective-permute-start.22) | collective-permute-done | bytes 163872 | tf_op jit(solution)/shard_map/ppermute | solution.py:50
  60.1 0.1 collective-permute-start.23
  60.2 0.3 collective-permute-start.24
  60.5 0.8 right.10
  61.3 0.8 right.8
  62.0 0.8 right.9
  62.8 1.2 %collective-permute-done.13.refs_4_.refs_1_ = f32[4,32,640]{2,1,0:T(8,128)S(1)} collective-permute-done((f32[4,32,640]{2,1,0:T(8,128)S(1)}, f32[4,32,640]{2,1,0:T(8,128)S(1)}, u32[]{:S(2)}, u32[]{:S(2)}) %collective-permute-start.13) | collective-permute-done | bytes 327712 | tf_op jit(solution)/shard_map/ppermute | solution.py:50
  64.0 0.7 right.12
  64.7 0.1 collective-permute-start.14
  64.8 0.8 right.11
  65.6 2.0 %collective-permute-done.24.refs_4_.refs_3_ = f32[4,32,640]{2,1,0:T(8,128)S(1)} collective-permute-done((f32[4,32,640]{2,1,0:T(8,128)S(1)}, f32[4,32,640]{2,1,0:T(8,128)S(1)}, u32[]{:S(2)}, u32[]{:S(2)}) %collective-permute-start.24) | collective-permute-done | bytes 327712 | tf_op jit(solution)/shard_map/ppermute | solution.py:50
  67.6 0.3 collective-permute-start.25
  67.9 0.7 right.13
  68.6 0.8 right.14
  69.4 0.8 right.15
  70.1 0.1 collective-permute-start.26
  70.2 2.9 %factor.1.refs_4_.refs_33_ = f32[3,32,32]{2,1,0:T(8,128)S(1)} custom-call(f32[2,32,32]{2,1,0:T(8,128)S(1)} %get-tuple-element.143.a0, f32[2,32,32]{2,1,0:T(8,128)S(1)} %get-tuple-element.144.a1, f32[2,32,32]{2,1,0:T(8,128)S(1)} %get-tuple-element.145.a2, f32[2,32,32]{2,1,0:T(8,128)S(1)} %get-tuple-element.146.a3, f32[2,32,32]{2,1,0:T(8,128)S(1)} %get-tuple-element.147.b0, ...), custom_call_target="tpu_custom_call" | custom-call | bytes 12000000 | tf_op jit(solution)/shard_map/factor/pallas_call | solution.py:286
  73.1 1.7 %collective-permute-done.26 = f32[32,768]{1,0:T(8,128)S(1)} collective-permute-done((f32[32,768]{1,0:T(8,128)S(1)}, f32[32,768]{1,0:T(8,128)S(1)}, u32[]{:S(2)}, u32[]{:S(2)}) %collective-permute-start.26) | collective-permute-done | bytes 98336 | tf_op jit(solution)/shard_map/ppermute | solution.py:50
  74.9 0.1 collective-permute-start.27
  74.9 2.0 %left.2 = (f32[2,32,8192]{2,1,0:T(8,128)}, f32[32,4096]{1,0:T(8,128)}, bf16[2,2,4,640,128]{4,3,2,1,0:T(8,128)(2,1)S(1)}) custom-call(f32[4,32,640]{2,1,0:T(8,128)S(1)} %pad_maximum_fusion.refs_4_.refs_0_, f32[4,32,640]{2,1,0:T(8,128)S(1)} %collective-permute-done.13.refs_4_.refs_1_, f32[4,32,640]{2,1,0:T(8,128)S(1)} %pad_maximum_fusion.1.refs_4_.refs_2_, ...), custom_call_target="tpu_custom_call" | custom-call | bytes 6000000 | tf_op jit(solution)/shard_map/left/pallas_call | solution.py:336
  76.9 2.6 %collective-permute-done.27 = f32[32,768]{1,0:T(8,128)S(1)} collective-permute-done((f32[32,768]{1,0:T(8,128)S(1)}, f32[32,768]{1,0:T(8,128)S(1)}, u32[]{:S(2)}, u32[]{:S(2)}) %collective-permute-start.27) | collective-permute-done | bytes 98336 | tf_op jit(solution)/shard_map/ppermute | solution.py:50
  79.6 1.0 %collective-permute-start.28 = (f32[32,768]{1,0:T(8,128)S(1)}, f32[32,768]{1,0:T(8,128)S(1)}, u32[]{:S(2)}, u32[]{:S(2)}) collective-permute-start(f32[32,768]{1,0:T(8,128)S(1)} %add.77), channel_id=1, source_target_pairs={{0,96},{1,25},{2,98},{3,27},{4,100},{5,29},{6,102},{7,31},{8,104},... | collective-permute-start | bytes 294920 | tf_op jit(solution)/shard_map/ppermute | solution.py:50
  80.6 2.0 %left.3 = (f32[2,32,8192]{2,1,0:T(8,128)}, f32[32,4096]{1,0:T(8,128)}, bf16[2,2,4,640,128]{4,3,2,1,0:T(8,128)(2,1)S(1)}) custom-call(f32[4,32,640]{2,1,0:T(8,128)S(1)} %collective-permute-done.12.refs_4_.refs_0_, f32[4,32,640]{2,1,0:T(8,128)S(1)} %collective-permute-done.14.refs_4_.refs_1_, ...), custom_call_target="tpu_custom_call", output_to_operand_aliasing={{0}: (5, {}), {1}: (6, {})} | custom-call | bytes 6000000 | tf_op jit(solution)/shard_map/left/pallas_call | solution.py:336
  82.6 2.9 %collective-permute-done.28 = f32[32,768]{1,0:T(8,128)S(1)} collective-permute-done((f32[32,768]{1,0:T(8,128)S(1)}, f32[32,768]{1,0:T(8,128)S(1)}, u32[]{:S(2)}, u32[]{:S(2)}) %collective-permute-start.28) | collective-permute-done | bytes 98336 | tf_op jit(solution)/shard_map/ppermute | solution.py:50
  85.5 2.1 %collective-permute-start.29 = (f32[32,768]{1,0:T(8,128)S(1)}, f32[32,768]{1,0:T(8,128)S(1)}, u32[]{:S(2)}, u32[]{:S(2)}) collective-permute-start(f32[32,768]{1,0:T(8,128)S(1)} %add.78), channel_id=1, source_target_pairs={{0,24},{1,97},{2,26},{3,99},{4,28},{5,101},{6,30},{7,103},{8,16},{... | collective-permute-start | bytes 294920 | tf_op jit(solution)/shard_map/ppermute | solution.py:50
  87.6 4.1 %collective-permute-done.29 = f32[32,768]{1,0:T(8,128)S(1)} collective-permute-done((f32[32,768]{1,0:T(8,128)S(1)}, f32[32,768]{1,0:T(8,128)S(1)}, u32[]{:S(2)}, u32[]{:S(2)}) %collective-permute-start.29) | collective-permute-done | bytes 98336 | tf_op jit(solution)/shard_map/ppermute | solution.py:50
  91.6 4.7 %errors.1 = (f32[2,32,128]{2,1,0:T(8,128)}, f32[32,512]{1,0:T(8,128)}, bf16[1,2,8192,128]{3,2,1,0:T(8,128)(2,1)}, bf16[1,4096,512]{2,1,0:T(8,128)(2,1)}) custom-call(bf16[2048,128]{1,0:T(8,128)(2,1)S(1)} %get-tuple-element.101.refs_6_.refs_0_, bf16[2048,128]{1,0:T(8,128)(2,1)S(1)} %get-tuple-element.102.refs_7_.refs_1_, ...), custom_call_target="tpu_custom_call" | custom-call | bytes 15000000 | tf_op jit(solution)/shard_map/errors/pallas_call | solution.py:398
  (38 shorter events, 0.4 us)
Async XLA Ops:
  4.4 3.6 %collective-permute-start.1 = (f32[4,32,640]{2,1,0:T(8,128)S(1)}, f32[4,32,640]{2,1,0:T(8,128)S(1)}, u32[]{:S(2)}, u32[]{:S(2)}) collective-permute-start(f32[4,32,640]{2,1,0:T(8,128)S(1)} %get-tuple-element.100), channel_id=1, source_target_pairs={{0,1},{1,0},{2,3},{3,2},{4,5},{5,4},{6,7},{7,6},{8,9},{9,8},{10,11... | collective-permute-start | bytes 983048 | tf_op jit(solution)/shard_map/ppermute | solution.py:50
  4.5 5.3 %collective-permute-start = (f32[4,32,640]{2,1,0:T(8,128)S(1)}, f32[4,32,640]{2,1,0:T(8,128)S(1)}, u32[]{:S(2)}, u32[]{:S(2)}) collective-permute-start(f32[4,32,640]{2,1,0:T(8,128)S(1)} %get-tuple-element.98), channel_id=1, source_target_pairs={{0,1},{1,0},{2,3},{3,2},{4,5},{5,4},{6,7},{7,6},{8,9},{9,8},{10,11... | collective-permute-start | bytes 983048 | tf_op jit(solution)/shard_map/ppermute | solution.py:50
  8.0 9.3 %collective-permute-start.2 = (f32[4,32,640]{2,1,0:T(8,128)S(1)}, f32[4,32,640]{2,1,0:T(8,128)S(1)}, u32[]{:S(2)}, u32[]{:S(2)}) collective-permute-start(f32[4,32,640]{2,1,0:T(8,128)S(1)} %add.61.refs_11_), channel_id=1, source_target_pairs={{0,32},{1,97},{2,34},{3,99},{4,36},{5,101},{6,38},{7,103},{8,40},{... | collective-permute-start | bytes 983048 | tf_op jit(solution)/shard_map/ppermute | solution.py:50
  9.8 8.9 %collective-permute-start.4 = (f32[4,32,640]{2,1,0:T(8,128)S(1)}, f32[4,32,640]{2,1,0:T(8,128)S(1)}, u32[]{:S(2)}, u32[]{:S(2)}) collective-permute-start(f32[4,32,640]{2,1,0:T(8,128)S(1)} %add.60.refs_10_), channel_id=1, source_target_pairs={{0,2},{1,7},{2,0},{3,5},{4,6},{5,3},{6,4},{7,1},{8,10},{9,15},{10,... | collective-permute-start | bytes 983048 | tf_op jit(solution)/shard_map/ppermute | solution.py:50
  14.9 3.8 %collective-permute-start.3 = (f32[4,32,640]{2,1,0:T(8,128)S(1)}, f32[4,32,640]{2,1,0:T(8,128)S(1)}, u32[]{:S(2)}, u32[]{:S(2)}) collective-permute-start(f32[4,32,640]{2,1,0:T(8,128)S(1)} %get-tuple-element.110), channel_id=1, source_target_pairs={{0,1},{1,0},{2,3},{3,2},{4,5},{5,4},{6,7},{7,6},{8,9},{9,8},{10,11... | collective-permute-start | bytes 983048 | tf_op jit(solution)/shard_map/ppermute | solution.py:50
  17.2 1.8 %collective-permute-start.15 = (f32[4,32,640]{2,1,0:T(8,128)S(1)}, f32[4,32,640]{2,1,0:T(8,128)S(1)}, u32[]{:S(2)}, u32[]{:S(2)}) collective-permute-start(f32[4,32,640]{2,1,0:T(8,128)S(1)} %get-tuple-element.115), channel_id=1, source_target_pairs={{0,1},{1,0},{2,3},{3,2},{4,5},{5,4},{6,7},{7,6},{8,9},{9,8},{10,11... | collective-permute-start | bytes 983048 | tf_op jit(solution)/shard_map/ppermute | solution.py:50
  18.8 5.4 %collective-permute-start.5 = (f32[2,32,640]{2,1,0:T(8,128)S(1)}, f32[2,32,640]{2,1,0:T(8,128)S(1)}, u32[]{:S(2)}, u32[]{:S(2)}) collective-permute-start(f32[2,32,640]{2,1,0:T(8,128)S(1)} %slice.33), channel_id=1, source_target_pairs={{0,32},{1,97},{2,34},{3,99},{4,36},{5,101},{6,38},{7,103},{8,40},{... | collective-permute-start | bytes 491528 | tf_op jit(solution)/shard_map/ppermute | solution.py:50
  19.1 7.1 %collective-permute-start.16 = (f32[2,32,640]{2,1,0:T(8,128)S(1)}, f32[2,32,640]{2,1,0:T(8,128)S(1)}, u32[]{:S(2)}, u32[]{:S(2)}) collective-permute-start(f32[2,32,640]{2,1,0:T(8,128)S(1)} %slice.37), channel_id=1, source_target_pairs={{0,8},{1,25},{2,10},{3,27},{4,12},{5,29},{6,14},{7,31},{8,0},{9,17... | collective-permute-start | bytes 491528 | tf_op jit(solution)/shard_map/ppermute | solution.py:50
  24.3 4.5 %collective-permute-start.6 = (f32[1,32,640]{2,1,0:T(8,128)S(1)}, f32[1,32,640]{2,1,0:T(8,128)S(1)}, u32[]{:S(2)}, u32[]{:S(2)}) collective-permute-start(f32[1,32,640]{2,1,0:T(8,128)S(1)} %slice.35), channel_id=1, source_target_pairs={{0,8},{1,25},{2,10},{3,27},{4,12},{5,29},{6,14},{7,31},{8,0},{9,17... | collective-permute-start | bytes 245768 | tf_op jit(solution)/shard_map/ppermute | solution.py:50
  26.3 4.5 %collective-permute-start.17 = (f32[1,32,640]{2,1,0:T(8,128)S(1)}, f32[1,32,640]{2,1,0:T(8,128)S(1)}, u32[]{:S(2)}, u32[]{:S(2)}) collective-permute-start(f32[1,32,640]{2,1,0:T(8,128)S(1)} %slice.39), channel_id=1, source_target_pairs={{0,2},{1,7},{2,0},{3,5},{4,6},{5,3},{6,4},{7,1},{8,10},{9,15},{10,... | collective-permute-start | bytes 245768 | tf_op jit(solution)/shard_map/ppermute | solution.py:50
  28.8 5.7 %collective-permute-start.7 = (f32[1,32,640]{2,1,0:T(8,128)S(1)}, f32[1,32,640]{2,1,0:T(8,128)S(1)}, u32[]{:S(2)}, u32[]{:S(2)}) collective-permute-start(f32[1,32,640]{2,1,0:T(8,128)S(1)} %slice_add_fusion.3), channel_id=1, source_target_pairs={{0,6},{1,3},{2,4},{3,1},{4,2},{5,7},{6,0},{7,5},{8,14},{9,11},{10,... | collective-permute-start | bytes 245768 | tf_op jit(solution)/shard_map/ppermute | solution.py:50
  30.9 5.7 %collective-permute-start.18 = (f32[1,32,640]{2,1,0:T(8,128)S(1)}, f32[1,32,640]{2,1,0:T(8,128)S(1)}, u32[]{:S(2)}, u32[]{:S(2)}) collective-permute-start(f32[1,32,640]{2,1,0:T(8,128)S(1)} %slice_add_fusion.2), channel_id=1, source_target_pairs={{0,96},{1,33},{2,98},{3,35},{4,100},{5,37},{6,102},{7,39},{8,104},... | collective-permute-start | bytes 245768 | tf_op jit(solution)/shard_map/ppermute | solution.py:50
  34.6 5.7 %collective-permute-start.8 = (f32[1,32,640]{2,1,0:T(8,128)S(1)}, f32[1,32,640]{2,1,0:T(8,128)S(1)}, u32[]{:S(2)}, u32[]{:S(2)}) collective-permute-start(f32[1,32,640]{2,1,0:T(8,128)S(1)} %add.66), channel_id=1, source_target_pairs={{0,96},{1,33},{2,98},{3,35},{4,100},{5,37},{6,102},{7,39},{8,104},... | collective-permute-start | bytes 245768 | tf_op jit(solution)/shard_map/ppermute | solution.py:50
  36.6 7.8 %collective-permute-start.19 = (f32[1,32,640]{2,1,0:T(8,128)S(1)}, f32[1,32,640]{2,1,0:T(8,128)S(1)}, u32[]{:S(2)}, u32[]{:S(2)}) collective-permute-start(f32[1,32,640]{2,1,0:T(8,128)S(1)} %add.73), channel_id=1, source_target_pairs={{0,24},{1,9},{2,26},{3,11},{4,28},{5,13},{6,30},{7,15},{8,16},{9,1... | collective-permute-start | bytes 245768 | tf_op jit(solution)/shard_map/ppermute | solution.py:50
  40.3 6.5 %collective-permute-start.9 = (f32[1,32,640]{2,1,0:T(8,128)S(1)}, f32[1,32,640]{2,1,0:T(8,128)S(1)}, u32[]{:S(2)}, u32[]{:S(2)}) collective-permute-start(f32[1,32,640]{2,1,0:T(8,128)S(1)} %add.67), channel_id=1, source_target_pairs={{0,24},{1,9},{2,26},{3,11},{4,28},{5,13},{6,30},{7,15},{8,16},{9,1... | collective-permute-start | bytes 245768 | tf_op jit(solution)/shard_map/ppermute | solution.py:50
  44.4 5.7 %collective-permute-start.20 = (f32[1,32,640]{2,1,0:T(8,128)S(1)}, f32[1,32,640]{2,1,0:T(8,128)S(1)}, u32[]{:S(2)}, u32[]{:S(2)}) collective-permute-start(f32[1,32,640]{2,1,0:T(8,128)S(1)} %add.74), channel_id=1, source_target_pairs={{0,6},{1,3},{2,4},{3,1},{4,2},{5,7},{6,0},{7,5},{8,14},{9,11},{10,... | collective-permute-start | bytes 245768 | tf_op jit(solution)/shard_map/ppermute | solution.py:50
  46.9 4.5 %collective-permute-start.10 = (f32[1,32,640]{2,1,0:T(8,128)S(1)}, f32[1,32,640]{2,1,0:T(8,128)S(1)}, u32[]{:S(2)}, u32[]{:S(2)}) collective-permute-start(f32[1,32,640]{2,1,0:T(8,128)S(1)} %add.68), channel_id=1, source_target_pairs={{0,8},{1,25},{2,10},{3,27},{4,12},{5,29},{6,14},{7,31},{8,0},{9,17... | collective-permute-start | bytes 245768 | tf_op jit(solution)/shard_map/ppermute | solution.py:50
  50.2 4.5 %collective-permute-start.21 = (f32[1,32,640]{2,1,0:T(8,128)S(1)}, f32[1,32,640]{2,1,0:T(8,128)S(1)}, u32[]{:S(2)}, u32[]{:S(2)}) collective-permute-start(f32[1,32,640]{2,1,0:T(8,128)S(1)} %add.75), channel_id=1, source_target_pairs={{0,2},{1,7},{2,0},{3,5},{4,6},{5,3},{6,4},{7,1},{8,10},{9,15},{10,... | collective-permute-start | bytes 245768 | tf_op jit(solution)/shard_map/ppermute | solution.py:50
  51.4 5.4 %collective-permute-start.11 = (f32[2,32,640]{2,1,0:T(8,128)S(1)}, f32[2,32,640]{2,1,0:T(8,128)S(1)}, u32[]{:S(2)}, u32[]{:S(2)}) collective-permute-start(f32[2,32,640]{2,1,0:T(8,128)S(1)} %pad_maximum_fusion.2), channel_id=1, source_target_pairs={{0,32},{1,97},{2,34},{3,99},{4,36},{5,101},{6,38},{7,103},{8,40},{... | collective-permute-start | bytes 491528 | tf_op jit(solution)/shard_map/ppermute | solution.py:50
  54.7 5.4 %collective-permute-start.22 = (f32[2,32,640]{2,1,0:T(8,128)S(1)}, f32[2,32,640]{2,1,0:T(8,128)S(1)}, u32[]{:S(2)}, u32[]{:S(2)}) collective-permute-start(f32[2,32,640]{2,1,0:T(8,128)S(1)} %pad_maximum_fusion.3), channel_id=1, source_target_pairs={{0,8},{1,25},{2,10},{3,27},{4,12},{5,29},{6,14},{7,31},{8,0},{9,17... | collective-permute-start | bytes 491528 | tf_op jit(solution)/shard_map/ppermute | solution.py:50
  56.8 7.2 %collective-permute-start.13 = (f32[4,32,640]{2,1,0:T(8,128)S(1)}, f32[4,32,640]{2,1,0:T(8,128)S(1)}, u32[]{:S(2)}, u32[]{:S(2)}) collective-permute-start(f32[4,32,640]{2,1,0:T(8,128)S(1)} %pad_maximum_fusion.refs_4_.refs_0_), channel_id=1, source_target_pairs={{0,2},{1,7},{2,0},{3,5},{4,6},{5,3},{6,4},{7,1},{8,10},{9,15},{10,... | collective-permute-start | bytes 983048 | tf_op jit(solution)/shard_map/ppermute | solution.py:50
  57.8 4.2 %collective-permute-start.12 = (f32[4,32,640]{2,1,0:T(8,128)S(1)}, f32[4,32,640]{2,1,0:T(8,128)S(1)}, u32[]{:S(2)}, u32[]{:S(2)}) collective-permute-start(f32[4,32,640]{2,1,0:T(8,128)S(1)} %pad_maximum_fusion.refs_4_.refs_0_), channel_id=1, source_target_pairs={{0,1},{1,0},{2,3},{3,2},{4,5},{5,4},{6,7},{7,6},{8,9},{9,8},{10,11... | collective-permute-start | bytes 983048 | tf_op jit(solution)/shard_map/ppermute | solution.py:50
  60.1 4.7 %collective-permute-start.23 = (f32[4,32,640]{2,1,0:T(8,128)S(1)}, f32[4,32,640]{2,1,0:T(8,128)S(1)}, u32[]{:S(2)}, u32[]{:S(2)}) collective-permute-start(f32[4,32,640]{2,1,0:T(8,128)S(1)} %pad_maximum_fusion.1.refs_4_.refs_2_), channel_id=1, source_target_pairs={{0,1},{1,0},{2,3},{3,2},{4,5},{5,4},{6,7},{7,6},{8,9},{9,8},{10,11... | collective-permute-start | bytes 983048 | tf_op jit(solution)/shard_map/ppermute | solution.py:50
  60.2 7.3 %collective-permute-start.24 = (f32[4,32,640]{2,1,0:T(8,128)S(1)}, f32[4,32,640]{2,1,0:T(8,128)S(1)}, u32[]{:S(2)}, u32[]{:S(2)}) collective-permute-start(f32[4,32,640]{2,1,0:T(8,128)S(1)} %pad_maximum_fusion.1.refs_4_.refs_2_), channel_id=1, source_target_pairs={{0,32},{1,97},{2,34},{3,99},{4,36},{5,101},{6,38},{7,103},{8,40},{... | collective-permute-start | bytes 983048 | tf_op jit(solution)/shard_map/ppermute | solution.py:50
  64.7 3.2 %collective-permute-start.14 = (f32[4,32,640]{2,1,0:T(8,128)S(1)}, f32[4,32,640]{2,1,0:T(8,128)S(1)}, u32[]{:S(2)}, u32[]{:S(2)}) collective-permute-start(f32[4,32,640]{2,1,0:T(8,128)S(1)} %collective-permute-done.13.refs_4_.refs_1_), channel_id=1, source_target_pairs={{0,1},{1,0},{2,3},{3,2},{4,5},{5,4},{6,7},{7,6},{8,9},{9,8},{10,11... | collective-permute-start | bytes 983048 | tf_op jit(solution)/shard_map/ppermute | solution.py:50
  67.6 1.8 %collective-permute-start.25 = (f32[4,32,640]{2,1,0:T(8,128)S(1)}, f32[4,32,640]{2,1,0:T(8,128)S(1)}, u32[]{:S(2)}, u32[]{:S(2)}) collective-permute-start(f32[4,32,640]{2,1,0:T(8,128)S(1)} %collective-permute-done.24.refs_4_.refs_3_), channel_id=1, source_target_pairs={{0,1},{1,0},{2,3},{3,2},{4,5},{5,4},{6,7},{7,6},{8,9},{9,8},{10,11... | collective-permute-start | bytes 983048 | tf_op jit(solution)/shard_map/ppermute | solution.py:50
  70.1 4.7 %collective-permute-start.26 = (f32[32,768]{1,0:T(8,128)S(1)}, f32[32,768]{1,0:T(8,128)S(1)}, u32[]{:S(2)}, u32[]{:S(2)}) collective-permute-start(f32[32,768]{1,0:T(8,128)S(1)} %get-tuple-element.142), channel_id=1, source_target_pairs={{0,32},{1,9},{2,34},{3,11},{4,36},{5,13},{6,38},{7,15},{8,40},{9,1... | collective-permute-start | bytes 294920 | tf_op jit(solution)/shard_map/ppermute | solution.py:50
  74.9 4.7 %collective-permute-start.27 = (f32[32,768]{1,0:T(8,128)S(1)}, f32[32,768]{1,0:T(8,128)S(1)}, u32[]{:S(2)}, u32[]{:S(2)}) collective-permute-start(f32[32,768]{1,0:T(8,128)S(1)} %add.76), channel_id=1, source_target_pairs={{0,8},{1,33},{2,10},{3,35},{4,12},{5,37},{6,14},{7,39},{8,0},{9,41... | collective-permute-start | bytes 294920 | tf_op jit(solution)/shard_map/ppermute | solution.py:50
  79.6 5.9 %collective-permute-start.28 = (f32[32,768]{1,0:T(8,128)S(1)}, f32[32,768]{1,0:T(8,128)S(1)}, u32[]{:S(2)}, u32[]{:S(2)}) collective-permute-start(f32[32,768]{1,0:T(8,128)S(1)} %add.77), channel_id=1, source_target_pairs={{0,96},{1,25},{2,98},{3,27},{4,100},{5,29},{6,102},{7,31},{8,104},... | collective-permute-start | bytes 294920 | tf_op jit(solution)/shard_map/ppermute | solution.py:50
  85.5 6.1 %collective-permute-start.29 = (f32[32,768]{1,0:T(8,128)S(1)}, f32[32,768]{1,0:T(8,128)S(1)}, u32[]{:S(2)}, u32[]{:S(2)}) collective-permute-start(f32[32,768]{1,0:T(8,128)S(1)} %add.78), channel_id=1, source_target_pairs={{0,24},{1,97},{2,26},{3,99},{4,28},{5,101},{6,30},{7,103},{8,16},{... | collective-permute-start | bytes 294920 | tf_op jit(solution)/shard_map/ppermute | solution.py:50
